TPU v7x, 32 devices: a whole 2x2x4 slice. The times are simulated.
32 devices in a mesh: batch: 4 (over y, core), seq: 8 (over z, x).
Axes of the slice: x: 2, y: 2, z: 4, core: 2. Of those that a mesh axis runs over, the one named last changes fastest.
Arguments:
- tokens: bfloat16 [20, 2048, 960], P('batch', 'seq'), may hold values from -6 to 6
- doc_starts: int32 [20, 2048], P('batch'), may hold values from 0 to 1, as said below
- pregain: bfloat16 [960], replicated, may hold values from 0.5 to 1.5
- query_base: bfloat16 [960, 960], replicated, may hold values from -0.1875 to 0.1875
- key_base: bfloat16 [960, 320], replicated, may hold values from -0.1875 to 0.1875
- value_base: bfloat16 [960, 320], replicated, may hold values from -0.1875 to 0.1875
- output_base: bfloat16 [960, 960], replicated, may hold values from -1.5 to 1.5
- query_down: bfloat16 [960, 8], replicated, may hold values from -0.1875 to 0.1875
- query_up: bfloat16 [8, 960], replicated, may hold values from -0.59765625 to 0.59765625
- key_down: bfloat16 [960, 8], replicated, may hold values from -0.1875 to 0.1875
- key_up: bfloat16 [8, 320], replicated, may hold values from -0.59765625 to 0.59765625
- value_down: bfloat16 [960, 8], replicated, may hold values from -0.1875 to 0.1875
- value_up: bfloat16 [8, 320], replicated, may hold values from -0.59765625 to 0.59765625
- out_down: bfloat16 [960, 8], replicated, may hold values from -1.5 to 1.5
- out_up: bfloat16 [8, 960], replicated, may hold values from -0.59765625 to 0.59765625
- query_map: bfloat16 [15, 64, 64], replicated, may hold values from -0.75 to 0.75
- key_map: bfloat16 [5, 64, 64], replicated, may hold values from -0.75 to 0.75
- postgain: bfloat16 [960], replicated, may hold values from 0.5 to 1.5
- gate_proj: bfloat16 [960, 2560], replicated, may hold values from -0.1875 to 0.1875
- up_proj: bfloat16 [960, 2560], replicated, may hold values from -0.1875 to 0.1875
- down_proj: bfloat16 [2560, 960], replicated, may hold values from -0.125 to 0.125
- cotangent: bfloat16 [20, 2048, 960], P('batch', 'seq'), may hold values from -6 to 6
Outputs:
- layer_out: bfloat16 [20, 2048, 960], P('batch', 'seq')
- grad_tokens: float32 [20, 2048, 960], P('batch', 'seq')
- grad_pregain: float32 [960], replicated
- grad_querydown: float32 [960, 8], replicated
- grad_queryup: float32 [8, 960], replicated
- grad_keydown: float32 [960, 8], replicated
- grad_keyup: float32 [8, 320], replicated
- grad_valuedown: float32 [960, 8], replicated
- grad_valueup: float32 [8, 320], replicated
- grad_outdown: float32 [960, 8], replicated
- grad_outup: float32 [8, 960], replicated
- grad_querymap: float32 [15, 64, 64], replicated
- grad_keymap: float32 [5, 64, 64], replicated
- grad_postgain: float32 [960], replicated
- grad_gateproj: float32 [960, 2560], replicated
- grad_upproj: float32 [960, 2560], replicated
- grad_downproj: float32 [2560, 960], replicated
Inputs may be any that keep to these rules, and one draw needn't show every extreme that they name: doc_starts is 1 at the first token of every row; in each aligned block of 5 rows one row, drawn from the seed, has no other start.
All inputs are finite; a program needn't handle non-finite values.
Results may differ from a plain program's by a relative error of at most 0.02.
Values may be sent and summed in bfloat16 or wider, within the bound.
A program may use at most 384 MiB of HBM per device.

v0:
```python
import jax
import jax.numpy as jnp
from jax import lax
from jax.sharding import PartitionSpec as P

WINDOW = 64


EPSILON = 1e-05
EXACT = lax.Precision.HIGHEST


def passed_along(block, axis, distance):
    devices = range(lax.axis_size(axis))
    route = [(i - distance, i) for i in devices if i - distance in devices]
    return lax.ppermute(block, axis, route)


def entering(value, axis, join, neutral):
    count, mine = (lax.axis_size(axis), lax.axis_index(axis))
    pieces = jax.tree.map(lambda part: lax.all_gather(part, axis), value)
    total = jax.tree.map(
        lambda part, zero: jnp.full_like(part, 0) + jnp.asarray(zero, part.dtype), value, neutral
    )

    def entering_turn(position, total):
        longer = join(total, jax.tree.map(lambda part: part[position], pieces))
        return jax.tree.map(lambda new, old: jnp.where(position < mine, new, old), longer, total)

    return lax.fori_loop(0, count - 1, entering_turn, total)


def prefix_2(array, axis, combine, identity):
    count, index = (lax.axis_size(axis), lax.axis_index(axis))
    everything = jax.tree.map(
        lambda part, kind: lax.all_gather(part.astype(kind), axis),
        array,
        (jnp.bfloat16, jnp.bfloat16, jnp.bfloat16),
    )
    start = jax.tree.map(
        lambda part, zero: jnp.broadcast_to(jnp.asarray(zero, part.dtype), part.shape),
        array,
        identity,
    )

    def prefix_turn(k, before):
        at = count - 1 - k
        reached = at > index
        new = combine(
            before, jax.tree.map(lambda part, own: part[at].astype(own.dtype), everything, array)
        )
        return jax.tree.map(lambda a, b: jnp.where(reached, a, b), new, before)

    return lax.fori_loop(0, count, prefix_turn, start)


def normalize(value, gain):
    return value * lax.rsqrt(jnp.mean(value * value, axis=-1, keepdims=True) + EPSILON) * gain


def feature(logit):
    return jnp.concatenate(
        [jax.nn.softmax(logit, axis=-1), jax.nn.softmax(-logit, axis=-1)], axis=-1
    )


def contract(form, left, right):
    return jnp.einsum(form, left, right, preferred_element_type=jnp.float32)


def precise(form, left, right):
    return jnp.einsum(form, left, right, precision=EXACT, preferred_element_type=jnp.float32)


def chain(earlier, later):
    first_keep, first_state, first_norm = earlier
    last_keep, last_state, last_norm = later
    return (
        first_keep * last_keep,
        last_state + last_keep[:, None, None, None] * first_state,
        last_norm + last_keep[:, None, None] * first_norm,
    )


def project(normed, base, down, upward):
    inner = contract("td,dr->tr", normed, down).astype(jnp.bfloat16)
    return (
        inner,
        (contract("td,de->te", normed, base) + 2.0 * contract("tr,re->te", inner, upward)).astype(
            jnp.bfloat16
        ),
    )


def project_back(normed, inner, base, down, upward, grad_out):
    grad_upward = 2.0 * contract("tr,te->re", inner, grad_out)
    grad_inner = (2.0 * contract("te,re->tr", grad_out, upward)).astype(jnp.bfloat16)
    grad_down = contract("td,tr->dr", normed, grad_inner)
    grad_in = contract("te,de->td", grad_out, base) + contract("tr,dr->td", grad_inner, down)
    return (grad_down, grad_upward, grad_in)


def frames(doc_starts, my_index, span, window):
    rows = doc_starts.shape[0]
    padded = jnp.concatenate([jnp.zeros((rows, window), jnp.int32), doc_starts], axis=1)
    marks = lax.dynamic_slice_in_dim(padded, my_index * span, span + window, 1)
    segment = jnp.cumsum(marks, axis=1)
    query_seg = segment[:, window:]
    key_pos = jnp.arange(span + window, dtype=jnp.int32)
    query_pos = jnp.arange(span, dtype=jnp.int32)
    same = query_seg[:, :, None] == segment[:, None, :]
    lin_mask = same & (key_pos[None, None, :] <= query_pos[None, :, None])
    win_mask = (
        same
        & (key_pos[None, None, :] > query_pos[None, :, None])
        & (key_pos[None, None, :] <= query_pos[None, :, None] + window)
    )
    shown = (query_seg == 0).astype(jnp.float32)
    keep_mask = ((key_pos[None, :] < span) & (segment == segment[:, span - 1 : span])).astype(
        jnp.float32
    )
    kept = (segment[:, span - 1] == 0).astype(jnp.float32)
    return (padded, lin_mask, win_mask, shown, keep_mask, kept)


def body(
    tokens,
    doc_starts,
    pregain,
    query_base,
    key_base,
    value_base,
    output_base,
    query_down,
    query_up,
    key_down,
    key_up,
    value_down,
    value_up,
    out_down,
    out_up,
    query_map,
    key_map,
    postgain,
    gate_proj,
    up_proj,
    down_proj,
    cotangent,
):
    rows, span, width = tokens.shape
    heads, head = (query_map.shape[0], query_map.shape[1])
    kv_heads = key_map.shape[0]
    group = heads // kv_heads
    kv_width = kv_heads * head
    window = WINDOW
    extent = span + window
    scale = head ** (-0.5)
    count = rows * span
    my_index = lax.axis_index("seq")
    flat = tokens.reshape(count, width).astype(jnp.float32)
    first_gain = pregain.astype(jnp.float32)
    normed = normalize(flat, first_gain).astype(jnp.bfloat16)
    query_inner, query = project(normed, query_base, query_down, query_up)
    key_inner, key = project(normed, key_base, key_down, key_up)
    value_inner, value = project(normed, value_base, value_down, value_up)
    key_rows = key.reshape(rows, span, kv_width)
    value_rows = value.reshape(rows, span, kv_width)
    trailing = jnp.concatenate(
        [key_rows[:, span - window :], value_rows[:, span - window :]], axis=2
    )
    received = passed_along(trailing, "seq", 1)
    key_ext = jnp.concatenate([received[:, :, :kv_width], key_rows], axis=1).reshape(
        rows, extent, kv_heads, head
    )
    value_ext = jnp.concatenate([received[:, :, kv_width:], value_rows], axis=1).reshape(
        rows, extent, kv_heads, head
    )
    query_four = query.reshape(rows, span, kv_heads, group, head)
    padded, lin_mask, win_mask, shown, keep_mask, kept = frames(doc_starts, my_index, span, window)
    query_table = query_map.reshape(kv_heads, group, head, head)
    key_logit = contract("rekd,kdf->rekf", key_ext, key_map)
    key_phi = feature(key_logit).astype(jnp.bfloat16)
    kept_phi = key_phi * keep_mask[:, :, None, None].astype(jnp.bfloat16)
    own_state = contract("rekd,rekf->rkdf", value_ext, kept_phi)
    own_norm = jnp.sum(kept_phi.astype(jnp.float32), axis=1)
    identity = (jnp.ones_like(kept), jnp.zeros_like(own_state), jnp.zeros_like(own_norm))
    prefix = entering((kept, own_state, own_norm), "seq", chain, identity)
    prior_state, prior_norm = (prefix[1], prefix[2])
    query_logit = contract("rlkgd,kgde->rlkge", query_four, query_table)
    query_phi = feature(query_logit).astype(jnp.bfloat16)
    linear = contract("rlkgf,rekf->rkgle", query_phi, key_phi)
    score = contract("rlkgd,rekd->rkgle", query_four, key_ext) * scale
    growth = jnp.exp(score)
    weights = jnp.where(lin_mask[:, None, None], linear, 0.0) + jnp.where(
        win_mask[:, None, None], growth, 0.0
    )
    rounded = weights.astype(jnp.bfloat16)
    seen_rows = shown[:, :, None, None]
    numer = contract("rkgle,rekd->rlkgd", rounded, value_ext) + seen_rows[..., None] * precise(
        "rlkgf,rkdf->rlkgd", query_phi.astype(jnp.float32), prior_state
    )
    denom = jnp.transpose(jnp.sum(weights, axis=-1), (0, 3, 1, 2)) + seen_rows * precise(
        "rlkgf,rkf->rlkg", query_phi.astype(jnp.float32), prior_norm
    )
    mixed = numer / denom[..., None]
    attended = mixed.astype(jnp.bfloat16).reshape(count, width)
    out_inner, branch_low = (None, None)
    out_inner = contract("td,dr->tr", attended, out_down).astype(jnp.bfloat16)
    branch = contract("td,de->te", attended, output_base) + 2.0 * contract(
        "tr,re->te", out_inner, out_up
    )
    middle = flat + branch
    second_gain = postgain.astype(jnp.float32)
    normed_two = normalize(middle, second_gain).astype(jnp.bfloat16)
    gate = contract("td,df->tf", normed_two, gate_proj)
    lifted = contract("td,df->tf", normed_two, up_proj)
    hidden = (jax.nn.silu(gate) * lifted).astype(jnp.bfloat16)
    layer_out = (
        (middle + contract("tf,fd->td", hidden, down_proj))
        .astype(jnp.bfloat16)
        .reshape(rows, span, width)
    )
    upstream = cotangent.reshape(count, width)
    grad_downproj = contract("tf,td->fd", hidden, upstream)
    grad_hidden = (
        contract("td,fd->tf", upstream, down_proj).astype(jnp.bfloat16).astype(jnp.float32)
    )
    swish_pull = jax.vjp(lambda left, right: jax.nn.silu(left) * right, gate, lifted)[1]
    grad_gate, grad_lift = swish_pull(grad_hidden)
    grad_gate = grad_gate.astype(jnp.bfloat16)
    grad_lift = grad_lift.astype(jnp.bfloat16)
    grad_gateproj = contract("td,tf->df", normed_two, grad_gate)
    grad_upproj = contract("td,tf->df", normed_two, grad_lift)
    grad_normed_two = contract("tf,df->td", grad_gate, gate_proj) + contract(
        "tf,df->td", grad_lift, up_proj
    )
    norm_pull = jax.vjp(normalize, middle, second_gain)[1]
    grad_middle_norm, grad_postgain = norm_pull(grad_normed_two)
    grad_middle = upstream.astype(jnp.float32) + grad_middle_norm
    grad_branch = grad_middle.astype(jnp.bfloat16)
    grad_outdown, grad_outup, grad_attended = project_back(
        attended, out_inner, output_base, out_down, out_up, grad_branch
    )
    grad_mixed = (
        grad_attended.astype(jnp.bfloat16)
        .astype(jnp.float32)
        .reshape(rows, span, kv_heads, group, head)
    )
    grad_denom = -jnp.sum(grad_mixed * mixed, axis=-1) / denom
    grad_numer = (grad_mixed / denom[..., None]).astype(jnp.bfloat16)
    grad_weights = (
        contract("rlkgd,rekd->rkgle", grad_numer, value_ext)
        + jnp.transpose(grad_denom, (0, 2, 3, 1))[..., None]
    )
    grad_value = contract("rkgle,rlkgd->rekd", rounded, grad_numer)
    seen_numer = grad_numer * seen_rows[..., None].astype(jnp.bfloat16)
    grad_prior_state = contract("rlkgd,rlkgf->rkdf", seen_numer, query_phi)
    grad_prior_norm = precise(
        "rlkg,rlkgf->rkf", grad_denom * seen_rows, query_phi.astype(jnp.float32)
    )
    grad_qphi = seen_rows[..., None] * (
        precise("rlkgd,rkdf->rlkgf", grad_numer.astype(jnp.float32), prior_state)
        + grad_denom[..., None] * prior_norm[:, None, :, None, :]
    )
    grad_linear = jnp.where(lin_mask[:, None, None], grad_weights, 0.0).astype(jnp.bfloat16)
    grad_score = jnp.where(win_mask[:, None, None], grad_weights * growth, 0.0).astype(jnp.bfloat16)
    grad_qphi = grad_qphi + contract("rkgle,rekf->rlkgf", grad_linear, key_phi)
    grad_kphi = contract("rkgle,rlkgf->rekf", grad_linear, query_phi)
    grad_query = contract("rkgle,rekd->rlkgd", grad_score, key_ext) * scale
    grad_key = contract("rkgle,rlkgd->rekd", grad_score, query_four) * scale
    suffix = prefix_2((kept, grad_prior_state, grad_prior_norm), "seq", chain, identity)
    grad_own_state, grad_own_norm = (suffix[1], suffix[2])
    keep_four = keep_mask[:, :, None, None]
    grad_kphi = grad_kphi + keep_four * (
        precise("rekd,rkdf->rekf", value_ext.astype(jnp.float32), grad_own_state)
        + grad_own_norm[:, None]
    )
    grad_value = grad_value + precise(
        "rekf,rkdf->rekd", kept_phi.astype(jnp.float32), grad_own_state
    )
    query_pull = jax.vjp(feature, query_logit)[1]
    grad_qlogit = query_pull(grad_qphi.astype(jnp.bfloat16).astype(jnp.float32))[0].astype(
        jnp.bfloat16
    )
    grad_querymap = contract("rlkgd,rlkge->kgde", query_four, grad_qlogit).reshape(
        heads, head, head
    )
    grad_query = grad_query + contract("rlkge,kgde->rlkgd", grad_qlogit, query_table)
    key_pull = jax.vjp(feature, key_logit)[1]
    grad_klogit = key_pull(grad_kphi.astype(jnp.bfloat16).astype(jnp.float32))[0].astype(
        jnp.bfloat16
    )
    grad_keymap = contract("rekd,rekf->kdf", key_ext, grad_klogit)
    grad_key = grad_key + contract("rekf,kdf->rekd", grad_klogit, key_map)
    grad_key = grad_key.reshape(rows, extent, kv_width)
    grad_value = grad_value.reshape(rows, extent, kv_width)
    leading = jnp.concatenate([grad_key[:, :window], grad_value[:, :window]], axis=2)
    returned = passed_along(leading.astype(jnp.bfloat16), "seq", -1).astype(leading.dtype)
    placed = jnp.pad(returned, ((0, 0), (span - window, 0), (0, 0)))
    key_total = (
        (grad_key[:, window:] + placed[:, :, :kv_width])
        .astype(jnp.bfloat16)
        .reshape(count, kv_width)
    )
    value_total = (
        (grad_value[:, window:] + placed[:, :, kv_width:])
        .astype(jnp.bfloat16)
        .reshape(count, kv_width)
    )
    query_total = grad_query.astype(jnp.bfloat16).reshape(count, width)
    grad_querydown, grad_queryup, from_query = project_back(
        normed, query_inner, query_base, query_down, query_up, query_total
    )
    grad_keydown, grad_keyup, from_key = project_back(
        normed, key_inner, key_base, key_down, key_up, key_total
    )
    grad_valuedown, grad_valueup, from_value = project_back(
        normed, value_inner, value_base, value_down, value_up, value_total
    )
    grad_normed = from_query + from_key + from_value
    first_pull = jax.vjp(normalize, flat, first_gain)[1]
    grad_flat_norm, grad_pregain = first_pull(grad_normed)
    grad_tokens = (grad_middle + grad_flat_norm).reshape(rows, span, width)
    summed = lax.psum(
        (
            grad_pregain,
            grad_querydown,
            grad_queryup,
            grad_keydown,
            grad_keyup,
            grad_valuedown,
            grad_valueup,
            grad_outdown,
            grad_outup,
            grad_querymap,
            grad_keymap,
            grad_postgain,
            grad_gateproj,
            grad_upproj,
            grad_downproj,
        ),
        ("batch", "seq"),
    )
    return (
        layer_out,
        grad_tokens,
        summed[0],
        summed[1],
        summed[2],
        summed[3],
        summed[4],
        summed[5],
        summed[6],
        summed[7],
        summed[8],
        summed[9],
        summed[10],
        summed[11],
        summed[12],
        summed[13],
        summed[14],
    )


def solution(mesh):
    return jax.shard_map(
        body,
        mesh=mesh,
        in_specs=(
            P("batch", "seq", None),
            P("batch", None),
            P(),
            P(),
            P(),
            P(),
            P(),
            P(),
            P(),
            P(),
            P(),
            P(),
            P(),
            P(),
            P(),
            P(),
            P(),
            P(),
            P(),
            P(),
            P(),
            P("batch", "seq", None),
        ),
        out_specs=(
            P("batch", "seq", None),
            P("batch", "seq", None),
            P(),
            P(),
            P(),
            P(),
            P(),
            P(),
            P(),
            P(),
            P(),
            P(),
            P(),
            P(),
            P(),
            P(),
            P(),
        ),
        check_vma=False,
    )
```

profile of v0, /device:TPU:0, one launch (start us, length us, event | category | flops | bytes accessed | tf_op | source)
XLA Modules:
  0.0 1287.0 jit_solution(12226514042090446653)
XLA Ops:
  9.6 4.9 copy.130
  14.5 5.8 copy.153
  36.9 5.0 collective-permute-start
  72.1 20.0 %all-reduce.4 = bf16[40]{0:T(256)(128)(2,1)S(1)} all-reduce(bf16[40]{0:T(256)(128)(2,1)S(1)} %dynamic-update-slice.1), channel_id=7, replica_groups=mesh['batch'=4,'seq'=8] {'seq'}, use_global_device_ids=true, to_apply=%add.4 | all-reduce | flops 40 | bytes 160
  92.8 17.8 %all-reduce.3 = f32[40]{0:T(128)S(1)} all-reduce(f32[40]{0:T(128)S(1)} %bitcast_dynamic-update-slice_fusion), channel_id=3, replica_groups=mesh['batch'=4,'seq'=8] {'seq'}, use_global_device_ids=true, to_apply=%add.3 | all-reduce | flops 40 | bytes 320
  122.5 5.3 fusion.138
  130.1 6.4 reshape.335
  140.2 8.3 fusion.132
  148.5 8.1 fusion.133
  163.5 11.4 convolution_convert_fusion
  174.9 31.0 %all-gather.2 = f32[40,5,128]{2,1,0:T(8,128)S(1)} all-gather(f32[5,5,128]{2,1,0:T(8,128)S(1)} %copy.150), channel_id=4, replica_groups=mesh['batch'=4,'seq'=8] {'seq'}, dimensions={0}, use_global_device_ids=true | all-gather | bytes 115200 | tf_op jit(solution)/shard_map/all_gather | solution.py:21
  206.5 11.8 fusion.85
  218.3 20.0 %fusion.136 = (f32[5,5,3,256]{3,2,1,0:T(4,128)S(1)}, bf16[5,5,3,256,320]{3,4,2,1,0:T(8,128)(2,1)}) fusion(f32[5,5,320,256,3]{3,2,4,1,0:T(8,128)} %fusion.85, pred[5,256,320]{1,2,0:T(8,128)(4,1)} %get-tuple-element.491, pred[5,256,320]{1,2,0:T(8,128)(4,1)} %get-tuple-element.490, bf16[5,320,5,64]{1,3,0,2:T(8,128)(2,1)} %copy-done.27, ...), kind=kOutput, calls=%fused_computation.236 | convolution fusion | flops 1623635200 | bytes 44723200 | tf_op jit(solution)/shard_map/rlkgf,rekf->rkgle/dot_general | solution.py:68
  238.3 15.2 %while.34 = (s32[]{:T(128)}, f32[5,5,64,128]{3,2,1,0:T(8,128)S(1)}, f32[5,5,128]{2,1,0:T(8,128)S(1)}, s32[]{:T(128)}, f32[8,5,5,64,128]{4,3,2,1,0:T(8,128)}, /*i...) while((s32[]{:T(128)}, f32[5,5,64,128]{3,2,1,0:T(8,128)S(1)}, ...), condition=%wide.region_13.14_spmd.clone, body=%wide.region_12.13_spmd.clone.sunk | while | flops 832004 | bytes 2496215 | solution.py:30
  254.2 6.9 fusion.54
  261.1 7.0 fusion.52
  268.1 7.2 copy.197
  275.3 10.5 fusion.137
  297.5 10.3 fusion.140
  307.9 24.2 %fusion.17 = (bf16[1280,2560]{1,0:T(8,128)(2,1)}, bf16[1280,2560]{1,0:T(8,128)(2,1)}, bf16[1280,2560]{1,0:T(8,128)(2,1)}) fusion(f32[1280,2560]{1,0:T(8,128)} %fusion.140, bf16[1280,2560]{1,0:T(8,128)(2,1)} %convolution_convert_fusion, bf16[1280,960]{0,1:T(8,128)(2,1)} %copy-done.45, bf16[960,2560]{1,0:T(8,128)(2,1)} %param.44), kind=kOutput, calls=%fused_computation.32 | convolution fusion | flops 6347161600 | bytes 46694400 | tf_op jit(solution)/shard_map/td,df->tf/dot_general | solution.py:68
  332.0 11.9 fusion.141
  344.0 12.1 multiply_reduce_fusion
  366.9 7.2 reshape.355
  374.2 7.2 multiply_reduce_fusion.5
  381.5 10.3 fusion.25
  391.8 6.5 fusion.63
  398.3 24.0 %fusion.13 = (bf16[5,5,3,256,320]{3,4,2,1,0:T(8,128)(2,1)}, bf16[5,5,3,256,320]{3,4,2,1,0:T(8,128)(2,1)}) fusion(f32[5,5,320,256,3]{3,2,4,1,0:T(8,128)} %fusion.85, f32[5,5,3,256]{3,2,1,0:T(4,128)S(1)} %fusion.116, pred[5,256,320]{1,2,0:T(8,128)(4,1)} %get-tuple-element.491, pred[5,256,320]{1,2,0:T(8,128)(4,1)} %get-tuple-element.490, ...), kind=kOutput, calls=%fused_computation.22 | convolution fusion | flops 831488000 | bytes 53529600 | tf_op jit(solution)/shard_map/rlkgd,rekd->rkgle/dot_general | solution.py:68
  422.4 12.3 fusion.31
  434.7 9.2 multiply_reduce_fusion.4
  444.3 6.9 add_convert_fusion
  465.2 9.5 fusion.152
  487.6 30.9 %all-gather.4 = bf16[40,5,128]{2,1,0:T(8,128)(2,1)S(1)} all-gather(bf16[5,5,128]{2,1,0:T(8,128)(2,1)S(1)} %bitcast.421), channel_id=6, replica_groups=mesh['batch'=4,'seq'=8] {'seq'}, dimensions={0}, use_global_device_ids=true | all-gather | bytes 57600 | tf_op jit(solution)/shard_map/all_gather | solution.py:36
  518.6 12.3 fusion.19
  530.9 12.4 fusion.151
  543.3 11.9 fusion.150
  555.2 16.8 %while.35 = (s32[]{:T(128)}, f32[5,5,64,128]{3,2,1,0:T(8,128)S(1)}, f32[5,5,128]{2,1,0:T(8,128)S(1)}, s32[]{:T(128)}, bf16[8,5,5,64,128]{4,3,2,1,0:T(8,128)(2,1)...) while((s32[]{:T(128)}, f32[5,5,64,128]{3,2,1,0:T(8,128)S(1)}, ...), condition=%wide.region_21.22_spmd.clone, body=%wide.region_20.21_spmd.clone.sunk | while | flops 1040013 | bytes 2080267 | solution.py:54
  576.2 6.4 convert_bitcast_fusion
  585.2 5.3 add_convert_fusion.4
  592.5 11.4 bitcast_add_fusion.9
  636.9 9.1 multiply_reduce_fusion.1
  647.5 12.2 add_convert_fusion.2
  668.5 8.7 fusion.30
  677.2 5.9 copy.182
  683.2 5.8 copy.185
  688.9 86.2 %all-reduce.10.cloned.1.call-done = (f32[960]{0:T(1024)}, f32[960,8]{0,1:T(8,128)}, f32[8,960]{1,0:T(8,128)}, f32[960,8]{0,1:T(8,128)}, f32[8,320]{1,0:T(8,128)}...) async-done(((f32[960]{0:T(1024)}, f32[960,8]{0,1:T(8,128)}, f32[8,960]{1,0:T(8,128)}, f32[960,8]{0,1:T(8,128)}, ...) | async-done | bytes 212496 | tf_op jit(solution)/shard_map/psum | solution.py:324
  775.1 467.3 %all-reduce.12.cloned.1.call-done = (f32[15,64,64]{2,1,0:T(8,128)}, f32[5,64,64]{2,1,0:T(8,128)}, f32[960,2560]{1,0:T(8,128)}, f32[960,2560]{1,0:T(8,128)}, f32[2560,960]{0,1:T(8,128)}) async-done(((f32[15,64,64]{2,1,0:T(8,128)}, f32[5,64,64]{2,1,0:T(8,128)}, f32[960,2560]{1,0:T(8,128)}, f32[960,2560]{1,0:T(8,128)}, f32[2560,960]{0,1:T(8,128)}), (f32[15,64,64]{2,1,0:T(8,128)}, f32[5,64,64]{2,1,0:T(8,128)}, ...) | async-done | bytes 29818896 | tf_op jit(solution)/shard_map/psum | solution.py:324
  1259.2 8.6 copy.372
  1267.9 8.4 copy.373
  (462 shorter events, 228.2 us)
Async XLA Ops:
  7.2 281.9 %copy-start = (bf16[960,960]{1,0:T(8,128)(2,1)S(1)}, bf16[960,960]{1,0:T(8,128)(2,1)}, u32[]{:S(2)}) copy-start(bf16[960,960]{1,0:T(8,128)(2,1)} %param.32) | copy-start | bytes 5529604
  7.2 231.1 %all-gather.9.cloned.1.call-start = ((), (), s32[]{:S(2)}) async-start(), calls=%async_computation | async-start | bytes 7372800 | tf_op jit(solution)/shard_map/all_gather | solution.py:21
  28.6 13.4 %copy-start.92 = (s32[5,2048]{1,0:T(8,128)S(1)}, s32[5,2048]{1,0:T(8,128)}, u32[]{:S(2)}) copy-start(s32[5,2048]{1,0:T(8,128)} %param.27) | copy-start | bytes 122884
  36.0 16.9 %copy-start.105 = (u32[32]{0:T(128)S(1)}, u32[32]{0:T(128)}, u32[]{:S(2)}) copy-start(u32[32]{0:T(128)} %constant.132) | copy-start | bytes 388
  36.9 18.2 %collective-permute-start = (bf16[5,64,640]{2,1,0:T(8,128)(2,1)}, bf16[5,64,640]{2,1,0:T(8,128)(2,1)S(1)}, u32[]{:S(2)}, u32[]{:S(2)}) collective-permute-start(bf16[5,64,640]{2,1,0:T(8,128)(2,1)} %pad_maximum_fusion.5), channel_id=1, source_target_pairs={{0,1},{1,2},{2,3},{3,4},{4,5},{5,6},{6,7},{8,9},{9,10},{10,11},{11... | collective-permute-start | bytes 1228808 | tf_op jit(solution)/shard_map/ppermute | solution.py:16
  44.2 12.9 %copy-start.67 = (bf16[5,64,64]{2,1,0:T(8,128)(2,1)S(1)}, bf16[5,64,64]{2,1,0:T(8,128)(2,1)}, u32[]{:S(2)}) copy-start(bf16[5,64,64]{2,1,0:T(8,128)(2,1)} %param.42) | copy-start | bytes 122884
  50.2 9.6 copy-start.24
  57.1 149.4 %copy-start.38 = (bf16[5,64,320]{1,2,0:T(8,128)(2,1)}, bf16[5,64,320]{1,2,0:T(8,128)(2,1)S(1)}, u32[]{:S(2)}) copy-start(bf16[5,64,320]{1,2,0:T(8,128)(2,1)S(1)} %copy.138) | copy-start | bytes 614404
  59.8 146.0 %copy-start.55 = (f32[5,320,5]{1,0,2:T(8,128)}, f32[5,320,5]{1,0,2:T(8,128)S(1)}, u32[]{:S(2)}) copy-start(f32[5,320,5]{1,0,2:T(8,128)S(1)} %get-tuple-element.498) | copy-start | bytes 96004
  66.9 25.2 %copy-start.103 = (bf16[960]{0:T(1024)(128)(2,1)S(1)}, bf16[960]{0:T(1024)(128)(2,1)}, u32[]{:S(2)}) copy-start(bf16[960]{0:T(1024)(128)(2,1)} %param.43) | copy-start | bytes 5764
  71.9 483.3 %all-gather.11.cloned.1.call-start = ((), (), s32[]{:S(2)}) async-start(), calls=%async_computation.1 | async-start | bytes 3686400 | tf_op jit(solution)/shard_map/all_gather | solution.py:36
  111.3 9.0 copy-start.86
  148.5 10.7 copy-start.4
  148.5 10.7 copy-start.47
  163.4 11.4 copy-start.80
  163.4 42.4 %copy-start.57 = (f32[5,320,5]{1,0,2:T(8,128)S(1)}, f32[5,320,5]{1,0,2:T(8,128)}, u32[]{:S(2)}) copy-start(f32[5,320,5]{1,0,2:T(8,128)} %get-tuple-element.500) | copy-start | bytes 96004
  163.4 43.1 %copy-start.15 = (bf16[5,256,5,3,64]{1,0,4,3,2:T(8,128)(2,1)S(1)}, bf16[5,256,5,3,64]{1,0,4,3,2:T(8,128)(2,1)}, u32[]{:S(2)}) copy-start(bf16[5,256,5,3,64]{1,0,4,3,2:T(8,128)(2,1)} %reshape.335) | copy-start | bytes 7372804
  163.5 43.1 %copy-start.25 = (bf16[5,256,5,64]{1,3,0,2:T(8,128)(2,1)S(1)}, bf16[5,256,5,64]{1,3,0,2:T(8,128)(2,1)}, u32[]{:S(2)}) copy-start(bf16[5,256,5,64]{1,3,0,2:T(8,128)(2,1)} %copy-done.24) | copy-start | bytes 2457604
  332.0 12.0 copy-start.10
  332.0 12.0 copy-start.106
  344.0 12.1 copy-start.35
  381.4 10.4 copy-start.17
  398.3 24.0 %copy-start.28 = (bf16[5,320,5,64]{1,3,0,2:T(8,128)(2,1)S(1)}, bf16[5,320,5,64]{1,3,0,2:T(8,128)(2,1)}, u32[]{:S(2)}) copy-start(bf16[5,320,5,64]{1,3,0,2:T(8,128)(2,1)} %copy-done.27) | copy-start | bytes 3072004
  398.3 24.0 %copy-start.30 = (bf16[5,320,5,64]{1,3,0,2:T(8,128)(2,1)S(1)}, bf16[5,320,5,64]{1,3,0,2:T(8,128)(2,1)}, u32[]{:S(2)}) copy-start(bf16[5,320,5,64]{1,3,0,2:T(8,128)(2,1)} %copy-done.29) | copy-start | bytes 3072004
  398.3 24.0 %copy-start.79 = (f32[5,5,128]{2,0,1:T(8,128)S(1)}, f32[5,5,128]{2,0,1:T(8,128)}, u32[]{:S(2)}) copy-start(f32[5,5,128]{2,0,1:T(8,128)} %copy.163) | copy-start | bytes 38404
  422.3 12.3 copy-start.65
  422.3 12.3 copy-start.66
  434.7 9.3 slice-start.4
  434.7 9.3 slice-start.5
  434.7 9.5 slice-start.6
  434.7 9.5 copy-start.48
  434.7 9.5 copy-start.50
  444.0 9.9 slice-start.7
  444.3 9.6 slice-start.8
  444.3 9.6 slice-start.9
  465.2 9.5 copy-start.21
  465.2 9.5 copy-start.23
  481.3 293.8 %all-reduce.10.cloned.1.call-start = ((), (), s32[]{:S(2)}) async-start(), calls=%async_computation.2 | async-start | bytes 458752 | tf_op jit(solution)/shard_map/psum | solution.py:324
  530.9 12.4 copy-start.46
  543.3 11.9 copy-start.12
  543.3 11.9 copy-start.61
  590.5 13.3 %copy-start.41 = (bf16[5,320,5,64]{1,3,0,2:T(8,128)(2,1)}, bf16[5,320,5,64]{1,3,0,2:T(8,128)(2,1)S(1)}, u32[]{:S(2)}) copy-start(bf16[5,320,5,64]{1,3,0,2:T(8,128)(2,1)S(1)} %add_convert_fusion.4) | copy-start | bytes 3072004
  606.1 15.0 %collective-permute-start.1 = (bf16[5,64,640]{2,1,0:T(8,128)(2,1)}, bf16[5,64,640]{2,1,0:T(8,128)(2,1)}, u32[]{:S(2)}, u32[]{:S(2)}) collective-permute-start(bf16[5,64,640]{2,1,0:T(8,128)(2,1)} %pad_maximum_fusion.6), channel_id=1, source_target_pairs={{1,0},{2,1},{3,2},{4,3},{5,4},{6,5},{7,6},{9,8},{10,9},{11,10},{12... | collective-permute-start | bytes 1228808 | tf_op jit(solution)/shard_map/ppermute | solution.py:16
  636.8 9.4 copy-start.42
  646.0 596.4 %all-reduce.12.cloned.1.call-start = ((), (), s32[]{:S(2)}) async-start(), calls=%async_computation.3 | async-start | bytes 60293120 | tf_op jit(solution)/shard_map/psum | solution.py:324
  659.7 8.8 copy-start.82
  1259.2 17.1 %slice-start.10 = ((s8[9830400]{0:T(1024)(128)(4,1)}), s8[4194304]{0:T(1024)(128)(4,1)S(1)}, s32[]{:S(2)}) async-start(s8[9830400]{0:T(1024)(128)(4,1)} %bitcast.394), calls=%async_computation.14 | async-start | bytes 8388608
  1259.2 17.1 %slice-start.11 = ((s8[9830400]{0:T(1024)(128)(4,1)}), s8[4194304]{0:T(1024)(128)(4,1)S(1)}, s32[]{:S(2)}) async-start(s8[9830400]{0:T(1024)(128)(4,1)} %bitcast.394), calls=%async_computation.15 | async-start | bytes 8388608
  (82 other events, 363.0 us)
Sparse Core Ops, SparseCore 0:
  72.0 103.2 all-gather.8
  481.5 61.1 all-gather.10
  646.1 128.9 all-reduce.9
  783.7 458.6 all-reduce.11
where the time goes:
time: 1300 us; the launch traced here: 1290 us
  waiting for transfers between devices  554 us (43%)
  matrix products  348 us (27%)
  local copies, waits for them, and re-layouts  147 us (11%)
  other arithmetic  114 us (9%)
  blocking collectives  99.7 us (8%)
  between operations  16.2 us (1%)
    psum x2, waiting for transfers between devices, body(): lax.psum((grad_pregain, grad_querydown, grad_queryup, grad_keydown, grad_...  553 us
    dot_general x58, matrix products, contract(): return jnp.einsum(form, left, right, preferred_element_type=jnp.float32)  313 us
    unnamed x278, local copies, waits for them, and re-layouts  70 us
    unnamed x2, blocking collectives  37.8 us
    dot_general x6, matrix products, precise(): jnp.einsum(form, left, right, precision=EXACT, preferred_element_type=jnp...  34.8 us
    all_gather x1, blocking collectives, entering(): pieces = jax.tree.map(lambda part: lax.all_gather(part, axis), value)  31 us
    all_gather x1, blocking collectives, prefix_2(): lax.all_gather(part.astype(kind), axis)  30.9 us
  transfers between devices with their start and end apart: 6, of which 2 were waited for; matrix products, arithmetic and copies ran while one was open for 16% of the time, Pallas kernels for 0%

commit v1 on v0

v1 whole, which is shorter than its diff:
```python
import functools

import jax
import jax.numpy as jnp
from jax import lax
from jax.experimental import pallas as pl
from jax.experimental.pallas import tpu as pltpu
from jax.sharding import PartitionSpec as P

WINDOW = 64
EPSILON = 1e-05
BF = jnp.bfloat16
F32 = jnp.float32
NN = (((1,), (0,)), ((), ()))
NT = (((1,), (1,)), ((), ()))
TN = (((0,), (0,)), ((), ()))
HI = 4
TILE = 256
AUG = 80
VMEM = 62 << 20


def dot(left, right, dims=NN):
    return lax.dot_general(left, right, dims, preferred_element_type=F32)


def split_seq(index, count):
    low = max(count // HI, 1)
    return index // low, index % low, count // low, low


def rms(value):
    return lax.rsqrt(jnp.mean(value * value, axis=0, keepdims=True) + EPSILON)


def soft_pair(logit):
    top = jnp.max(logit, axis=0, keepdims=True)
    low = jnp.min(logit, axis=0, keepdims=True)
    up = jnp.exp(logit - top)
    down = jnp.exp(low - logit)
    up = up / jnp.sum(up, axis=0, keepdims=True)
    down = down / jnp.sum(down, axis=0, keepdims=True)
    return jnp.concatenate([up, down], axis=0).astype(BF)


def soft_pair_back(phi, grad):
    half = phi.shape[0] // 2
    up, down = phi[:half].astype(F32), phi[half:].astype(F32)
    gu, gd = grad[:half], grad[half:]
    gu = up * (gu - jnp.sum(up * gu, axis=0, keepdims=True))
    gd = down * (gd - jnp.sum(down * gd, axis=0, keepdims=True))
    return (gu - gd).astype(BF)


def qkv_kernel(tok, gain, wq, wkv, down, qkv, normed, inner, tails, ext):
    width = tok.shape[1]
    kv = wkv.shape[0]
    value = tok[0].astype(F32)
    norm = (value * rms(value) * gain[...]).astype(BF)
    normed[0] = norm
    low = dot(down[...], norm).astype(BF)
    inner[0] = low
    ext[0:width] = norm
    ext[width:] = jnp.zeros((ext.shape[0] - width, ext.shape[1]), BF)
    ext[width : width + low.shape[0]] = low
    qkv[0, 0:width] = dot(wq[...], ext[...], TN).astype(BF)
    both = dot(wkv[...], ext[...]).astype(BF)
    qkv[0, width:] = both
    span = tok.shape[2]
    tails[0] = jnp.concatenate(
        [both[: kv // 2, span - WINDOW :], both[kv // 2 :, span - WINDOW :]], axis=1
    )


def aug_value(value):
    extra = lax.broadcasted_iota(jnp.int32, (AUG - value.shape[0], value.shape[1]), 0) == 0
    return jnp.concatenate([value, jnp.where(extra, 1.0, 0.0).astype(BF)], axis=0)


def key_kernel(kv_heads, qkv, tails, kmap, keep, phi, con):
    head = kmap.shape[1]
    first = qkv.shape[1] - 2 * kv_heads * head
    keeping = keep[0].astype(BF)
    for k in range(kv_heads):
        at = first + k * head
        key = jnp.concatenate([qkv[0, at : at + head], tails[0, k * head : (k + 1) * head, :WINDOW]], axis=1)
        at += kv_heads * head
        val = jnp.concatenate([qkv[0, at : at + head], tails[0, k * head : (k + 1) * head, WINDOW:]], axis=1)
        feat = soft_pair(dot(kmap[k], key, TN))
        phi[0, k] = feat
        con[0, k * AUG : (k + 1) * AUG] = dot(aug_value(val), feat * keeping, NT).astype(BF)


def masks(segq, segk, span):
    extent = segk.shape[0]
    row = lax.broadcasted_iota(jnp.int32, (extent, span), 0)
    pos = jnp.where(row < span, row, row - extent)
    query = lax.broadcasted_iota(jnp.int32, (extent, span), 1)
    same = segk == segq
    far = pos + WINDOW <= query
    return same & far, same & (pos <= query) & jnp.logical_not(far)


def attend_kernel(
    kv_heads, group, qkv, tails, phik, state, segq, segk, qmap, tok, wo, down, gain,
    mixed, den, phiq, middle, normed, inner, ext, lin_bias, win_bias,
):
    head = qmap.shape[1]
    width = tok.shape[1]
    span = tok.shape[2]
    far, near = masks(segq[0], segk[0], span)
    lin_bias[...] = jnp.where(far, 1.0, 0.0)
    win_bias[...] = jnp.where(near, 0.0, -1e30)
    shown = jnp.where(segq[0] == 0, 1.0, 0.0)
    shown3 = jnp.concatenate([shown] * group, axis=1)
    den[0] = jnp.zeros_like(den[0])
    for k in range(kv_heads):
        at = width + k * head
        key = jnp.concatenate([qkv[0, at : at + head], tails[0, k * head : (k + 1) * head, :WINDOW]], axis=1)
        at += kv_heads * head
        val = jnp.concatenate([qkv[0, at : at + head], tails[0, k * head : (k + 1) * head, WINDOW:]], axis=1)
        queries, feats = [], []
        for h in range(k * group, (k + 1) * group):
            q = qkv[0, h * head : (h + 1) * head]
            f = soft_pair(dot(qmap[h], q, TN))
            phiq[0, h] = f
            queries.append(q)
            feats.append(f)
        query = jnp.concatenate(queries, axis=1) * (head**-0.5)
        feat = jnp.concatenate(feats, axis=1)
        lin = dot(phik[0, k], feat, TN)
        score = dot(key, query, TN)
        lb = jnp.concatenate([lin_bias[...]] * group, axis=1)
        wb = jnp.concatenate([win_bias[...]] * group, axis=1)
        weights = lin * lb + jnp.exp(score + wb)
        carried = dot(state[0, k * AUG : (k + 1) * AUG], feat) * shown3
        total = jnp.sum(weights, axis=0, keepdims=True) + carried[head : head + 1]
        numer = dot(val, weights.astype(BF)) + carried[:head]
        out = (numer / total).astype(BF)
        for g in range(group):
            h = k * group + g
            ext[h * head : (h + 1) * head] = out[:, g * span : (g + 1) * span]
            den[0, h : h + 1] = total[:, g * span : (g + 1) * span]
    got = ext[0:width]
    mixed[0] = got
    low = dot(down[...], got).astype(BF)
    inner[0] = low
    ext[width:] = jnp.zeros((ext.shape[0] - width, span), BF)
    ext[width : width + low.shape[0]] = low
    mid = tok[0].astype(F32) + dot(wo[...], ext[...], TN)
    middle[0] = mid
    normed[0] = (mid * rms(mid) * gain[...]).astype(BF)


def ff_kernel(
    width, normed_h, cot_h, middle, gain, gate_h, up_h, down_h,
    out, grad_mid, grad_gain, grads,
    normed, cot, gate_v, up_v, down_v, hid, dgate, dup, sem, act_sem,
):
    step = pl.program_id(0)
    rows = normed_h.shape[0]
    span = normed_h.shape[2]
    high = normed.shape[0]
    hidden = gate_h.shape[1]
    tiles = hidden // TILE

    def act_copies():
        made = []
        for r in range(rows):
            at = pl.ds(r * span, span)
            made.append(pltpu.make_async_copy(normed_h.at[r], normed.at[0:width, at], act_sem.at[r, 0]))
            made.append(pltpu.make_async_copy(cot_h.at[r], cot.at[0:width, at], act_sem.at[r, 1]))
        return made

    def tile_copies(j):
        at = pl.ds(pl.multiple_of(j * TILE, TILE), TILE)
        return [
            pltpu.make_async_copy(gate_h.at[:, at], gate_v.at[0:width, at], sem.at[j, 0]),
            pltpu.make_async_copy(up_h.at[:, at], up_v.at[0:width, at], sem.at[j, 1]),
            pltpu.make_async_copy(down_h.at[:, at], down_v.at[0:width, at], sem.at[j, 2]),
        ]

    @pl.when(step == 0)
    def _():
        for copy in act_copies():
            copy.start()
        for j in range(tiles):
            for copy in tile_copies(j):
                copy.start()
        for ref in (gate_v, up_v, down_v):
            ref[width:] = jnp.zeros((high - width, hidden), BF)
        for ref in (normed, cot):
            ref[width:] = jnp.zeros((high - width, rows * span), BF)
        for copy in act_copies():
            copy.wait()

    @pl.when(step < tiles)
    def _():
        for copy in tile_copies(step):
            copy.wait()
        at = pl.ds(pl.multiple_of(step * TILE, TILE), TILE)
        gate, up, down = gate_v[:, at], up_v[:, at], down_v[:, at]
        for r in range(rows):
            lane = pl.ds(r * span, span)
            n2 = normed[:, lane]
            g = dot(gate, n2, TN)
            u = dot(up, n2, TN)
            dh = dot(down, cot[:, lane], TN).astype(BF).astype(F32)
            sig = 1.0 / (1.0 + jnp.exp(-g))
            act = g * sig
            hid[at, lane] = (act * u).astype(BF)
            dup[at, lane] = (dh * act).astype(BF)
            dgate[at, lane] = (dh * u * (sig + act * (1.0 - sig))).astype(BF)
        grads[0, 0] = dot(normed[...], dgate[at, :], NT)[:width].astype(BF)
        grads[0, 1] = dot(normed[...], dup[at, :], NT)[:width].astype(BF)
        grads[0, 2] = dot(cot[...], hid[at, :], NT)[:width].astype(BF)

    @pl.when(step >= tiles)
    def _():
        r = step - tiles
        lane = pl.ds(pl.multiple_of(r * span, span), span)
        back = dot(gate_v[0:width], dgate[:, lane]) + dot(up_v[0:width], dup[:, lane])
        mid = middle[0]
        scale = rms(mid)
        unit = mid * scale
        grad_unit = back * gain[...]
        grad_mid[0] = cot[0:width, lane].astype(F32) + scale * (
            grad_unit - unit * jnp.mean(grad_unit * unit, axis=0, keepdims=True)
        )

        @pl.when(r == 0)
        def _():
            grad_gain[...] = jnp.zeros_like(grad_gain)

        grad_gain[...] += jnp.sum(back * unit, axis=1, keepdims=True)
        out[0] = (mid + dot(down_v[0:width], hid[:, lane])).astype(BF)


def pull_kernel(
    kv_heads, group, grad_mid, mixed, den, phiq, segq, inner, wo, down,
    dnum, dden, dstate, gup, gdown,
):
    width = mixed.shape[1]
    span = mixed.shape[2]
    head = width // (kv_heads * group)
    low = inner.shape[1]

    @pl.when(pl.program_id(0) == 0)
    def _():
        gup[...] = jnp.zeros_like(gup)
        gdown[...] = jnp.zeros_like(gdown)

    branch = grad_mid[0].astype(BF)
    wide = dot(wo[...], branch)
    grad_inner = wide[width : width + low].astype(BF)
    grad = (wide[:width] + dot(down[...], grad_inner, TN)).astype(BF).astype(F32)
    gup[...] += 2.0 * dot(inner[0], branch, NT)
    gdown[...] += dot(grad_inner, mixed[0], NT)
    shown = jnp.where(segq[0] == 0, 1.0, 0.0)
    dden[0] = jnp.zeros_like(dden[0])
    pad = jnp.zeros((AUG - head - 1, span), F32)
    for k in range(kv_heads):
        total = None
        for g in range(group):
            h = k * group + g
            at = pl.ds(h * head, head)
            dm = grad[h * head : (h + 1) * head]
            inv = 1.0 / den[0, h : h + 1]
            dd = -jnp.sum(dm * mixed[0, at].astype(F32), axis=0, keepdims=True) * inv
            dn = (dm * inv).astype(BF)
            dnum[0, at] = dn
            dden[0, h : h + 1] = dd
            aug = (jnp.concatenate([dn.astype(F32), dd, pad], axis=0) * shown).astype(BF)
            part = dot(aug, phiq[0, h], NT)
            total = part if total is None else total + part
        dstate[0, k * AUG : (k + 1) * AUG] = total.astype(BF)


def back_kernel(
    kv_heads, group, qkv, tails, phik, phiq, state, dcon, dnum, dden, segq, segk, keep, qmap, kmap,
    dq_out, dkv_out, dtails, gqmap, gkmap, lin_bias, win_bias,
):
    head = qmap.shape[1]
    width = dq_out.shape[1]
    span = dq_out.shape[2]
    scale = head**-0.5

    @pl.when(pl.program_id(0) == 0)
    def _():
        gqmap[...] = jnp.zeros_like(gqmap)
        gkmap[...] = jnp.zeros_like(gkmap)

    far, near = masks(segq[0], segk[0], span)
    lin_bias[...] = jnp.where(far, 1.0, 0.0)
    win_bias[...] = jnp.where(near, 0.0, -1e30)
    shown = jnp.where(segq[0] == 0, 1.0, 0.0)
    shown3 = jnp.concatenate([shown] * group, axis=1)
    keeping = keep[0]
    pad = jnp.zeros((AUG - head - 1, group * span), F32)
    for k in range(kv_heads):
        at = width + k * head
        key = jnp.concatenate([qkv[0, at : at + head], tails[0, k * head : (k + 1) * head, :WINDOW]], axis=1)
        at += kv_heads * head
        val = jnp.concatenate([qkv[0, at : at + head], tails[0, k * head : (k + 1) * head, WINDOW:]], axis=1)
        hs = range(k * group, (k + 1) * group)
        queries = [qkv[0, h * head : (h + 1) * head] for h in hs]
        query = jnp.concatenate(queries, axis=1) * scale
        feat = jnp.concatenate([phiq[0, h] for h in hs], axis=1)
        dn = jnp.concatenate([dnum[0, h * head : (h + 1) * head] for h in hs], axis=1)
        dd = jnp.concatenate([dden[0, h : h + 1] for h in hs], axis=1)
        kfeat = phik[0, k]
        lb = jnp.concatenate([lin_bias[...]] * group, axis=1)
        wb = jnp.concatenate([win_bias[...]] * group, axis=1)
        growth = jnp.exp(dot(key, query, TN) + wb)
        weights = (dot(kfeat, feat, TN) * lb + growth).astype(BF)
        dw = dot(val, dn, TN) + dd
        dlin = (dw * lb).astype(BF)
        dscore = (dw * growth).astype(BF)
        dv = dot(dn, weights, NT)
        aug = (jnp.concatenate([dn.astype(F32), dd, pad], axis=0) * shown3).astype(BF)
        held = state[0, k * AUG : (k + 1) * AUG]
        dfeat = dot(kfeat, dlin) + dot(held, aug, TN)
        con = dcon[0, k * AUG : (k + 1) * AUG]
        dkfeat = dot(feat, dlin, NT) + dot(con, aug_value(val), TN) * keeping
        dv = dv + dot(con[:head], kfeat * keeping.astype(BF))
        dq = dot(key, dscore) * scale
        dk = dot(query, dscore, NT)
        dt = soft_pair_back(feat, dfeat.astype(BF).astype(F32))
        for g in range(group):
            h = k * group + g
            part = dt[:, g * span : (g + 1) * span]
            gqmap[h] += dot(queries[g], part, NT)
            full = dq[:, g * span : (g + 1) * span] + dot(qmap[h], part)
            dq_out[0, h * head : (h + 1) * head] = full.astype(BF)
        dtk = soft_pair_back(kfeat, dkfeat.astype(BF).astype(F32))
        gkmap[k] += dot(key, dtk, NT)
        dk = dk + dot(kmap[k], dtk)
        ks, vs = k * head, (kv_heads + k) * head
        dkv_out[0, ks : ks + head] = dk[:, :span]
        dkv_out[0, vs : vs + head] = dv[:, :span]
        dtails[0, ks : ks + head] = jnp.concatenate([dk[:, span:], dv[:, span:]], axis=1).astype(BF)


def final_kernel(
    tok, grad_mid, gain, dq, dkv, returned, normed, inner, wq, wkv, down,
    grad_tok, ggain, gdown, gup,
):
    width = tok.shape[1]
    span = tok.shape[2]
    low = down.shape[0]

    @pl.when(pl.program_id(0) == 0)
    def _():
        ggain[...] = jnp.zeros_like(ggain)
        gdown[...] = jnp.zeros_like(gdown)
        gup[...] = jnp.zeros_like(gup)

    got = returned[0].astype(F32)
    got = jnp.concatenate([got[:, :WINDOW], got[:, WINDOW:]], axis=0)
    own = dkv[0]
    both = jnp.concatenate([own[:, : span - WINDOW], own[:, span - WINDOW :] + got], axis=1).astype(BF)
    grad_q = dq[0]
    wide = dot(wq[...], grad_q) + dot(wkv[...], both, TN)
    grad_inner = wide[width : width + low].astype(BF)
    back = wide[:width] + dot(down[...], grad_inner, TN)
    gdown[...] += dot(grad_inner, normed[0], NT)
    gup[:, :width] += 2.0 * dot(inner[0], grad_q, NT)
    gup[:, width:] += 2.0 * dot(inner[0], both, NT)
    value = tok[0].astype(F32)
    scale = rms(value)
    unit = value * scale
    grad_unit = back * gain[...]
    ggain[...] += jnp.sum(back * unit, axis=1, keepdims=True)
    grad_tok[0] = grad_mid[0] + scale * (
        grad_unit - unit * jnp.mean(grad_unit * unit, axis=0, keepdims=True)
    )


def row_spec(*shape):
    zeros = (0,) * len(shape)
    return pl.BlockSpec((1,) + shape, lambda r: (r,) + zeros)


def whole_spec(*shape):
    zeros = (0,) * len(shape)
    return pl.BlockSpec(shape, lambda r: zeros, pipeline_mode=pl.Buffered(1))


def shape_of(shape, kind):
    return jax.ShapeDtypeStruct(shape, kind)


def row_call(kernel, rows, args, outs, scratch=()):
    in_specs = [row_spec(*a.shape[1:]) if by_row else whole_spec(*a.shape) for a, by_row in args]
    out_specs = tuple(row_spec(*s[1:]) if by_row else pl.BlockSpec(s, functools.partial(lambda n, r: (0,) * n, len(s))) for s, _, by_row in outs)
    return pl.pallas_call(
        kernel,
        grid=(rows,),
        in_specs=in_specs,
        out_specs=out_specs,
        out_shape=tuple(shape_of(s, kind) for s, kind, _ in outs),
        scratch_shapes=list(scratch),
        compiler_params=pltpu.CompilerParams(vmem_limit_bytes=VMEM),
    )(*[a for a, _ in args])


def shifted(array, route):
    return lax.ppermute(array, "seq", route)


def fold(parts, keeps):
    total = None
    for part, keep in zip(parts, keeps):
        total = part if total is None else part + keep[:, None, None] * total
    return total


def carried_states(own, kept, index, count, reverse):
    hi, lo, n_hi, n_lo = split_seq(index, count)
    step = -1 if reverse else 1
    ranks = range(count)

    def keep_of(at):
        return lax.dynamic_slice_in_dim(kept, at, 1, 1)[:, 0]

    around = [own]
    for d in range(1, n_lo):
        route = [(i, i // n_lo * n_lo + (i % n_lo + d) % n_lo) for i in ranks]
        around.append(shifted(own, route))
    around = jnp.stack(around).astype(F32)
    order = list(range(n_lo))[::step]
    total = jnp.zeros_like(around[0])
    before = jnp.zeros_like(around[0])
    keep_all = jnp.ones_like(kept[:, 0])
    keep_before = keep_all
    for pos in order:
        here = lo == pos
        before = jnp.where(here, total, before)
        keep_before = jnp.where(here, keep_all, keep_before)
        part = lax.dynamic_index_in_dim(around, (lo - pos) % n_lo, 0, False)
        keep = keep_of(hi * n_lo + pos)
        total = part + keep[:, None, None] * total
        keep_all = keep * keep_all
    entering = jnp.zeros_like(total)
    for hop in range(n_hi - 1):
        leaving = (total + keep_all[:, None, None] * entering).astype(BF)
        route = [(i, i + step * n_lo) for i in ranks if 0 <= i + step * n_lo < count]
        got = shifted(leaving, route).astype(F32)
        at = n_hi - 2 - hop if reverse else hop + 1
        entering = jnp.where(hi == at, got, entering)
    return (before + keep_before[:, None, None] * entering).astype(BF)


def frames(doc_starts, index, count, span):
    rows = doc_starts.shape[0]
    padded = jnp.concatenate([jnp.zeros((rows, WINDOW), jnp.int32), doc_starts], axis=1)
    kept = jnp.sum(padded[:, : count * span].reshape(rows, count, span), axis=2) == 0
    marks = lax.dynamic_slice_in_dim(padded, index * span, span + WINDOW, 1)
    segment = jnp.cumsum(marks, axis=1)
    own, tail = segment[:, WINDOW:], segment[:, :WINDOW]
    last = own[:, span - WINDOW - 1 : span - WINDOW]
    keys = jnp.concatenate([own, tail], axis=1)
    valid = jnp.concatenate([jnp.arange(span) < span - WINDOW, jnp.full((WINDOW,), True)])
    keep = ((keys == last) & valid[None]).astype(F32)
    return kept.astype(F32), own[:, None, :], keys[:, :, None], keep[:, None, :]


def body(
    tokens, doc_starts, pregain, query_base, key_base, value_base, output_base, query_down, query_up,
    key_down, key_up, value_down, value_up, out_down, out_up, query_map, key_map, postgain, gate_proj,
    up_proj, down_proj, cotangent,
):
    rows, span, width = tokens.shape
    heads, head, _ = query_map.shape
    kv_heads = key_map.shape[0]
    group = heads // kv_heads
    kv_width = kv_heads * head
    rank = query_up.shape[0]
    extent = span + WINDOW
    hidden = gate_proj.shape[1]
    tiles = hidden // TILE
    high = -(-width // 256) * 256
    feats = 2 * head
    slots = -(-heads // 8) * 8
    count = lax.axis_size("seq")
    index = lax.axis_index("seq")

    tok = jnp.swapaxes(tokens, 1, 2)
    cot = jnp.swapaxes(cotangent, 1, 2)
    gain_one = pregain.astype(F32)[:, None]
    gain_two = postgain.astype(F32)[:, None]
    kept, segq, segk, keep = frames(doc_starts, index, count, span)

    zeros = functools.partial(jnp.zeros, dtype=BF)
    wq = jnp.concatenate([query_base, 2 * query_up, zeros((high - width - rank, width))], axis=0)
    kup = jnp.concatenate([zeros((kv_width, rank)), 2 * key_up.T, zeros((kv_width, high - width - 2 * rank))], axis=1)
    vup = jnp.concatenate([zeros((kv_width, 2 * rank)), 2 * value_up.T, zeros((kv_width, high - width - 3 * rank))], axis=1)
    wkv = jnp.concatenate(
        [jnp.concatenate([key_base.T, value_base.T], axis=0), jnp.concatenate([kup, vup], axis=0)], axis=1
    )
    wo = jnp.concatenate([output_base, 2 * out_up, zeros((high - width - rank, width))], axis=0)
    down = jnp.concatenate([query_down.T, key_down.T, value_down.T], axis=0)
    odown = out_down.T

    ext = pltpu.VMEM((high, span), BF)
    biases = [pltpu.VMEM((extent, span), F32)] * 2
    qkv, normed, inner, tails = row_call(
        qkv_kernel,
        rows,
        [(tok, 1), (gain_one, 0), (wq, 0), (wkv, 0), (down, 0)],
        [
            ((rows, width + 2 * kv_width, span), BF, 1),
            ((rows, width, span), BF, 1),
            ((rows, 3 * rank, span), BF, 1),
            ((rows, kv_width, 2 * WINDOW), BF, 1),
        ],
        [ext],
    )
    tails = shifted(tails, [(i, i + 1) for i in range(count - 1)])
    phik, con = row_call(
        functools.partial(key_kernel, kv_heads),
        rows,
        [(qkv, 1), (tails, 1), (key_map, 0), (keep, 1)],
        [((rows, kv_heads, feats, extent), BF, 1), ((rows, kv_heads * AUG, feats), BF, 1)],
    )
    state = carried_states(con, kept, index, count, False)
    mixed, den, phiq, middle, normed2, inner_o = row_call(
        functools.partial(attend_kernel, kv_heads, group),
        rows,
        [
            (qkv, 1), (tails, 1), (phik, 1), (state, 1), (segq, 1), (segk, 1), (query_map, 0), (tok, 1),
            (wo, 0), (odown, 0), (gain_two, 0),
        ],
        [
            ((rows, width, span), BF, 1),
            ((rows, slots, span), F32, 1),
            ((rows, heads, feats, span), BF, 1),
            ((rows, width, span), F32, 1),
            ((rows, width, span), BF, 1),
            ((rows, rank, span), BF, 1),
        ],
        [ext] + biases,
    )

    last = lambda s: (jnp.maximum(s - tiles, 0), 0, 0)
    fixed = lambda s: (0, 0)
    anywhere = pl.BlockSpec(memory_space=pl.ANY)
    layer_out, grad_mid, grad_postgain, grads = pl.pallas_call(
        functools.partial(ff_kernel, width),
        grid=(tiles + rows,),
        in_specs=[anywhere, anywhere, pl.BlockSpec((1, width, span), last), pl.BlockSpec((width, 1), fixed)]
        + [anywhere] * 3,
        out_specs=(
            pl.BlockSpec((1, width, span), last),
            pl.BlockSpec((1, width, span), last),
            pl.BlockSpec((width, 1), fixed),
            pl.BlockSpec((1, 3, width, TILE), lambda s: (jnp.minimum(s, tiles - 1), 0, 0, 0)),
        ),
        out_shape=(
            shape_of((rows, width, span), BF),
            shape_of((rows, width, span), F32),
            shape_of((width, 1), F32),
            shape_of((tiles, 3, width, TILE), BF),
        ),
        scratch_shapes=[pltpu.VMEM((high, rows * span), BF)] * 2
        + [pltpu.VMEM((high, hidden), BF)] * 3
        + [pltpu.VMEM((hidden, rows * span), BF)] * 3
        + [pltpu.SemaphoreType.DMA((tiles, 3)), pltpu.SemaphoreType.DMA((rows, 2))],
        compiler_params=pltpu.CompilerParams(vmem_limit_bytes=VMEM),
    )(normed2, cot, middle, gain_two, gate_proj, up_proj, down_proj.T)

    dnum, dden, dstate, gup_o, gdown_o = row_call(
        functools.partial(pull_kernel, kv_heads, group),
        rows,
        [
            (grad_mid, 1), (mixed, 1), (den, 1), (phiq, 1), (segq, 1), (inner_o, 1), (wo, 0), (odown, 0),
        ],
        [
            ((rows, width, span), BF, 1),
            ((rows, slots, span), F32, 1),
            ((rows, kv_heads * AUG, feats), BF, 1),
            ((rank, width), F32, 0),
            ((rank, width), F32, 0),
        ],
    )
    dcon = carried_states(dstate, kept, index, count, True)
    dq, dkv, dtails, gqmap, gkmap = row_call(
        functools.partial(back_kernel, kv_heads, group),
        rows,
        [
            (qkv, 1), (tails, 1), (phik, 1), (phiq, 1), (state, 1), (dcon, 1), (dnum, 1), (dden, 1),
            (segq, 1), (segk, 1), (keep, 1), (query_map, 0), (key_map, 0),
        ],
        [
            ((rows, width, span), BF, 1),
            ((rows, 2 * kv_width, span), F32, 1),
            ((rows, kv_width, 2 * WINDOW), BF, 1),
            ((heads, head, head), F32, 0),
            ((kv_heads, head, head), F32, 0),
        ],
        biases,
    )
    returned = shifted(dtails, [(i, i - 1) for i in range(1, count)])
    grad_tok, grad_pregain, gdown, gup = row_call(
        final_kernel,
        rows,
        [
            (tok, 1), (grad_mid, 1), (gain_one, 0), (dq, 1), (dkv, 1), (returned, 1), (normed, 1), (inner, 1),
            (wq, 0), (wkv, 0), (down, 0),
        ],
        [
            ((rows, width, span), F32, 1),
            ((width, 1), F32, 0),
            ((3 * rank, width), F32, 0),
            ((3 * rank, width + 2 * kv_width), F32, 0),
        ],
    )

    both = ("batch", "seq")
    small = lax.psum(
        (grad_pregain, gdown, gup, gdown_o, gup_o, gqmap, gkmap, grad_postgain), both
    )
    grad_pregain, gdown, gup, gdown_o, gup_o, gqmap, gkmap, grad_postgain = small
    grads = lax.psum(grads, both).astype(F32)
    grads = jnp.moveaxis(grads, 0, 2).reshape(3, width, hidden)
    ends = (width, width + kv_width, width + 2 * kv_width)
    return (
        jnp.swapaxes(layer_out, 1, 2),
        jnp.swapaxes(grad_tok, 1, 2),
        grad_pregain[:, 0],
        gdown[:rank].T,
        gup[:rank, : ends[0]],
        gdown[rank : 2 * rank].T,
        gup[rank : 2 * rank, ends[0] : ends[1]],
        gdown[2 * rank :].T,
        gup[2 * rank :, ends[1] :],
        gdown_o.T,
        gup_o,
        gqmap,
        gkmap,
        grad_postgain[:, 0],
        grads[0],
        grads[1],
        grads[2].T,
    )


def solution(mesh):
    wide = P("batch", "seq", None)
    return jax.shard_map(
        body,
        mesh=mesh,
        in_specs=(wide, P("batch", None)) + (P(),) * 19 + (wide,),
        out_specs=(wide, wide) + (P(),) * 15,
        check_vma=False,
    )
```

time: 1300 us -> 899 us (0.69)
  matrix products: 348 us -> 0 us
  Pallas kernels: 0 us -> 205 us
  blocking collectives: 99.7 us -> 0 us
  other arithmetic: 114 us -> 28.3 us
  local copies, waits for them, and re-layouts: 147 us -> 99.6 us
  waiting for transfers between devices: 554 us -> 520 us
  starting transfers between devices: 7.12 us -> 28.4 us
    dot_general x64 -> x0, matrix products: 348 us -> none  [the longest x58 313 us: contract(): return jnp.einsum(form, left, right, preferred_element_type=jnp.float32)]
    pallas_call x0 -> x7, Pallas kernels: none -> 205 us  [the longest x6 116 us: row_call(): pl.pallas_call(kernel, grid=(rows,), in_specs=in_specs, out_specs=out_spe...]
    psum x2 -> x3, waiting for transfers between devices: 553 us -> 430 us  [the longest x1 257 us: body(): grads = lax.psum(grads, both).astype(F32)]
    ppermute x2 -> x10, waiting for transfers between devices: 0.01 us -> 89.6 us  [shifted(): return lax.ppermute(array, 'seq', route)]
    all_gather x2 -> x0, blocking collectives: 61.9 us -> none  [the longest x1 31 us: entering(): pieces = jax.tree.map(lambda part: lax.all_gather(part, axis), value)]
    slice x13 -> x12, local copies, waits for them, and re-layouts: 7.87 us -> 52.2 us  [the longest x2 26 us: body(): grads[2]]
    unnamed x2 -> x0, blocking collectives: 37.8 us -> none
    unnamed x278 -> x32, local copies, waits for them, and re-layouts: 70 us -> 41.9 us
  transfers between devices with their start and end apart: 6 -> 13, of which waited for: 2 -> 13; matrix products, arithmetic and copies ran while one was open for 16% -> 10% of each run, Pallas kernels for 0% -> 0%
where the time goes in v1:
time: 899 us; the launch traced here: 896 us
  waiting for transfers between devices  520 us (58%)
  Pallas kernels  205 us (23%)
  local copies, waits for them, and re-layouts  99.6 us (11%)
  starting transfers between devices  28.4 us (3%)
  other arithmetic  28.3 us (3%)
  between operations  14.1 us (2%)
    psum x1, waiting for transfers between devices, body(): grads = lax.psum(grads, both).astype(F32)  257 us
    psum x2, waiting for transfers between devices, body(): lax.psum((grad_pregain, gdown, gup, gdown_o, gup_o, gqmap, gkmap, grad_po...  172 us
    pallas_call x6, Pallas kernels, row_call(): pl.pallas_call(kernel, grid=(rows,), in_specs=in_specs, out_specs=out_spe...  116 us
    ppermute x10, waiting for transfers between devices, shifted(): return lax.ppermute(array, 'seq', route)  89.6 us
    pallas_call x1, Pallas kernels, body(): pl.pallas_call(functools.partial(ff_kernel, width), grid=(tiles + rows,),...  89.2 us
    unnamed x32, local copies, waits for them, and re-layouts  41.9 us
    ppermute x10, starting transfers between devices, shifted(): return lax.ppermute(array, 'seq', route)  28 us
    slice x2, local copies, waits for them, and re-layouts, body(): grads[2]  26 us
  transfers between devices with their start and end apart: 13, of which 13 were waited for; matrix products, arithmetic and copies ran while one was open for 10% of the time, Pallas kernels for 0%

profile of v1, /device:TPU:0, one launch (start us, length us, event | category | flops | bytes accessed | tf_op | source)
XLA Modules:
  0.0 895.6 jit_solution(5301400404200632943)
XLA Ops:
  11.4 1.4 pad_maximum_fusion.down
  12.8 4.8 maximum_maximum_fusion.1
  17.7 1.4 maximum_maximum_fusion.2.wkv
  19.1 9.8 %shard_map.341 = (bf16[5,1600,256]{2,1,0:T(8,128)(2,1)}, bf16[5,960,256]{2,1,0:T(8,128)(2,1)}, bf16[5,24,256]{2,1,0:T(8,128)(2,1)}, bf16[5,320,128]{2,1,0:T(8,128)(2,1)}) custom-call(bf16[5,960,256]{2,1,0:T(8,128)(2,1)} %bitcast.69, f32[960,1]{1,0:T(8,128)} %copy.119.gain, bf16[1024,960]{1,0:T(8,128)(2,1)} %get-tuple-element.172.wq, ...), custom_call_target="tpu_custom_call" | custom-call | tf_op jit(solution)/shard_map/pallas_call | solution.py:396
  28.9 4.9 collective-permute-start
  33.9 1.5 reduce-window.6
  37.0 5.8 collective-permute-done.tails
  43.5 7.5 shard_map.342
  51.0 2.4 collective-permute-start.1
  53.8 10.6 %collective-permute-done.1 = bf16[5,400,128]{2,1,0:T(8,128)(2,1)S(1)} collective-permute-done((bf16[5,400,128]{2,1,0:T(8,128)(2,1)}, bf16[5,400,128]{2,1,0:T(8,128)(2,1)S(1)}, u32[]{:S(2)}, u32[]{:S(2)}) %collective-permute-start.1) | collective-permute-done | bytes 512032 | tf_op jit(solution)/shard_map/ppermute | solution.py:408
  66.6 5.4 collective-permute-start.2
  72.0 8.6 collective-permute-done.2
  80.7 2.0 add_convert_fusion.6
  82.7 5.2 collective-permute-start.3
  87.9 7.7 collective-permute-done.3
  95.6 2.2 add_convert_fusion.5
  97.8 4.4 collective-permute-start.4
  104.5 5.3 collective-permute-done.4
  109.7 2.3 add_convert_fusion.4.state
  112.1 27.4 %shard_map.343 = (bf16[5,960,256]{2,1,0:T(8,128)(2,1)}, f32[5,16,256]{2,1,0:T(8,128)}, bf16[5,15,128,256]{3,2,1,0:T(8,128)(2,1)}, f32[5,960,256]{2,1,0:T(8,128)}...) custom-call(bf16[5,1600,256]{2,1,0:T(8,128)(2,1)} %get-tuple-element.47.qkv, bf16[5,320,128]{2,1,0:T(8,128)(2,1)} %copy-done, ...), custom_call_target="tpu_custom_call" | custom-call | tf_op jit(solution)/shard_map/pallas_call | solution.py:396
  139.5 89.2 %shard_map.344 = (bf16[5,960,256]{2,1,0:T(8,128)(2,1)}, f32[5,960,256]{2,1,0:T(8,128)}, f32[960,1]{1,0:T(8,128)}, bf16[10,3,960,256]{3,2,1,0:T(8,128)(2,1)}) custom-call(bf16[5,960,256]{2,1,0:T(8,128)(2,1)} %get-tuple-element.51.normed_h, bf16[5,960,256]{2,1,0:T(8,128)(2,1)} %bitcast.74, f32[5,960,256]{2,1,0:T(8,128)} %get-tuple-element.52.middle, ...), custom_call_target="tpu_custom_call" | custom-call | tf_op jit(solution)/shard_map/pallas_call | solution.py:548
  228.6 16.8 %shard_map.345 = (bf16[5,960,256]{2,1,0:T(8,128)(2,1)}, f32[5,16,256]{2,1,0:T(8,128)}, bf16[5,400,128]{2,1,0:T(8,128)(2,1)}, f32[8,960]{1,0:T(8,128)}, f32[8,960]{1,0:T(8,128)}) custom-call(f32[5,960,256]{2,1,0:T(8,128)} %get-tuple-element.54.grad_mid, bf16[5,960,256]{2,1,0:T(8,128)(2,1)} %get-tuple-element.56.mixed, f32[5,16,256]{2,1,0:T(8,128)} %get-tuple-element.57.den, ...), custom_call_target="tpu_custom_call" | custom-call | tf_op jit(solution)/shard_map/pallas_call | solution.py:396
  246.0 8.7 collective-permute-done.5
  256.2 1.3 collective-permute-start.6
  257.5 12.0 %collective-permute-done.6 = bf16[5,400,128]{2,1,0:T(8,128)(2,1)S(1)} collective-permute-done((bf16[5,400,128]{2,1,0:T(8,128)(2,1)S(1)}, bf16[5,400,128]{2,1,0:T(8,128)(2,1)S(1)}, u32[]{:S(2)}, u32[]{:S(2)}) %collective-permute-start.6) | collective-permute-done | bytes 512032 | tf_op jit(solution)/shard_map/ppermute | solution.py:408
  269.7 1.3 collective-permute-start.7
  271.0 11.9 %collective-permute-done.7 = bf16[5,400,128]{2,1,0:T(8,128)(2,1)S(1)} collective-permute-done((bf16[5,400,128]{2,1,0:T(8,128)(2,1)S(1)}, bf16[5,400,128]{2,1,0:T(8,128)(2,1)S(1)}, u32[]{:S(2)}, u32[]{:S(2)}) %collective-permute-start.7) | collective-permute-done | bytes 512032 | tf_op jit(solution)/shard_map/ppermute | solution.py:408
  285.2 10.2 %collective-permute-done.8 = bf16[5,400,128]{2,1,0:T(8,128)(2,1)} collective-permute-done((bf16[5,400,128]{2,1,0:T(8,128)(2,1)}, bf16[5,400,128]{2,1,0:T(8,128)(2,1)}, u32[]{:S(2)}, u32[]{:S(2)}) %collective-permute-start.8) | collective-permute-done | bytes 512032 | tf_op jit(solution)/shard_map/ppermute | solution.py:408
  295.5 2.2 add_convert_fusion.dcon
  297.7 37.5 %shard_map.346 = (bf16[5,960,256]{2,1,0:T(8,128)(2,1)}, f32[5,640,256]{2,1,0:T(8,128)}, bf16[5,320,128]{2,1,0:T(8,128)(2,1)}, f32[15,64,64]{2,1,0:T(8,128)}, f32[5,64,64]{2,1,0:T(8,128)}) custom-call(bf16[5,1600,256]{2,1,0:T(8,128)(2,1)} %get-tuple-element.47.qkv, bf16[5,320,128]{2,1,0:T(8,128)(2,1)} %copy-done, ...), custom_call_target="tpu_custom_call" | custom-call | tf_op jit(solution)/shard_map/pallas_call | solution.py:396
  335.2 1.3 collective-permute-start.9
  336.5 8.8 collective-permute-done.9.returned
  346.0 17.2 %shard_map.347 = (f32[5,960,256]{2,1,0:T(8,128)}, f32[960,1]{1,0:T(8,128)}, f32[24,960]{1,0:T(8,128)}, f32[24,1600]{1,0:T(8,128)}) custom-call(bf16[5,960,256]{2,1,0:T(8,128)(2,1)} %bitcast.71, f32[5,960,256]{2,1,0:T(8,128)} %get-tuple-element.54.grad_mid, f32[960,1]{1,0:T(8,128)} %copy.119.gain, bf16[5,960,256]{2,1,0:T(8,128)(2,1)} %get-tuple-element.62.dq, ...), custom_call_target="tpu_custom_call" | custom-call | tf_op jit(solution)/shard_map/pallas_call | solution.py:396
  365.9 128.8 %all-reduce.13.cloned.1.call-done = (f32[24,960]{1,0:T(8,128)}, f32[24,1600]{1,0:T(8,128)}, f32[15,64,64]{2,1,0:T(8,128)}, f32[5,64,64]{2,1,0:T(8,128)}) async-done(((f32[24,960]{1,0:T(8,128)}, f32[24,1600]{1,0:T(8,128)}, f32[15,64,64]{2,1,0:T(8,128)}, f32[5,64,64]{2,1,0:T(8,128)}), (f32[24,960]{1,0:T(8,128)}, f32[24,1600]{1,0:T(8,128)}, f32[15,64,64]{2,1,0:T(8,128)}, ...) | async-done | bytes 573456 | tf_op jit(solution)/shard_map/psum | solution.py:620
  494.7 1.4 slice.75
  496.1 1.4 fusion.1
  497.5 1.4 slice_bitcast_fusion
  498.9 257.2 %all-reduce.9.cloned.1.call-done = bf16[3,960,10,256]{3,1,0,2:T(8,128)(2,1)} async-done(((bf16[3,960,10,256]{3,1,0,2:T(8,128)(2,1)}), bf16[3,960,10,256]{3,1,0,2:T(8,128)(2,1)}) %all-reduce.9.cloned.1.call-update) | async-done | bytes 14745616 | tf_op jit(solution)/shard_map/psum | solution.py:624
  756.1 14.6 %fusion = (f32[1,960,10,256]{3,1,0,2:T(8,128)}, f32[1,960,10,256]{3,1,0,2:T(8,128)}, f32[1,960,10,256]{3,1,0,2:T(8,128)}) fusion(bf16[3,960,10,256]{3,1,0,2:T(8,128)(2,1)} %all-reduce.9.cloned.1.call-done), kind=kLoop, calls=%fused_computation.47 | loop fusion | bytes 58982400 | tf_op jit(solution)/shard_map/slice | solution.py:644
  770.7 11.4 %copy.131 = f32[1,960,10,256]{1,3,2,0:T(8,128)} copy(f32[1,960,10,256]{3,1,0,2:T(8,128)} %get-tuple-element.163) | data formatting | bytes 19660800 | tf_op jit(solution)/shard_map/slice | solution.py:642
  782.1 11.2 %copy.134 = f32[960,2560]{1,0:T(8,128)} copy(f32[960,2560]{0,1:T(8,128)} %bitcast.66) | data formatting | bytes 19660800
  793.4 11.4 %copy.132 = f32[1,960,10,256]{1,3,2,0:T(8,128)} copy(f32[1,960,10,256]{3,1,0,2:T(8,128)} %get-tuple-element.162) | data formatting | bytes 19660800 | tf_op jit(solution)/shard_map/slice | solution.py:643
  804.8 11.2 %copy.135 = f32[960,2560]{1,0:T(8,128)} copy(f32[960,2560]{0,1:T(8,128)} %bitcast.67) | data formatting | bytes 19660800
  815.9 11.4 %copy.133 = f32[1,960,10,256]{1,3,2,0:T(8,128)} copy(f32[1,960,10,256]{3,1,0,2:T(8,128)} %get-tuple-element.161) | data formatting | bytes 19660800 | tf_op jit(solution)/shard_map/slice | solution.py:644
  827.4 11.2 %copy.136 = f32[2560,960]{0,1:T(8,128)} copy(f32[2560,960]{1,0:T(8,128)} %bitcast.68) | data formatting | bytes 19660800
  838.6 43.7 %all-reduce.11.cloned.1.call-done = (f32[960]{0:T(1024)}, f32[960,8]{0,1:T(8,128)}, f32[8,960]{1,0:T(8,128)}, f32[960]{0:T(1024)}) async-done(((f32[960]{0:T(1024)}, f32[960,8]{0,1:T(8,128)}, f32[8,960]{1,0:T(8,128)}, f32[960]{0:T(1024)}), (f32[960]{0:T(1024)}, f32[960,8]{0,1:T(8,128)}, f32[8,960]{1,0:T(8,128)}, f32[960]{0:T(1024)})) %all-reduce.11.cloned.1.call-update) | async-done | bytes 69136 | tf_op jit(solution)/shard_map/psum | solution.py:620
  883.6 1.4 copy.152
  885.0 1.4 copy.153
  (81 shorter events, 23.6 us)
Async XLA Ops:
  7.2 487.5 %all-reduce.13.cloned.1.call-start = ((), (), s32[]{:S(2)}) async-start(), calls=%async_computation.2 | async-start | bytes 1826816 | tf_op jit(solution)/shard_map/psum | solution.py:620
  12.8 4.9 copy-start.1
  12.8 4.9 copy-start.2
  19.1 14.7 %copy-start.7 = (s32[5,2048]{1,0:T(8,128)S(1)}, s32[5,2048]{1,0:T(8,128)}, u32[]{:S(2)}) copy-start(s32[5,2048]{1,0:T(8,128)} %param.23) | copy-start | bytes 122884
  28.9 13.9 %collective-permute-start = (bf16[5,320,128]{2,1,0:T(8,128)(2,1)}, bf16[5,320,128]{2,1,0:T(8,128)(2,1)S(1)}, u32[]{:S(2)}, u32[]{:S(2)}) collective-permute-start(bf16[5,320,128]{2,1,0:T(8,128)(2,1)} %get-tuple-element.48), channel_id=1, source_target_pairs={{0,1},{1,2},{2,3},{3,4},{4,5},{5,6},{6,7},{8,9},{9,10},{10,11},{11... | collective-permute-start | bytes 1228808 | tf_op jit(solution)/shard_map/ppermute | solution.py:408
  36.2 29.3 %copy-start.9 = (s32[5,1,256]{2,1,0:T(1,128)}, s32[5,1,256]{2,1,0:T(1,128)S(1)}, u32[]{:S(2)}) copy-start(s32[5,1,256]{2,1,0:T(1,128)S(1)} %copy.122.segq) | copy-start | bytes 15364
  42.8 0.7 copy-start
  51.0 13.4 %collective-permute-start.1 = (bf16[5,400,128]{2,1,0:T(8,128)(2,1)}, bf16[5,400,128]{2,1,0:T(8,128)(2,1)S(1)}, u32[]{:S(2)}, u32[]{:S(2)}) collective-permute-start(bf16[5,400,128]{2,1,0:T(8,128)(2,1)} %get-tuple-element.50), channel_id=1, source_target_pairs={{0,1},{1,0},{2,3},{3,2},{4,5},{5,4},{6,7},{7,6},{8,9},{9,8},{10,11... | collective-permute-start | bytes 1536008 | tf_op jit(solution)/shard_map/ppermute | solution.py:408
  66.6 14.1 %collective-permute-start.2 = (bf16[5,400,128]{2,1,0:T(8,128)(2,1)}, bf16[5,400,128]{2,1,0:T(8,128)(2,1)}, u32[]{:S(2)}, u32[]{:S(2)}) collective-permute-start(bf16[5,400,128]{2,1,0:T(8,128)(2,1)} %get-tuple-element.157), channel_id=1, source_target_pairs={{0,2},{1,3},{2,4},{3,5},{4,6},{5,7},{8,10},{9,11},{10,12},{11,13},... | collective-permute-start | bytes 1536008 | tf_op jit(solution)/shard_map/ppermute | solution.py:408
  80.7 22.8 %copy-start.10 = (bf16[960]{0:T(1024)(128)(2,1)S(1)}, bf16[960]{0:T(1024)(128)(2,1)}, u32[]{:S(2)}) copy-start(bf16[960]{0:T(1024)(128)(2,1)} %param.39) | copy-start | bytes 5764
  82.7 12.9 %collective-permute-start.3 = (bf16[5,400,128]{2,1,0:T(8,128)(2,1)}, bf16[5,400,128]{2,1,0:T(8,128)(2,1)}, u32[]{:S(2)}, u32[]{:S(2)}) collective-permute-start(bf16[5,400,128]{2,1,0:T(8,128)(2,1)} %add_convert_fusion.6), channel_id=1, source_target_pairs={{0,2},{1,3},{2,4},{3,5},{4,6},{5,7},{8,10},{9,11},{10,12},{11,13},... | collective-permute-start | bytes 1536008 | tf_op jit(solution)/shard_map/ppermute | solution.py:408
  97.8 12.0 %collective-permute-start.4 = (bf16[5,400,128]{2,1,0:T(8,128)(2,1)}, bf16[5,400,128]{2,1,0:T(8,128)(2,1)S(1)}, u32[]{:S(2)}, u32[]{:S(2)}) collective-permute-start(bf16[5,400,128]{2,1,0:T(8,128)(2,1)} %add_convert_fusion.5), channel_id=1, source_target_pairs={{0,2},{1,3},{2,4},{3,5},{4,6},{5,7},{8,10},{9,11},{10,12},{11,13},... | collective-permute-start | bytes 1536008 | tf_op jit(solution)/shard_map/ppermute | solution.py:408
  245.4 9.3 %collective-permute-start.5 = (bf16[5,400,128]{2,1,0:T(8,128)(2,1)}, bf16[5,400,128]{2,1,0:T(8,128)(2,1)S(1)}, u32[]{:S(2)}, u32[]{:S(2)}) collective-permute-start(bf16[5,400,128]{2,1,0:T(8,128)(2,1)} %get-tuple-element.59), channel_id=1, source_target_pairs={{0,1},{1,0},{2,3},{3,2},{4,5},{5,4},{6,7},{7,6},{8,9},{9,8},{10,11... | collective-permute-start | bytes 1536008 | tf_op jit(solution)/shard_map/ppermute | solution.py:408
  256.2 13.3 %collective-permute-start.6 = (bf16[5,400,128]{2,1,0:T(8,128)(2,1)S(1)}, bf16[5,400,128]{2,1,0:T(8,128)(2,1)S(1)}, u32[]{:S(2)}, u32[]{:S(2)}) collective-permute-start(bf16[5,400,128]{2,1,0:T(8,128)(2,1)S(1)} %get-tuple-element.155), channel_id=1, source_target_pairs={{2,0},{3,1},{4,2},{5,3},{6,4},{7,5},{10,8},{11,9},{12,10},{13,11},... | collective-permute-start | bytes 1536008 | tf_op jit(solution)/shard_map/ppermute | solution.py:408
  269.7 13.2 %collective-permute-start.7 = (bf16[5,400,128]{2,1,0:T(8,128)(2,1)S(1)}, bf16[5,400,128]{2,1,0:T(8,128)(2,1)S(1)}, u32[]{:S(2)}, u32[]{:S(2)}) collective-permute-start(bf16[5,400,128]{2,1,0:T(8,128)(2,1)S(1)} %add_convert_fusion.2), channel_id=1, source_target_pairs={{2,0},{3,1},{4,2},{5,3},{6,4},{7,5},{10,8},{11,9},{12,10},{13,11},... | collective-permute-start | bytes 1536008 | tf_op jit(solution)/shard_map/ppermute | solution.py:408
  284.0 11.5 %collective-permute-start.8 = (bf16[5,400,128]{2,1,0:T(8,128)(2,1)}, bf16[5,400,128]{2,1,0:T(8,128)(2,1)}, u32[]{:S(2)}, u32[]{:S(2)}) collective-permute-start(bf16[5,400,128]{2,1,0:T(8,128)(2,1)} %add_convert_fusion.1), channel_id=1, source_target_pairs={{2,0},{3,1},{4,2},{5,3},{6,4},{7,5},{10,8},{11,9},{12,10},{13,11},... | collective-permute-start | bytes 1536008 | tf_op jit(solution)/shard_map/ppermute | solution.py:408
  335.2 10.1 %collective-permute-start.9 = (bf16[5,320,128]{2,1,0:T(8,128)(2,1)}, bf16[5,320,128]{2,1,0:T(8,128)(2,1)S(1)}, u32[]{:S(2)}, u32[]{:S(2)}) collective-permute-start(bf16[5,320,128]{2,1,0:T(8,128)(2,1)} %get-tuple-element.64), channel_id=1, source_target_pairs={{1,0},{2,1},{3,2},{4,3},{5,4},{6,5},{7,6},{9,8},{10,9},{11,10},{12... | collective-permute-start | bytes 1228808 | tf_op jit(solution)/shard_map/ppermute | solution.py:408
  345.2 0.8 copy-start.6
  363.2 392.9 %all-reduce.9.cloned.1.call-start = ((), (), s32[]{:S(2)}) async-start(), calls=%async_computation | async-start | bytes 29491200 | tf_op jit(solution)/shard_map/psum | solution.py:624
  363.3 1.0 copy-start.3
  363.3 1.8 copy-start.5
  364.0 518.4 %all-reduce.11.cloned.1.call-start = ((), (), s32[]{:S(2)}) async-start(), calls=%async_computation.1 | async-start | bytes 147456 | tf_op jit(solution)/shard_map/psum | solution.py:620
  827.4 59.0 %copy-start.4 = (f32[15,64,64]{2,1,0:T(8,128)S(1)}, f32[15,64,64]{2,1,0:T(8,128)}, u32[]{:S(2)}) copy-start(f32[15,64,64]{2,1,0:T(8,128)} %get-tuple-element.192) | copy-start | bytes 737284
  827.4 59.7 %copy-start.8 = (f32[5,64,64]{2,1,0:T(8,128)S(1)}, f32[5,64,64]{2,1,0:T(8,128)}, u32[]{:S(2)}) copy-start(f32[5,64,64]{2,1,0:T(8,128)} %get-tuple-element.193) | copy-start | bytes 245764
Sparse Core Ops, SparseCore 0:
  363.3 131.3 all-reduce.12
  501.0 255.0 all-reduce.8
  763.4 118.8 all-reduce.10

commit v2 on v1

--- a/solution.py
+++ b/solution.py
@@ -18,6 +18,7 @@
 TILE = 256
 AUG = 80
 VMEM = 62 << 20
+MESH = pl.DeviceIdType.MESH
 
 
 def dot(left, right, dims=NN):
@@ -27,6 +28,456 @@
 def split_seq(index, count):
     low = max(count // HI, 1)
     return index // low, index % low, count // low, low
+
+
+class Place:
+    def __init__(self):
+        batch, seq = lax.axis_index("batch"), lax.axis_index("seq")
+        n_seq = lax.axis_size("seq")
+        hi, lo, n_hi, n_lo = split_seq(seq, n_seq)
+        self.batch, self.seq = batch, seq
+        self.at = {"core": batch % 2, "y": batch // 2, "hi": hi, "lo": lo}
+        self.size = axis_sizes()
+
+    def peer(self, axis, distance):
+        at = dict(self.at)
+        at[axis] = (at[axis] + distance) % self.size[axis]
+        return (at["y"] * 2 + at["core"], at["hi"] * self.size["lo"] + at["lo"])
+
+    def along(self, distance):
+        return (self.batch, self.seq + distance)
+
+    def inside(self, distance):
+        return (self.seq + distance >= 0) & (self.seq + distance < self.size["hi"] * self.size["lo"])
+
+    def greet(self):
+        barrier = pltpu.get_barrier_semaphore()
+        total = 0
+        for d in (-1, 1):
+
+            @pl.when(self.inside(d))
+            def _():
+                pl.semaphore_signal(barrier, inc=1, device_id=self.along(d), device_id_type=MESH)
+
+            total = total + jnp.where(self.inside(d), 1, 0)
+        for axis, size in self.size.items():
+            for d in range(1, size):
+                pl.semaphore_signal(barrier, inc=1, device_id=self.peer(axis, d), device_id_type=MESH)
+                total = total + 1
+        pl.semaphore_wait(barrier, total)
+
+
+def axis_sizes():
+    _, _, n_hi, n_lo = split_seq(0, lax.axis_size("seq"))
+    return {"core": 2, "y": lax.axis_size("batch") // 2, "hi": n_hi, "lo": n_lo}
+
+
+def stream_plan(rows):
+    size = axis_sizes()
+    orders = [("lo", "y", "hi"), ("y", "lo", "hi")]
+    devices = size["lo"] * size["y"] * size["hi"]
+    if rows // (2 * devices) % 16:
+        orders = orders[:1]
+    part = rows // len(orders)
+    plan = []
+    for i, order in enumerate(orders):
+        left, stages = part, []
+        for axis in order:
+            left = left // size[axis]
+            stages.append((axis, left))
+        plan.append((i * part, part, stages))
+    return plan
+
+
+def remote(src, dst, send, recv, peer):
+    return pltpu.make_async_remote_copy(
+        src_ref=src, dst_ref=dst, send_sem=send, recv_sem=recv, device_id=peer, device_id_type=MESH
+    )
+
+
+LAGS = (1, 3, 4, 5)
+
+
+def stage_slots(k, slots):
+    return 2 * slots if k == 1 else slots
+
+
+def scatter_scratch(rows, kind, slots=2):
+    size = axis_sizes()
+    made = [
+        pltpu.VMEM((slots, 2, rows, 128), kind),
+        pltpu.VMEM((slots, rows, 128), kind),
+        pltpu.VMEM((stage_slots(1, slots), rows, 128), kind),
+        pltpu.SemaphoreType.DMA((2, slots)),
+    ]
+    for _, _, stages in stream_plan(rows):
+        for k, (axis, left) in enumerate(stages, 1):
+            peers = max(size[axis] - 1, 1)
+            made.append(pltpu.VMEM((stage_slots(k, slots), peers, left, 128), kind))
+            made.append(pltpu.VMEM((slots, left, 128), kind))
+            made.append(pltpu.SemaphoreType.DMA((2, stage_slots(k, slots), peers)))
+    return made
+
+
+class Scatter:
+    def __init__(self, place, rows, refs, slots=2):
+        self.place, self.rows, self.slots = place, rows, slots
+        self.mine, self.other, self.base, self.core_sem = refs[:4]
+        self.streams = []
+        at = 4
+        for first, part, stages in stream_plan(rows):
+            made = []
+            for axis, left in stages:
+                made.append((axis, left) + tuple(refs[at : at + 3]))
+                at += 3
+            self.streams.append((first, part, made))
+
+    def core_copy(self, t):
+        slot = t % self.slots
+        core = self.place.at["core"]
+        return remote(
+            self.mine.at[slot, 1 - core], self.other.at[slot],
+            self.core_sem.at[0, slot], self.core_sem.at[1, slot], self.place.peer("core", 1),
+        )
+
+    def copies(self, k, t):
+        slot = t % stage_slots(k, self.slots)
+        made = []
+        for first, part, stages in self.streams:
+            axis, left, got, _, sem = stages[k - 1]
+            size = self.place.size[axis]
+            for d in range(1, size):
+                to = (self.place.at[axis] + d) % size
+                if k == 1:
+                    src = self.base.at[slot, pl.ds(pl.multiple_of(first + to * left, 16), left)]
+                else:
+                    src = stages[k - 2][3].at[t % self.slots, pl.ds(pl.multiple_of(to * left, 16), left)]
+                made.append(
+                    remote(
+                        src, got.at[slot, d - 1], sem.at[0, slot, d - 1], sem.at[1, slot, d - 1],
+                        self.place.peer(axis, d),
+                    )
+                )
+        return made
+
+    def start(self, k, t):
+        for copy in [self.core_copy(t)] if k == 0 else self.copies(k, t):
+            copy.start()
+
+    def finish(self, k, t, into=None):
+        slot = t % self.slots
+        ahead = t % stage_slots(k, self.slots)
+        if k == 0:
+            self.core_copy(t).wait()
+            core = self.place.at["core"]
+            self.base[t % stage_slots(1, self.slots)] = (self.mine[slot, core].astype(F32) + self.other[slot].astype(F32)).astype(self.base.dtype)
+            return
+        for copy in self.copies(k, t):
+            copy.wait()
+        for i, (first, part, stages) in enumerate(self.streams):
+            axis, left, got, out, _ = stages[k - 1]
+            at = self.place.at[axis] * left
+            if k == 1:
+                own = self.base[ahead, pl.ds(pl.multiple_of(first + at, 16), left)]
+            else:
+                own = stages[k - 2][3][slot, pl.ds(pl.multiple_of(at, 16), left)]
+            total = own.astype(F32)
+            for d in range(1, self.place.size[axis]):
+                total = total + got[ahead, d - 1].astype(F32)
+            if k == 3:
+                into(i, total)
+            else:
+                out[slot] = total.astype(out.dtype)
+
+    def run(self, into):
+        self.start(0, 0)
+        for k in range(4):
+            self.finish(k, 0, into)
+            if k < 3:
+                self.start(k + 1, 0)
+
+    def turn(self, step, tiles, into):
+        for k in (3, 2, 1, 0):
+            t = step - LAGS[k]
+
+            @pl.when((t >= 0) & (t < tiles))
+            def _():
+                self.finish(k, t, functools.partial(into, t))
+                if k < 3:
+                    self.start(k + 1, t)
+
+        @pl.when(step < tiles)
+        def _():
+            self.start(0, step)
+
+
+WAYS = (6, 5, 3, 1)
+
+
+def gather_scratch(rows, tiles):
+    size = axis_sizes()
+    made = [pltpu.SemaphoreType.DMA((2, tiles)), pltpu.SemaphoreType.DMA((tiles, len(stream_plan(rows))))]
+    for _, _, stages in stream_plan(rows):
+        for axis, left in stages:
+            made.append(pltpu.SemaphoreType.DMA((2, tiles, max(size[axis] - 1, 1))))
+    return made
+
+
+class Gather:
+    def __init__(self, place, rows, shards, whole, refs):
+        self.place, self.rows, self.shards, self.whole = place, rows, shards, whole
+        self.core_sem, self.own_sem = refs[:2]
+        self.streams = []
+        at = 2
+        for first, part, stages in stream_plan(rows):
+            self.streams.append((first, part, [st + (refs[at + i],) for i, st in enumerate(stages)]))
+            at += len(stages)
+
+    def region(self, t, stream, k):
+        first, _, stages = self.streams[stream]
+        at = first
+        for axis, left, _ in stages[:k]:
+            at = at + self.place.at[axis] * left
+        return self.whole.at[t, self.place.at["core"], pl.ds(pl.multiple_of(at, 16), stages[k - 1][1])]
+
+    def own_copies(self, t):
+        return [
+            pltpu.make_async_copy(self.shards.at[t, i], self.region(t, i, 3), self.own_sem.at[t, i])
+            for i in range(len(self.streams))
+        ]
+
+    def copies(self, k, t):
+        if k == 0:
+            half = self.whole.at[t, self.place.at["core"]]
+            return [remote(half, half, self.core_sem.at[0, t], self.core_sem.at[1, t], self.place.peer("core", 1))]
+        made = []
+        for i, (_, _, stages) in enumerate(self.streams):
+            axis, left, sem = stages[k - 1]
+            dst = self.region(t, i, k)
+            src = self.shards.at[t, i] if k == 3 else dst
+            for d in range(1, self.place.size[axis]):
+                made.append(remote(src, dst, sem.at[0, t, d - 1], sem.at[1, t, d - 1], self.place.peer(axis, d)))
+        return made
+
+    def run(self):
+        for copy in self.own_copies(0) + self.copies(3, 0):
+            copy.start()
+        for k in (3, 2, 1, 0):
+            for copy in self.copies(k, 0) + (self.own_copies(0) if k == 3 else []):
+                copy.wait()
+            if k > 0:
+                for copy in self.copies(k - 1, 0):
+                    copy.start()
+
+    def turn(self, step, tiles):
+        for k in (0, 1, 2, 3):
+            t = step - WAYS[k]
+
+            @pl.when((t >= 0) & (t < tiles))
+            def _():
+                for copy in self.copies(k, t):
+                    copy.wait()
+                if k == 3:
+                    for copy in self.own_copies(t):
+                        copy.wait()
+                if k > 0:
+                    for copy in self.copies(k - 1, t):
+                        copy.start()
+
+        @pl.when(step < tiles)
+        def _():
+            for copy in self.own_copies(step) + self.copies(3, step):
+                copy.start()
+
+
+class Chain:
+    def __init__(self, place, reverse, kept, own, around, total, before, leaving, entering, result, lo_sem, hi_sem):
+        self.place, self.reverse, self.kept = place, reverse, kept
+        self.own, self.around, self.total, self.before = own, around, total, before
+        self.leaving, self.entering, self.result = leaving, entering, result
+        self.lo_sem, self.hi_sem = lo_sem, hi_sem
+        self.n_hi, self.n_lo = place.size["hi"], place.size["lo"]
+        hi = place.at["hi"]
+        self.rank = self.n_hi - 1 - hi if reverse else hi
+
+    def lo_copies(self, r):
+        return [
+            remote(
+                self.own.at[r], self.around.at[d - 1, r], self.lo_sem.at[0, r, d - 1], self.lo_sem.at[1, r, d - 1],
+                self.place.peer("lo", d),
+            )
+            for d in range(1, self.n_lo)
+        ]
+
+    def hi_copy(self, r):
+        return remote(
+            self.leaving.at[r], self.entering.at[r], self.hi_sem.at[0, r], self.hi_sem.at[1, r],
+            self.place.peer("hi", -1 if self.reverse else 1),
+        )
+
+    def keep(self, r, pos):
+        return self.kept[r, self.place.at["hi"] * self.n_lo + pos]
+
+    def order(self):
+        return list(range(self.n_lo))[:: -1 if self.reverse else 1]
+
+    def begin(self, r):
+        for copy in self.lo_copies(r):
+            copy.start()
+
+    def leave(self, r, value):
+        @pl.when(self.rank < self.n_hi - 1)
+        def _():
+            self.leaving[r] = value.astype(BF)
+            self.hi_copy(r).start()
+
+    def join(self, r):
+        for copy in self.lo_copies(r):
+            copy.wait()
+        lo = self.place.at["lo"]
+        total = jnp.zeros(self.own.shape[1:], F32)
+        before = total
+        for pos in self.order():
+            part = self.own[r].astype(F32)
+            before = jnp.where(lo == pos, total, before)
+            for d in range(1, self.n_lo):
+                part = jnp.where((lo - pos) % self.n_lo == d, self.around[d - 1, r].astype(F32), part)
+            total = part + self.keep(r, pos) * total
+        self.total[r] = total
+        self.before[r] = before
+
+        @pl.when(self.rank == 0)
+        def _():
+            self.leave(r, total)
+            self.result[r] = before.astype(BF)
+
+    def hop(self, r):
+        self.hi_copy(r).wait_recv()
+        entering = self.entering[r].astype(F32)
+        lo = self.place.at["lo"]
+        keep_all, keep_before = jnp.float32(1), jnp.float32(1)
+        for pos in self.order():
+            keep_before = jnp.where(lo == pos, keep_all, keep_before)
+            keep_all = keep_all * self.keep(r, pos)
+        self.leave(r, self.total[r] + keep_all * entering)
+        self.result[r] = (self.before[r] + keep_before * entering).astype(BF)
+
+    def turn(self, step, rows):
+        for q in range(self.n_hi - 1, 0, -1):
+            r = step - 1 - q
+
+            @pl.when((r >= 0) & (r < rows) & (self.rank == q))
+            def _():
+                self.hop(r)
+
+        r = step - 1
+
+        @pl.when((r >= 0) & (r < rows))
+        def _():
+            self.join(r)
+
+        @pl.when(step < rows)
+        def _():
+            self.begin(step)
+
+    def close(self, rows):
+        @pl.when(self.rank < self.n_hi - 1)
+        def _():
+            for r in range(rows):
+                self.hi_copy(r).wait_send()
+
+
+def chain_scratch(rows, height, feats):
+    size = axis_sizes()
+    peers = max(size["lo"] - 1, 1)
+    shape = (rows, height, feats)
+    return [
+        pltpu.VMEM(shape, BF),
+        pltpu.VMEM((peers,) + shape, BF),
+        pltpu.VMEM(shape, F32),
+        pltpu.VMEM(shape, F32),
+        pltpu.VMEM(shape, BF),
+        pltpu.VMEM(shape, BF),
+        pltpu.VMEM(shape, BF),
+        pltpu.SemaphoreType.DMA((2, rows, peers)),
+        pltpu.SemaphoreType.DMA((2, rows)),
+    ]
+
+
+class Small:
+    def __init__(self, rank, width, kv_width, heads, kv_heads, head):
+        def chunks(lanes):
+            return -(-lanes // 128)
+
+        tall = -(-(3 * rank + 2) // 16) * 16
+        flat = -(-2 * rank // 16) * 16
+        sections = [
+            ("down", tall, chunks(width)),
+            ("out", flat, chunks(width)),
+            ("q_up", -(-rank // 16) * 16, chunks(width)),
+            ("kv_up", -(-2 * rank // 16) * 16, chunks(kv_width)),
+            ("qmap", head, (heads + 1) // 2),
+            ("kmap", head, (kv_heads + 1) // 2),
+        ]
+        need = sum(rows * n for _, rows, n in sections)
+        size = axis_sizes()
+        grain = 16 * size["lo"] * size["y"] * size["hi"]
+        self.rows = -(-(need + 64) // (2 * grain)) * grain
+        self.place = {}
+        half, at = 0, 0
+        for name, rows, n in sections:
+            self.place[name] = []
+            for _ in range(n):
+                if at + rows > self.rows:
+                    half, at = half + 1, 0
+                self.place[name].append((half, at, rows))
+                at += rows
+
+    def put(self, ref, name, value):
+        for c, (half, at, rows) in enumerate(self.place[name]):
+            part = value[:, c * 128 : (c + 1) * 128]
+            ref[0, half, at : at + part.shape[0], 0 : part.shape[1]] = part.astype(ref.dtype)
+
+    def put_heads(self, ref, name, maps):
+        for c, (half, at, rows) in enumerate(self.place[name]):
+            pair = [maps[h] for h in range(2 * c, min(2 * c + 2, maps.shape[0]))]
+            pair = jnp.concatenate(pair, axis=1) if len(pair) > 1 else pair[0]
+            ref[0, half, at : at + rows, 0 : pair.shape[1]] = pair.astype(ref.dtype)
+
+    def take(self, ref, name, lanes):
+        parts = [ref[0, half, at : at + rows].astype(F32) for half, at, rows in self.place[name]]
+        return jnp.concatenate(parts, axis=1)[:, :lanes]
+
+
+def widen_kernel(width, high, rank, layout, whole, small, gate, up, down, *outs):
+    for i, out in enumerate((gate, up, down)):
+        out[...] = whole[0, 0, i * high : i * high + width].astype(F32)
+
+    @pl.when(pl.program_id(0) == 0)
+    def _():
+        pre, post, qd, kd, vd, qu, ku, vu, od, ou, qmap, kmap = outs
+        downs = layout.take(small, "down", width)
+        for i, out in enumerate((qd, kd, vd)):
+            out[...] = downs[i * rank : (i + 1) * rank]
+        pre[...] = downs[3 * rank : 3 * rank + 1]
+        post[...] = downs[3 * rank + 1 : 3 * rank + 2]
+        pair = layout.take(small, "out", width)
+        od[...] = pair[:rank]
+        ou[...] = pair[rank : 2 * rank]
+        qu[...] = layout.take(small, "q_up", width)[:rank]
+        pair = layout.take(small, "kv_up", ku.shape[1])
+        ku[...] = pair[:rank]
+        vu[...] = pair[rank : 2 * rank]
+        head = qmap.shape[1]
+        for name, out in (("qmap", qmap), ("kmap", kmap)):
+            for h in range(out.shape[0]):
+                half, at, rows = layout.place[name][h // 2]
+                both = small[0, half, at : at + rows].astype(F32)
+                out[h] = both[:, (h % 2) * head : (h % 2 + 1) * head]
+
+
+def row_sum(value):
+    return dot(jnp.ones((8, value.shape[1]), BF), value.astype(BF), NT)
 
 
 def rms(value):
@@ -154,8 +605,8 @@
 
 def ff_kernel(
     width, normed_h, cot_h, middle, gain, gate_h, up_h, down_h,
-    out, grad_mid, grad_gain, grads,
-    normed, cot, gate_v, up_v, down_v, hid, dgate, dup, sem, act_sem,
+    out, grad_mid, grad_gain, shards,
+    normed, cot, gate_v, up_v, down_v, hid, dgate, dup, sem, act_sem, *refs,
 ):
     step = pl.program_id(0)
     rows = normed_h.shape[0]
@@ -163,6 +614,8 @@
     high = normed.shape[0]
     hidden = gate_h.shape[1]
     tiles = hidden // TILE
+    place = Place()
+    scatter = Scatter(place, 3 * high, refs)
 
     def act_copies():
         made = []
@@ -182,6 +635,7 @@
 
     @pl.when(step == 0)
     def _():
+        place.greet()
         for copy in act_copies():
             copy.start()
         for j in range(tiles):
@@ -211,9 +665,11 @@
             hid[at, lane] = (act * u).astype(BF)
             dup[at, lane] = (dh * act).astype(BF)
             dgate[at, lane] = (dh * u * (sig + act * (1.0 - sig))).astype(BF)
-        grads[0, 0] = dot(normed[...], dgate[at, :], NT)[:width].astype(BF)
-        grads[0, 1] = dot(normed[...], dup[at, :], NT)[:width].astype(BF)
-        grads[0, 2] = dot(cot[...], hid[at, :], NT)[:width].astype(BF)
+        slot = step % 2
+        for i, (left, right) in enumerate(((normed, dgate), (normed, dup), (cot, hid))):
+            grad = dot(left[...], right[at, :], NT).astype(BF)
+            for half in range(2):
+                scatter.mine[slot, half, i * high : (i + 1) * high] = grad[:, half * 128 : (half + 1) * 128]
 
     @pl.when(step >= tiles)
     def _():
@@ -232,8 +688,13 @@
         def _():
             grad_gain[...] = jnp.zeros_like(grad_gain)
 
-        grad_gain[...] += jnp.sum(back * unit, axis=1, keepdims=True)
+        grad_gain[...] += row_sum(back * unit)
         out[0] = (mid + dot(down_v[0:width], hid[:, lane])).astype(BF)
+
+    def into(tile, stream, total):
+        shards[tile, stream] = total.astype(BF)
+
+    scatter.turn(step, tiles, into)
 
 
 def pull_kernel(
@@ -244,11 +705,6 @@
     span = mixed.shape[2]
     head = width // (kv_heads * group)
     low = inner.shape[1]
-
-    @pl.when(pl.program_id(0) == 0)
-    def _():
-        gup[...] = jnp.zeros_like(gup)
-        gdown[...] = jnp.zeros_like(gdown)
 
     branch = grad_mid[0].astype(BF)
     wide = dot(wo[...], branch)
@@ -278,17 +734,12 @@
 
 def back_kernel(
     kv_heads, group, qkv, tails, phik, phiq, state, dcon, dnum, dden, segq, segk, keep, qmap, kmap,
-    dq_out, dkv_out, dtails, gqmap, gkmap, lin_bias, win_bias,
+    dq_out, dkv_out, dtails, gqmap, gkmap, lin_bias, win_bias, between,
 ):
     head = qmap.shape[1]
     width = dq_out.shape[1]
     span = dq_out.shape[2]
     scale = head**-0.5
-
-    @pl.when(pl.program_id(0) == 0)
-    def _():
-        gqmap[...] = jnp.zeros_like(gqmap)
-        gkmap[...] = jnp.zeros_like(gkmap)
 
     far, near = masks(segq[0], segk[0], span)
     lin_bias[...] = jnp.where(far, 1.0, 0.0)
@@ -339,6 +790,7 @@
         dkv_out[0, ks : ks + head] = dk[:, :span]
         dkv_out[0, vs : vs + head] = dv[:, :span]
         dtails[0, ks : ks + head] = jnp.concatenate([dk[:, span:], dv[:, span:]], axis=1).astype(BF)
+        between(k)
 
 
 def final_kernel(
@@ -348,12 +800,6 @@
     width = tok.shape[1]
     span = tok.shape[2]
     low = down.shape[0]
-
-    @pl.when(pl.program_id(0) == 0)
-    def _():
-        ggain[...] = jnp.zeros_like(ggain)
-        gdown[...] = jnp.zeros_like(gdown)
-        gup[...] = jnp.zeros_like(gup)
 
     got = returned[0].astype(F32)
     got = jnp.concatenate([got[:, :WINDOW], got[:, WINDOW:]], axis=0)
@@ -370,10 +816,127 @@
     scale = rms(value)
     unit = value * scale
     grad_unit = back * gain[...]
-    ggain[...] += jnp.sum(back * unit, axis=1, keepdims=True)
+    ggain[...] += row_sum(back * unit)
     grad_tok[0] = grad_mid[0] + scale * (
         grad_unit - unit * jnp.mean(grad_unit * unit, axis=0, keepdims=True)
     )
+
+
+def backward_kernel(
+    rows, kv_heads, group, tiles, shard_rows, layout,
+    kept, grad_mid_p, mixed, den, phiq_p, segq_p, inner_o, wo, odown,
+    qkv, tails, phik, phiq, state, segq, segk, keep, qmap, kmap,
+    tok, grad_mid, gain, normed, inner, wq, wkv, down, gpost, shards,
+    grad_tok, whole, small_out,
+    dnum, dden, dq, dkv, dtails, returned, gup_o, gdown_o, gqmap, gkmap, ggain, gdown, gup, lin_bias, win_bias,
+    tail_sem, small_shard, small, *refs,
+):
+    step = pl.program_id(0)
+    place = Place()
+    chain = Chain(place, True, kept, *refs[:9])
+    refs = refs[9:]
+    n_gather = len(gather_scratch(shard_rows, tiles))
+    gather = Gather(place, shard_rows, shards, whole, refs[:n_gather])
+    refs = refs[n_gather:]
+    n_small = len(gather_scratch(layout.rows, 1))
+    small_gather = Gather(place, layout.rows, small_shard, small, refs[:n_small])
+    small_scatter = Scatter(place, layout.rows, refs[n_small:], 1)
+
+    def row(ref, r):
+        return ref.at[pl.ds(r, 1)]
+
+    def tail_copy(r):
+        return remote(dtails.at[r], returned.at[r], tail_sem.at[0, r], tail_sem.at[1, r], place.along(-1))
+
+    @pl.when(step == 0)
+    def _():
+        place.greet()
+        for ref in (gup_o, gdown_o, gqmap, gkmap, ggain, gdown, gup):
+            ref[...] = jnp.zeros_like(ref)
+
+        @pl.when(jnp.logical_not(place.inside(1)))
+        def _():
+            returned[...] = jnp.zeros_like(returned)
+
+    @pl.when(step < rows)
+    def _():
+        pull_kernel(
+            kv_heads, group, grad_mid_p, mixed, den, phiq_p, segq_p, inner_o, wo, odown,
+            row(dnum, step), row(dden, step), row(chain.own, step), gup_o, gdown_o,
+        )
+
+    @pl.when((step >= rows) & (step < 2 * rows))
+    def _():
+        r = step - rows
+
+        def between(k):
+            if k == kv_heads // 2:
+                gather.turn(2 * r, tiles)
+
+        back_kernel(
+            kv_heads, group, qkv, tails, phik, phiq, state, row(chain.result, r), row(dnum, r), row(dden, r),
+            segq, segk, keep, qmap, kmap,
+            row(dq, r), row(dkv, r), row(dtails, r), gqmap, gkmap, lin_bias, win_bias, between,
+        )
+
+        @pl.when(place.inside(-1))
+        def _():
+            tail_copy(r).start()
+
+    @pl.when(step >= 2 * rows)
+    def _():
+        r = step - 2 * rows
+
+        @pl.when(place.inside(1))
+        def _():
+            tail_copy(r).wait_recv()
+
+        final_kernel(
+            tok, grad_mid, gain, row(dq, r), row(dkv, r), row(returned, r), normed, inner, wq, wkv, down,
+            grad_tok, ggain, gdown, gup,
+        )
+
+    chain.turn(step, rows)
+
+    @pl.when(step >= rows)
+    def _():
+        gather.turn(jnp.where(step < 2 * rows, 2 * (step - rows) + 1, step), tiles)
+
+    @pl.when(step == 3 * rows - 1)
+    def _():
+        chain.close(rows)
+
+        @pl.when(place.inside(-1))
+        def _():
+            for r in range(rows):
+                tail_copy(r).wait_send()
+
+        rank = gdown_o.shape[0]
+        width = gdown_o.shape[1]
+        kv_width = kv_heads * qmap.shape[1]
+        mine = small_scatter.mine
+        mine[...] = jnp.zeros_like(mine)
+        pad = [jnp.zeros((6, width), F32)]
+        layout.put(mine, "down", jnp.concatenate([gdown[...], ggain[0:1], gpost[0:1]] + pad, axis=0))
+        layout.put(mine, "out", jnp.concatenate([gdown_o[...], gup_o[...]], axis=0))
+        layout.put(mine, "q_up", jnp.concatenate([gup[0:rank, :width], jnp.zeros((rank, width), F32)], axis=0))
+        layout.put(
+            mine, "kv_up",
+            jnp.concatenate(
+                [gup[rank : 2 * rank, width : width + kv_width], gup[2 * rank :, width + kv_width :]], axis=0
+            ),
+        )
+        layout.put_heads(mine, "qmap", gqmap)
+        layout.put_heads(mine, "kmap", gkmap)
+
+        def into(stream, total):
+            small_shard[0, stream] = total.astype(BF)
+
+        small_scatter.run(into)
+        small_gather.run()
+        small_out[...] = small[...]
+        for turn in range(3 * rows, tiles + WAYS[0]):
+            gather.turn(jnp.int32(turn), tiles)
 
 
 def row_spec(*shape):
@@ -545,7 +1108,9 @@
     last = lambda s: (jnp.maximum(s - tiles, 0), 0, 0)
     fixed = lambda s: (0, 0)
     anywhere = pl.BlockSpec(memory_space=pl.ANY)
-    layer_out, grad_mid, grad_postgain, grads = pl.pallas_call(
+    streams = stream_plan(3 * high)
+    shard_shape = (tiles, len(streams), streams[0][2][-1][1], 128)
+    layer_out, grad_mid, gpost, shards = pl.pallas_call(
         functools.partial(ff_kernel, width),
         grid=(tiles + rows,),
         in_specs=[anywhere, anywhere, pl.BlockSpec((1, width, span), last), pl.BlockSpec((width, 1), fixed)]
@@ -553,95 +1118,126 @@
         out_specs=(
             pl.BlockSpec((1, width, span), last),
             pl.BlockSpec((1, width, span), last),
-            pl.BlockSpec((width, 1), fixed),
-            pl.BlockSpec((1, 3, width, TILE), lambda s: (jnp.minimum(s, tiles - 1), 0, 0, 0)),
+            pl.BlockSpec((8, width), fixed),
+            pl.BlockSpec(shard_shape, lambda s: (0, 0, 0, 0)),
         ),
         out_shape=(
             shape_of((rows, width, span), BF),
             shape_of((rows, width, span), F32),
-            shape_of((width, 1), F32),
-            shape_of((tiles, 3, width, TILE), BF),
+            shape_of((8, width), F32),
+            shape_of(shard_shape, BF),
         ),
         scratch_shapes=[pltpu.VMEM((high, rows * span), BF)] * 2
         + [pltpu.VMEM((high, hidden), BF)] * 3
         + [pltpu.VMEM((hidden, rows * span), BF)] * 3
-        + [pltpu.SemaphoreType.DMA((tiles, 3)), pltpu.SemaphoreType.DMA((rows, 2))],
+        + [pltpu.SemaphoreType.DMA((tiles, 3)), pltpu.SemaphoreType.DMA((rows, 2))]
+        + scatter_scratch(3 * high, BF),
+        compiler_params=pltpu.CompilerParams(vmem_limit_bytes=VMEM, collective_id=0, has_side_effects=True),
+    )(normed2, cot, middle, gain_two, gate_proj, up_proj, down_proj.T)
+
+    layout = Small(rank, width, kv_width, heads, kv_heads, head)
+    args, specs = [kept], [pl.BlockSpec(memory_space=pltpu.SMEM)]
+    for phase, arrays in enumerate(
+        (
+            (grad_mid, mixed, den, phiq, segq, inner_o),
+            (qkv, tails, phik, phiq, state, segq, segk, keep),
+            (tok, grad_mid, normed, inner),
+        )
+    ):
+        def at(s, *, phase=phase, n=0):
+            return (jnp.clip(s - phase * rows, 0, rows - 1),) + (0,) * n
+
+        for array in arrays:
+            args.append(array)
+            specs.append(
+                pl.BlockSpec((1,) + array.shape[1:], functools.partial(at, n=array.ndim - 1))
+            )
+        fixed_args = ((wo, odown), (query_map, key_map), (wq, wkv, down, gpost))[phase]
+        if phase == 2:
+            args.insert(len(args) - 2, gain_one)
+            specs.insert(len(specs) - 2, whole_spec(*gain_one.shape))
+        for array in fixed_args:
+            args.append(array)
+            specs.append(whole_spec(*array.shape))
+    args.append(shards)
+    specs.append(anywhere)
+    last = lambda s: (jnp.maximum(s - 2 * rows, 0), 0, 0)
+    small_streams = stream_plan(layout.rows)
+    grad_tok, whole, small = pl.pallas_call(
+        functools.partial(backward_kernel, rows, kv_heads, group, tiles, 3 * high, layout),
+        grid=(3 * rows,),
+        in_specs=specs,
+        out_specs=(
+            pl.BlockSpec((1, width, span), last),
+            anywhere,
+            pl.BlockSpec((1, 2, layout.rows, 128), lambda s: (0, 0, 0, 0)),
+        ),
+        out_shape=(
+            shape_of((rows, width, span), F32),
+            shape_of((tiles, 2, 3 * high, 128), BF),
+            shape_of((1, 2, layout.rows, 128), BF),
+        ),
+        scratch_shapes=[
+            pltpu.VMEM((rows, width, span), BF),
+            pltpu.VMEM((rows, slots, span), F32),
+            pltpu.VMEM((rows, width, span), BF),
+            pltpu.VMEM((rows, 2 * kv_width, span), F32),
+            pltpu.VMEM((rows, kv_width, 2 * WINDOW), BF),
+            pltpu.VMEM((rows, kv_width, 2 * WINDOW), BF),
+            pltpu.VMEM((rank, width), F32),
+            pltpu.VMEM((rank, width), F32),
+            pltpu.VMEM((heads, head, head), F32),
+            pltpu.VMEM((kv_heads, head, head), F32),
+            pltpu.VMEM((8, width), F32),
+            pltpu.VMEM((3 * rank, width), F32),
+            pltpu.VMEM((3 * rank, width + 2 * kv_width), F32),
+        ]
+        + biases
+        + [
+            pltpu.SemaphoreType.DMA((2, rows)),
+            pltpu.VMEM((1, len(small_streams), small_streams[0][2][-1][1], 128), BF),
+            pltpu.VMEM((1, 2, layout.rows, 128), BF),
+        ]
+        + chain_scratch(rows, kv_heads * AUG, feats)
+        + gather_scratch(3 * high, tiles)
+        + gather_scratch(layout.rows, 1)
+        + scatter_scratch(layout.rows, BF, 1),
+        compiler_params=pltpu.CompilerParams(vmem_limit_bytes=VMEM, collective_id=1, has_side_effects=True),
+    )(*args)
+
+    column = pl.BlockSpec((width, 128), lambda j: (0, j))
+    flat = [(1, width)] * 2 + [(rank, width)] * 4 + [(rank, kv_width)] * 2 + [(rank, width)] * 2
+    flat += [query_map.shape, key_map.shape]
+    outs = pl.pallas_call(
+        functools.partial(widen_kernel, width, high, rank, layout),
+        grid=(2 * tiles,),
+        in_specs=[
+            pl.BlockSpec((1, 1, 3 * high, 128), lambda j: (j // 2, j % 2, 0, 0)),
+            pl.BlockSpec((1, 2, layout.rows, 128), lambda j: (0, 0, 0, 0)),
+        ],
+        out_specs=(column,) * 3 + tuple(pl.BlockSpec(f, functools.partial(lambda n, j: (0,) * n, len(f))) for f in flat),
+        out_shape=(shape_of((width, hidden), F32),) * 3 + tuple(shape_of(f, F32) for f in flat),
         compiler_params=pltpu.CompilerParams(vmem_limit_bytes=VMEM),
-    )(normed2, cot, middle, gain_two, gate_proj, up_proj, down_proj.T)
-
-    dnum, dden, dstate, gup_o, gdown_o = row_call(
-        functools.partial(pull_kernel, kv_heads, group),
-        rows,
-        [
-            (grad_mid, 1), (mixed, 1), (den, 1), (phiq, 1), (segq, 1), (inner_o, 1), (wo, 0), (odown, 0),
-        ],
-        [
-            ((rows, width, span), BF, 1),
-            ((rows, slots, span), F32, 1),
-            ((rows, kv_heads * AUG, feats), BF, 1),
-            ((rank, width), F32, 0),
-            ((rank, width), F32, 0),
-        ],
-    )
-    dcon = carried_states(dstate, kept, index, count, True)
-    dq, dkv, dtails, gqmap, gkmap = row_call(
-        functools.partial(back_kernel, kv_heads, group),
-        rows,
-        [
-            (qkv, 1), (tails, 1), (phik, 1), (phiq, 1), (state, 1), (dcon, 1), (dnum, 1), (dden, 1),
-            (segq, 1), (segk, 1), (keep, 1), (query_map, 0), (key_map, 0),
-        ],
-        [
-            ((rows, width, span), BF, 1),
-            ((rows, 2 * kv_width, span), F32, 1),
-            ((rows, kv_width, 2 * WINDOW), BF, 1),
-            ((heads, head, head), F32, 0),
-            ((kv_heads, head, head), F32, 0),
-        ],
-        biases,
-    )
-    returned = shifted(dtails, [(i, i - 1) for i in range(1, count)])
-    grad_tok, grad_pregain, gdown, gup = row_call(
-        final_kernel,
-        rows,
-        [
-            (tok, 1), (grad_mid, 1), (gain_one, 0), (dq, 1), (dkv, 1), (returned, 1), (normed, 1), (inner, 1),
-            (wq, 0), (wkv, 0), (down, 0),
-        ],
-        [
-            ((rows, width, span), F32, 1),
-            ((width, 1), F32, 0),
-            ((3 * rank, width), F32, 0),
-            ((3 * rank, width + 2 * kv_width), F32, 0),
-        ],
-    )
-
-    both = ("batch", "seq")
-    small = lax.psum(
-        (grad_pregain, gdown, gup, gdown_o, gup_o, gqmap, gkmap, grad_postgain), both
-    )
-    grad_pregain, gdown, gup, gdown_o, gup_o, gqmap, gkmap, grad_postgain = small
-    grads = lax.psum(grads, both).astype(F32)
-    grads = jnp.moveaxis(grads, 0, 2).reshape(3, width, hidden)
-    ends = (width, width + kv_width, width + 2 * kv_width)
+    )(whole, small)
+    gate, up, down_t, pre, post, qd, kd, vd, qu, ku, vu, od, ou, gq, gk = outs
     return (
         jnp.swapaxes(layer_out, 1, 2),
         jnp.swapaxes(grad_tok, 1, 2),
-        grad_pregain[:, 0],
-        gdown[:rank].T,
-        gup[:rank, : ends[0]],
-        gdown[rank : 2 * rank].T,
-        gup[rank : 2 * rank, ends[0] : ends[1]],
-        gdown[2 * rank :].T,
-        gup[2 * rank :, ends[1] :],
-        gdown_o.T,
-        gup_o,
-        gqmap,
-        gkmap,
-        grad_postgain[:, 0],
-        grads[0],
-        grads[1],
-        grads[2].T,
+        pre[0],
+        qd.T,
+        qu,
+        kd.T,
+        ku,
+        vd.T,
+        vu,
+        od.T,
+        ou,
+        gq,
+        gk,
+        post[0],
+        gate,
+        up,
+        down_t.T,
     )
 
 

time: 899 us -> 413 us (0.46)
  waiting for transfers between devices: 520 us -> 38 us
  Pallas kernels: 205 us -> 314 us
  local copies, waits for them, and re-layouts: 99.6 us -> 13.9 us
  between operations: 14.1 us -> 0.96 us
    psum x3 -> x0, waiting for transfers between devices: 430 us -> none  [the longest x1 257 us: body(): grads = lax.psum(grads, both).astype(F32)]
    pallas_call x0 -> x2, Pallas kernels: none -> 162 us  [the longest x1 141 us: body(): pl.pallas_call(functools.partial(backward_kernel, rows, kv_heads, group,...]
    pallas_call x6 -> x3, Pallas kernels: 116 us -> 44.6 us  [row_call(): pl.pallas_call(kernel, grid=(rows,), in_specs=in_specs, out_specs=out_spe...]
    slice x8 -> x2, local copies, waits for them, and re-layouts: 51.8 us -> 0.19 us  [the longest x2 26 us: body(): grads[2]]
    ppermute x10 -> x5, waiting for transfers between devices: 89.6 us -> 38 us  [shifted(): return lax.ppermute(array, 'seq', route)]
    unnamed x32 -> x17, local copies, waits for them, and re-layouts: 41.9 us -> 9.25 us
    pallas_call x1, Pallas kernels: 89.2 us -> 108 us  [body(): pl.pallas_call(functools.partial(ff_kernel, width), grid=(tiles + rows,),...]
    ppermute x10 -> x5, starting transfers between devices: 28 us -> 22.3 us  [shifted(): return lax.ppermute(array, 'seq', route)]
  transfers between devices with their start and end apart: 13 -> 5, of which waited for: 13 -> 5; matrix products, arithmetic and copies ran while one was open for 10% -> 1% of each run, Pallas kernels for 0% -> 0%
where the time goes in v2:
time: 413 us; the launch traced here: 411 us
  Pallas kernels  314 us (76%)
  waiting for transfers between devices  38 us (9%)
  starting transfers between devices  22.3 us (5%)
  other arithmetic  21.7 us (5%)
  local copies, waits for them, and re-layouts  13.9 us (3%)
    pallas_call x1, Pallas kernels, body(): pl.pallas_call(functools.partial(backward_kernel, rows, kv_heads, group,...  141 us
    pallas_call x1, Pallas kernels, body(): pl.pallas_call(functools.partial(ff_kernel, width), grid=(tiles + rows,),...  108 us
    pallas_call x3, Pallas kernels, row_call(): pl.pallas_call(kernel, grid=(rows,), in_specs=in_specs, out_specs=out_spe...  44.6 us
    ppermute x5, waiting for transfers between devices, shifted(): return lax.ppermute(array, 'seq', route)  38 us
    ppermute x5, starting transfers between devices, shifted(): return lax.ppermute(array, 'seq', route)  22.3 us
    pallas_call x1, Pallas kernels, body(): pl.pallas_call(functools.partial(widen_kernel, width, high, rank, layout)...  20.9 us
    unnamed x17, local copies, waits for them, and re-layouts  9.25 us
  transfers between devices with their start and end apart: 5, of which 5 were waited for; matrix products, arithmetic and copies ran while one was open for 1% of the time, Pallas kernels for 0%

profile of v2, /device:TPU:0, one launch (start us, length us, event | category | flops | bytes accessed | tf_op | source)
XLA Modules:
  0.0 411.2 jit_solution(1881717701484069850)
XLA Ops:
  0.7 0.7 broadcast_in_dim.43
  1.3 0.7 broadcast_multiply_fusion.3
  2.0 0.7 broadcast_multiply_fusion.2
  2.7 0.1 copy.68
  2.9 0.1 copy.67
  3.0 1.0 copy.69.gain
  4.0 0.1 pad.28.clone
  4.1 0.7 broadcast_multiply_fusion
  4.8 1.4 pad_maximum_fusion.down
  6.2 4.8 %maximum_maximum_fusion.1 = (bf16[1024,960]{1,0:T(8,128)(2,1)}, bf16[1024,960]{1,0:T(8,128)(2,1)}) fusion(bf16[8,960]{1,0:T(8,128)(2,1)S(1)} %get-tuple-element.97, bf16[960,960]{1,0:T(8,128)(2,1)} %param.28, bf16[1024]{0:T(1024)(128)(2,1)S(1)} %pad.28.clone, bf16[8,960]{1,0:T(8,128)(2,1)S(1)} %get-tuple-element.98, bf16[960,960]{1,0:T(8,128)(2,1)} %param.25), kind=kLoop, calls=%fused_computation.1 | loop fusion | flops 10813440 | bytes 7651328 | tf_op jit(solution)/shard_map/concatenate | solution.py:1064
  11.1 1.3 maximum_maximum_fusion.2.wkv
  12.5 9.8 %shard_map.341 = (bf16[5,1600,256]{2,1,0:T(8,128)(2,1)}, bf16[5,960,256]{2,1,0:T(8,128)(2,1)}, bf16[5,24,256]{2,1,0:T(8,128)(2,1)}, bf16[5,320,128]{2,1,0:T(8,128)(2,1)}) custom-call(bf16[5,960,256]{2,1,0:T(8,128)(2,1)} %bitcast.48, f32[960,1]{1,0:T(8,128)} %copy.69.gain, bf16[1024,960]{1,0:T(8,128)(2,1)} %get-tuple-element.94.wq, ...), custom_call_target="tpu_custom_call" | custom-call | tf_op jit(solution)/shard_map/pallas_call | solution.py:959
  22.2 4.8 %collective-permute-start = (bf16[5,320,128]{2,1,0:T(8,128)(2,1)}, bf16[5,320,128]{2,1,0:T(8,128)(2,1)S(1)}, u32[]{:S(2)}, u32[]{:S(2)}) collective-permute-start(bf16[5,320,128]{2,1,0:T(8,128)(2,1)} %get-tuple-element.52), channel_id=1, source_target_pairs={{0,1},{1,2},{2,3},{3,4},{4,5},{5,6},{6,7},{8,9},{9,10},{10,11},{11... | collective-permute-start | bytes 1228808 | tf_op jit(solution)/shard_map/ppermute | solution.py:971
  27.2 0.1 pad_dynamic-slice_fusion
  27.3 1.5 reduce-window.6
  28.8 0.1 slice.31
  28.9 0.1 copy.70
  29.0 0.1 copy.71
  29.1 0.1 add_bitcast_fusion.1
  29.2 0.2 slice_reduce_fusion
  29.5 0.7 and_convert_fusion.keep
  30.2 0.1 pad_slice_fusion
  30.3 5.8 %collective-permute-done.tails = bf16[5,320,128]{2,1,0:T(8,128)(2,1)S(1)} collective-permute-done((bf16[5,320,128]{2,1,0:T(8,128)(2,1)}, bf16[5,320,128]{2,1,0:T(8,128)(2,1)S(1)}, u32[]{:S(2)}, u32[]{:S(2)}) %collective-permute-start) | collective-permute-done | bytes 409632 | tf_op jit(solution)/shard_map/ppermute | solution.py:971
  36.1 0.8 copy-done
  36.8 7.5 %shard_map.342 = (bf16[5,5,128,320]{3,2,1,0:T(8,128)(2,1)}, bf16[5,400,128]{2,1,0:T(8,128)(2,1)}) custom-call(bf16[5,1600,256]{2,1,0:T(8,128)(2,1)} %get-tuple-element.51.qkv, bf16[5,320,128]{2,1,0:T(8,128)(2,1)} %copy-done, bf16[5,64,64]{2,1,0:T(8,128)(2,1)} %kmap.3, f32[5,1,320]{2,1,0:T(1,128)} %and_convert_fusion.keep), custom_call_target="tpu_custom_call" | custom-call | tf_op jit(solution)/shard_map/pallas_call | solution.py:959
  44.3 2.4 collective-permute-start.1
  46.7 0.2 bitcast_reduce_fusion
  46.9 0.2 dynamic-slice_reduce_fusion.1
  47.1 10.6 %collective-permute-done.1 = bf16[5,400,128]{2,1,0:T(8,128)(2,1)S(1)} collective-permute-done((bf16[5,400,128]{2,1,0:T(8,128)(2,1)}, bf16[5,400,128]{2,1,0:T(8,128)(2,1)S(1)}, u32[]{:S(2)}, u32[]{:S(2)}) %collective-permute-start.1) | collective-permute-done | bytes 512032 | tf_op jit(solution)/shard_map/ppermute | solution.py:971
  57.7 1.2 maximum_convert_fusion
  58.9 1.1 add_convert_fusion.3
  59.9 5.5 %collective-permute-start.2 = (bf16[5,400,128]{2,1,0:T(8,128)(2,1)}, bf16[5,400,128]{2,1,0:T(8,128)(2,1)}, u32[]{:S(2)}, u32[]{:S(2)}) collective-permute-start(bf16[5,400,128]{2,1,0:T(8,128)(2,1)} %get-tuple-element.87), channel_id=1, source_target_pairs={{0,2},{1,3},{2,4},{3,5},{4,6},{5,7},{8,10},{9,11},{10,12},{11,13},... | collective-permute-start | bytes 1536008 | tf_op jit(solution)/shard_map/ppermute | solution.py:971
  65.5 8.6 %collective-permute-done.2 = bf16[5,400,128]{2,1,0:T(8,128)(2,1)} collective-permute-done((bf16[5,400,128]{2,1,0:T(8,128)(2,1)}, bf16[5,400,128]{2,1,0:T(8,128)(2,1)}, u32[]{:S(2)}, u32[]{:S(2)}) %collective-permute-start.2) | collective-permute-done | bytes 512032 | tf_op jit(solution)/shard_map/ppermute | solution.py:971
  74.1 2.0 add_convert_fusion.2
  76.1 5.2 %collective-permute-start.3 = (bf16[5,400,128]{2,1,0:T(8,128)(2,1)}, bf16[5,400,128]{2,1,0:T(8,128)(2,1)}, u32[]{:S(2)}, u32[]{:S(2)}) collective-permute-start(bf16[5,400,128]{2,1,0:T(8,128)(2,1)} %add_convert_fusion.2), channel_id=1, source_target_pairs={{0,2},{1,3},{2,4},{3,5},{4,6},{5,7},{8,10},{9,11},{10,12},{11,13},... | collective-permute-start | bytes 1536008 | tf_op jit(solution)/shard_map/ppermute | solution.py:971
  81.3 7.7 %collective-permute-done.3 = bf16[5,400,128]{2,1,0:T(8,128)(2,1)} collective-permute-done((bf16[5,400,128]{2,1,0:T(8,128)(2,1)}, bf16[5,400,128]{2,1,0:T(8,128)(2,1)}, u32[]{:S(2)}, u32[]{:S(2)}) %collective-permute-start.3) | collective-permute-done | bytes 512032 | tf_op jit(solution)/shard_map/ppermute | solution.py:971
  89.0 2.2 add_convert_fusion.1
  91.2 4.4 %collective-permute-start.4 = (bf16[5,400,128]{2,1,0:T(8,128)(2,1)}, bf16[5,400,128]{2,1,0:T(8,128)(2,1)S(1)}, u32[]{:S(2)}, u32[]{:S(2)}) collective-permute-start(bf16[5,400,128]{2,1,0:T(8,128)(2,1)} %add_convert_fusion.1), channel_id=1, source_target_pairs={{0,2},{1,3},{2,4},{3,5},{4,6},{5,7},{8,10},{9,11},{10,12},{11,13},... | collective-permute-start | bytes 1536008 | tf_op jit(solution)/shard_map/ppermute | solution.py:971
  95.6 1.0 copy.75.gain
  96.7 1.2 copy.74.segk
  97.9 5.3 %collective-permute-done.4 = bf16[5,400,128]{2,1,0:T(8,128)(2,1)S(1)} collective-permute-done((bf16[5,400,128]{2,1,0:T(8,128)(2,1)}, bf16[5,400,128]{2,1,0:T(8,128)(2,1)S(1)}, u32[]{:S(2)}, u32[]{:S(2)}) %collective-permute-start.4) | collective-permute-done | bytes 512032 | tf_op jit(solution)/shard_map/ppermute | solution.py:971
  103.2 2.4 add_convert_fusion.state
  105.5 27.4 %shard_map.343 = (bf16[5,960,256]{2,1,0:T(8,128)(2,1)}, f32[5,16,256]{2,1,0:T(8,128)}, bf16[5,15,128,256]{3,2,1,0:T(8,128)(2,1)}, f32[5,960,256]{2,1,0:T(8,128)}...) custom-call(bf16[5,1600,256]{2,1,0:T(8,128)(2,1)} %get-tuple-element.51.qkv, bf16[5,320,128]{2,1,0:T(8,128)(2,1)} %copy-done, ...), custom_call_target="tpu_custom_call" | custom-call | tf_op jit(solution)/shard_map/pallas_call | solution.py:959
  132.9 107.7 %shard_map.344 = (bf16[5,960,256]{2,1,0:T(8,128)(2,1)}, f32[5,960,256]{2,1,0:T(8,128)}, f32[8,960]{1,0:T(8,128)}, bf16[10,2,96,128]{3,2,1,0:T(8,128)(2,1)}) custom-call(bf16[5,960,256]{2,1,0:T(8,128)(2,1)} %get-tuple-element.55.normed_h, bf16[5,960,256]{2,1,0:T(8,128)(2,1)} %bitcast.53, f32[5,960,256]{2,1,0:T(8,128)} %get-tuple-element.56.middle, ...), custom_call_target="tpu_custom_call" | custom-call | tf_op jit(solution)/shard_map/pallas_call | solution.py:1113
  240.6 141.2 %shard_map.345 = (f32[5,960,256]{2,1,0:T(8,128)}, bf16[10,2,3072,128]{3,2,1,0:T(8,128)(2,1)}, bf16[1,2,768,128]{3,2,1,0:T(8,128)(2,1)}) custom-call(f32[5,8]{1,0:T(8,128)} %copy-done.5, f32[5,960,256]{2,1,0:T(8,128)} %get-tuple-element.58.grad_mid_p.grad_mid, bf16[5,960,256]{2,1,0:T(8,128)(2,1)} %get-tuple-element.59.mixed, ...), custom_call_target="tpu_custom_call" | custom-call | tf_op jit(solution)/shard_map/pallas_call | solution.py:1166
  381.8 20.9 %shard_map.346 = (f32[960,2560]{1,0:T(8,128)}, f32[960,2560]{1,0:T(8,128)}, f32[960,2560]{1,0:T(8,128)}, f32[1,960]{1,0:T(1,128)}, f32[1,960]{1,0:T(1,128)}, /*i...) custom-call(bf16[10,2,3072,128]{3,2,1,0:T(8,128)(2,1)} %get-tuple-el, ...), custom_call_target="tpu_custom_call" | custom-call | tf_op jit(solution)/shard_map/pallas_call | solution.py:1211
  402.7 3.3 copy.88
  406.0 5.2 %copy.89 = f32[5,256,960]{1,2,0:T(8,128)} copy(f32[5,256,960]{1,2,0:T(8,128)} %bitcast.52) | data formatting | bytes 9830400
  (32 shorter events, 0.3 us)
Async XLA Ops:
  6.2 4.9 %copy-start.1 = (bf16[960,320]{0,1:T(8,128)(2,1)S(1)}, bf16[960,320]{0,1:T(8,128)(2,1)}, u32[]{:S(2)}) copy-start(bf16[960,320]{0,1:T(8,128)(2,1)} %param.27) | copy-start | bytes 1843204
  6.2 4.9 %copy-start.2 = (bf16[960,320]{0,1:T(8,128)(2,1)S(1)}, bf16[960,320]{0,1:T(8,128)(2,1)}, u32[]{:S(2)}) copy-start(bf16[960,320]{0,1:T(8,128)(2,1)} %param.26) | copy-start | bytes 1843204
  12.5 14.7 %copy-start.3 = (s32[5,2048]{1,0:T(8,128)S(1)}, s32[5,2048]{1,0:T(8,128)}, u32[]{:S(2)}) copy-start(s32[5,2048]{1,0:T(8,128)} %param.23) | copy-start | bytes 122884
  22.2 13.9 %collective-permute-start = (bf16[5,320,128]{2,1,0:T(8,128)(2,1)}, bf16[5,320,128]{2,1,0:T(8,128)(2,1)S(1)}, u32[]{:S(2)}, u32[]{:S(2)}) collective-permute-start(bf16[5,320,128]{2,1,0:T(8,128)(2,1)} %get-tuple-element.52), channel_id=1, source_target_pairs={{0,1},{1,2},{2,3},{3,4},{4,5},{5,6},{6,7},{8,9},{9,10},{10,11},{11... | collective-permute-start | bytes 1228808 | tf_op jit(solution)/shard_map/ppermute | solution.py:971
  29.5 29.4 %copy-start.4 = (s32[5,1,256]{2,1,0:T(1,128)}, s32[5,1,256]{2,1,0:T(1,128)S(1)}, u32[]{:S(2)}) copy-start(s32[5,1,256]{2,1,0:T(1,128)S(1)} %copy.72.segq.segq_p) | copy-start | bytes 15364
  36.1 0.8 copy-start
  44.3 13.4 %collective-permute-start.1 = (bf16[5,400,128]{2,1,0:T(8,128)(2,1)}, bf16[5,400,128]{2,1,0:T(8,128)(2,1)S(1)}, u32[]{:S(2)}, u32[]{:S(2)}) collective-permute-start(bf16[5,400,128]{2,1,0:T(8,128)(2,1)} %get-tuple-element.54), channel_id=1, source_target_pairs={{0,1},{1,0},{2,3},{3,2},{4,5},{5,4},{6,7},{7,6},{8,9},{9,8},{10,11... | collective-permute-start | bytes 1536008 | tf_op jit(solution)/shard_map/ppermute | solution.py:971
  46.9 13.1 %copy-start.5 = (f32[5,8]{1,0:T(8,128)}, f32[5,8]{1,0:T(8,128)S(1)}, u32[]{:S(2)}) copy-start(f32[5,8]{1,0:T(8,128)S(1)} %compare_convert_fusion.kept) | copy-start | bytes 484
  59.9 35.7 %copy-start.6 = (bf16[960]{0:T(1024)(128)(2,1)S(1)}, bf16[960]{0:T(1024)(128)(2,1)}, u32[]{:S(2)}) copy-start(bf16[960]{0:T(1024)(128)(2,1)} %param.39) | copy-start | bytes 5764
  59.9 14.1 %collective-permute-start.2 = (bf16[5,400,128]{2,1,0:T(8,128)(2,1)}, bf16[5,400,128]{2,1,0:T(8,128)(2,1)}, u32[]{:S(2)}, u32[]{:S(2)}) collective-permute-start(bf16[5,400,128]{2,1,0:T(8,128)(2,1)} %get-tuple-element.87), channel_id=1, source_target_pairs={{0,2},{1,3},{2,4},{3,5},{4,6},{5,7},{8,10},{9,11},{10,12},{11,13},... | collective-permute-start | bytes 1536008 | tf_op jit(solution)/shard_map/ppermute | solution.py:971
  76.1 12.9 %collective-permute-start.3 = (bf16[5,400,128]{2,1,0:T(8,128)(2,1)}, bf16[5,400,128]{2,1,0:T(8,128)(2,1)}, u32[]{:S(2)}, u32[]{:S(2)}) collective-permute-start(bf16[5,400,128]{2,1,0:T(8,128)(2,1)} %add_convert_fusion.2), channel_id=1, source_target_pairs={{0,2},{1,3},{2,4},{3,5},{4,6},{5,7},{8,10},{9,11},{10,12},{11,13},... | collective-permute-start | bytes 1536008 | tf_op jit(solution)/shard_map/ppermute | solution.py:971
  91.2 11.9 %collective-permute-start.4 = (bf16[5,400,128]{2,1,0:T(8,128)(2,1)}, bf16[5,400,128]{2,1,0:T(8,128)(2,1)S(1)}, u32[]{:S(2)}, u32[]{:S(2)}) collective-permute-start(bf16[5,400,128]{2,1,0:T(8,128)(2,1)} %add_convert_fusion.1), channel_id=1, source_target_pairs={{0,2},{1,3},{2,4},{3,5},{4,6},{5,7},{8,10},{9,11},{10,12},{11,13},... | collective-permute-start | bytes 1536008 | tf_op jit(solution)/shard_map/ppermute | solution.py:971

commit v3 on v2

--- a/solution.py
+++ b/solution.py
@@ -291,8 +291,8 @@
 
 
 class Chain:
-    def __init__(self, place, reverse, kept, own, around, total, before, leaving, entering, result, lo_sem, hi_sem):
-        self.place, self.reverse, self.kept = place, reverse, kept
+    def __init__(self, place, reverse, lag, kept, own, around, total, before, leaving, entering, result, lo_sem, hi_sem):
+        self.place, self.reverse, self.lag, self.kept = place, reverse, lag, kept
         self.own, self.around, self.total, self.before = own, around, total, before
         self.leaving, self.entering, self.result = leaving, entering, result
         self.lo_sem, self.hi_sem = lo_sem, hi_sem
@@ -316,7 +316,9 @@
         )
 
     def keep(self, r, pos):
-        return self.kept[r, self.place.at["hi"] * self.n_lo + pos]
+        flags = self.kept[pl.ds(r, 1), :]
+        here = lax.broadcasted_iota(jnp.int32, flags.shape, 1) == self.place.at["hi"] * self.n_lo + pos
+        return jnp.sum(jnp.where(here, flags, 0.0), axis=1, keepdims=True)
 
     def order(self):
         return list(range(self.n_lo))[:: -1 if self.reverse else 1]
@@ -355,30 +357,32 @@
         self.hi_copy(r).wait_recv()
         entering = self.entering[r].astype(F32)
         lo = self.place.at["lo"]
-        keep_all, keep_before = jnp.float32(1), jnp.float32(1)
+        keep_all = keep_before = jnp.ones((1, 1), F32)
         for pos in self.order():
             keep_before = jnp.where(lo == pos, keep_all, keep_before)
             keep_all = keep_all * self.keep(r, pos)
         self.leave(r, self.total[r] + keep_all * entering)
         self.result[r] = (self.before[r] + keep_before * entering).astype(BF)
 
-    def turn(self, step, rows):
+    def turn(self, step, rows, starts=True):
         for q in range(self.n_hi - 1, 0, -1):
-            r = step - 1 - q
+            r = step - self.lag * (1 + q)
 
             @pl.when((r >= 0) & (r < rows) & (self.rank == q))
             def _():
                 self.hop(r)
 
-        r = step - 1
+        r = step - self.lag
 
         @pl.when((r >= 0) & (r < rows))
         def _():
             self.join(r)
 
-        @pl.when(step < rows)
-        def _():
-            self.begin(step)
+        if starts:
+
+            @pl.when(step < rows)
+            def _():
+                self.begin(step)
 
     def close(self, rows):
         @pl.when(self.rank < self.n_hi - 1)
@@ -449,9 +453,12 @@
         return jnp.concatenate(parts, axis=1)[:, :lanes]
 
 
-def widen_kernel(width, high, rank, layout, whole, small, gate, up, down, *outs):
+def widen_kernel(width, high, rank, layout, whole, small, out_in, tok_in, out_out, tok_out, gate, up, down, *outs):
+    out_out[...] = out_in[...]
+    tok_out[...] = tok_in[...]
     for i, out in enumerate((gate, up, down)):
-        out[...] = whole[0, 0, i * high : i * high + width].astype(F32)
+        for half in range(2):
+            out[:, half * 128 : (half + 1) * 128] = whole[0, half, i * high : i * high + width].astype(F32)
 
     @pl.when(pl.program_id(0) == 0)
     def _():
@@ -503,6 +510,72 @@
     return (gu - gd).astype(BF)
 
 
+def frame(place, span, doc, seg, kept):
+    rows, length = doc.shape
+    index = place.seq
+    high = seg.shape[0]
+    more = jnp.zeros((high - rows, span), F32)
+    own = doc[:, pl.ds(pl.multiple_of(index * span, span), span)].astype(F32)
+    prev = doc[:, pl.ds(pl.multiple_of(jnp.maximum(index - 1, 0) * span, span), span)].astype(F32)
+    lane = lax.broadcasted_iota(jnp.int32, (rows, span), 1)
+    prev = jnp.where((lane >= span - WINDOW) & (index > 0), prev, 0.0)
+    upper = lax.broadcasted_iota(jnp.int32, (span, span), 0) <= lax.broadcasted_iota(jnp.int32, (span, span), 1)
+    upper = jnp.where(upper, 1.0, 0.0).astype(BF)
+    before = jnp.concatenate([prev, more], axis=0)
+    tail = dot(before.astype(BF), upper)
+    mine = dot(jnp.concatenate([own, more], axis=0).astype(BF), upper) + jnp.sum(before, axis=1, keepdims=True)
+    seg[:, :span] = mine
+    seg[:, span:] = tail[:, span - WINDOW :]
+    total = jnp.zeros(kept.shape, F32)
+    for b in range(length // span):
+        at = lax.broadcasted_iota(jnp.int32, (span, 128), 0)
+        block = lax.broadcasted_iota(jnp.int32, (span, 128), 1)
+        here = jnp.where(at < span - WINDOW, b, b + 1) == block
+        marks = jnp.concatenate([doc[:, b * span : (b + 1) * span].astype(F32), more], axis=0)
+        total = total + dot(marks.astype(BF), jnp.where(here, 1.0, 0.0).astype(BF))
+    kept[...] = jnp.where(total == 0, 1.0, 0.0)
+
+
+def frame_row(seg, r, span):
+    keys = seg[pl.ds(r, 1), :]
+    query = keys[:, :span]
+    column = jnp.broadcast_to(keys, (8, keys.shape[1])).T[:, :1]
+    lane = lax.broadcasted_iota(jnp.int32, keys.shape, 1)
+    last = jnp.sum(jnp.where(lane == span - WINDOW - 1, keys, 0.0), axis=1, keepdims=True)
+    keep = (keys == last) & ((lane < span - WINDOW) | (lane >= span))
+    return query, column, jnp.where(keep, 1.0, 0.0)
+
+
+def assemble(width, bases, gains, wq, wkv, wo, down, columns):
+    qb, kb, vb, ob, qu, ku, vu, ou, qd, kd, vd = bases
+    rank = qu.shape[0]
+    high = wq.shape[0]
+    extra = high - width
+    for out, base, up in ((wq, qb, qu), (wo, ob, ou)):
+        out[0:width] = base[...]
+        rows = jnp.concatenate([2.0 * up[...].astype(F32), jnp.zeros((extra - rank, width), F32)], axis=0)
+        out[width:] = rows.astype(BF)
+    kv = kb.shape[0]
+    wkv[0:kv, 0:width] = kb[...]
+    wkv[kv:, 0:width] = vb[...]
+    none = jnp.zeros((rank, kv), F32)
+    pair = jnp.concatenate(
+        [
+            jnp.concatenate([none, none], axis=1),
+            jnp.concatenate([2.0 * ku[...].astype(F32), none], axis=1),
+            jnp.concatenate([none, 2.0 * vu[...].astype(F32)], axis=1),
+            jnp.zeros((extra - 3 * rank, 2 * kv), F32),
+        ],
+        axis=0,
+    )
+    wkv[:, width:] = pair.T.astype(BF)
+    down[...] = jnp.concatenate([qd[...].astype(F32), kd[...].astype(F32), vd[...].astype(F32)], axis=0).astype(BF)
+    wide = gains[...]
+    wide = jnp.concatenate([wide, jnp.zeros((8 - wide.shape[0], width), F32)], axis=0).T
+    columns[0] = wide[:, 0:1]
+    columns[1] = wide[:, 1:2]
+
+
 def qkv_kernel(tok, gain, wq, wkv, down, qkv, normed, inner, tails, ext):
     width = tok.shape[1]
     kv = wkv.shape[0]
@@ -531,7 +604,7 @@
 def key_kernel(kv_heads, qkv, tails, kmap, keep, phi, con):
     head = kmap.shape[1]
     first = qkv.shape[1] - 2 * kv_heads * head
-    keeping = keep[0].astype(BF)
+    keeping = keep.astype(BF)
     for k in range(kv_heads):
         at = first + k * head
         key = jnp.concatenate([qkv[0, at : at + head], tails[0, k * head : (k + 1) * head, :WINDOW]], axis=1)
@@ -552,19 +625,16 @@
     return same & far, same & (pos <= query) & jnp.logical_not(far)
 
 
-def attend_kernel(
-    kv_heads, group, qkv, tails, phik, state, segq, segk, qmap, tok, wo, down, gain,
-    mixed, den, phiq, middle, normed, inner, ext, lin_bias, win_bias,
+def local_kernel(
+    kv_heads, group, qkv, tails, phik, frames, qmap, phiq, numer, den, lin_bias, win_bias, between,
 ):
     head = qmap.shape[1]
-    width = tok.shape[1]
-    span = tok.shape[2]
-    far, near = masks(segq[0], segk[0], span)
+    span = qkv.shape[2]
+    width = kv_heads * group * head
+    segq, segk, _ = frames
+    far, near = masks(segq, segk, span)
     lin_bias[...] = jnp.where(far, 1.0, 0.0)
     win_bias[...] = jnp.where(near, 0.0, -1e30)
-    shown = jnp.where(segq[0] == 0, 1.0, 0.0)
-    shown3 = jnp.concatenate([shown] * group, axis=1)
-    den[0] = jnp.zeros_like(den[0])
     for k in range(kv_heads):
         at = width + k * head
         key = jnp.concatenate([qkv[0, at : at + head], tails[0, k * head : (k + 1) * head, :WINDOW]], axis=1)
@@ -584,14 +654,31 @@
         lb = jnp.concatenate([lin_bias[...]] * group, axis=1)
         wb = jnp.concatenate([win_bias[...]] * group, axis=1)
         weights = lin * lb + jnp.exp(score + wb)
-        carried = dot(state[0, k * AUG : (k + 1) * AUG], feat) * shown3
-        total = jnp.sum(weights, axis=0, keepdims=True) + carried[head : head + 1]
-        numer = dot(val, weights.astype(BF)) + carried[:head]
-        out = (numer / total).astype(BF)
+        total = jnp.sum(weights, axis=0, keepdims=True)
+        out = dot(val, weights.astype(BF))
         for g in range(group):
             h = k * group + g
-            ext[h * head : (h + 1) * head] = out[:, g * span : (g + 1) * span]
+            numer[0, h * head : (h + 1) * head] = out[:, g * span : (g + 1) * span]
             den[0, h : h + 1] = total[:, g * span : (g + 1) * span]
+        between(k)
+
+
+def join_kernel(
+    kv_heads, group, phiq, numer, den_local, state, frames, tok, wo, down, gain,
+    mixed, den, middle, normed, inner, ext,
+):
+    width = tok.shape[1]
+    span = tok.shape[2]
+    head = width // (kv_heads * group)
+    shown = jnp.where(frames[0] == 0, 1.0, 0.0)
+    den[0] = jnp.zeros_like(den[0])
+    for h in range(kv_heads * group):
+        k = h // group
+        carried = dot(state[0, k * AUG : (k + 1) * AUG], phiq[0, h]) * shown
+        total = den_local[0, h : h + 1] + carried[head : head + 1]
+        at = pl.ds(h * head, head)
+        ext[at] = ((numer[0, at] + carried[:head]) * (1.0 / total)).astype(BF)
+        den[0, h : h + 1] = total
     got = ext[0:width]
     mixed[0] = got
     low = dot(down[...], got).astype(BF)
@@ -601,6 +688,93 @@
     mid = tok[0].astype(F32) + dot(wo[...], ext[...], TN)
     middle[0] = mid
     normed[0] = (mid * rms(mid) * gain[...]).astype(BF)
+
+
+def forward_kernel(
+    rows, kv_heads, group,
+    tok, tok_again, doc, gains, qb, kb, vb, ob, qu, ku, vu, ou, qd, kd, vd, od, qmap, kmap,
+    qkv_out, normed, inner, tails_out, phik_out, phiq_out, state_out, mixed, den, middle, normed2, inner_o,
+    wq, wkv, wo, down, columns,
+    seg, kept, ext, qkv, sent, tails, phik, phiq, numer, den_local, lin_bias, win_bias, tail_sem, *refs,
+):
+    step = pl.program_id(0)
+    place = Place()
+    chain = Chain(place, False, 2, kept, *refs)
+    width, span = tok.shape[1], tok.shape[2]
+
+    def row(ref, r):
+        return ref.at[pl.ds(r, 1)]
+
+    def tail_copy(r):
+        return remote(sent.at[r], tails.at[r], tail_sem.at[0, r], tail_sem.at[1, r], place.along(1))
+
+    @pl.when(step == 0)
+    def _():
+        place.greet()
+
+        @pl.when(jnp.logical_not(place.inside(-1)))
+        def _():
+            tails[...] = jnp.zeros_like(tails)
+
+        frame(place, span, doc, seg, kept)
+        assemble(width, (qb, kb, vb, ob, qu, ku, vu, ou, qd, kd, vd), gains, wq, wkv, wo, down, columns)
+
+    @pl.when(step < rows)
+    def _():
+        qkv_kernel(tok, columns.at[0], wq, wkv, down, row(qkv, step), normed, inner, row(sent, step), ext)
+        qkv_out[...] = qkv[pl.ds(step, 1)]
+
+        @pl.when(place.inside(1))
+        def _():
+            tail_copy(step).start()
+
+    @pl.when((step >= rows) & (step < 2 * rows))
+    def _():
+        r = step - rows
+
+        @pl.when(place.inside(-1))
+        def _():
+            tail_copy(r).wait_recv()
+
+        tails_out[...] = tails[pl.ds(r, 1)]
+        keep = frame_row(seg, r, span)[2]
+        key_kernel(kv_heads, row(qkv, r), row(tails, r), kmap, keep, row(phik, r), row(chain.own, r))
+        phik_out[...] = phik[pl.ds(r, 1)]
+        chain.turn(r, rows)
+
+    @pl.when((step >= 2 * rows) & (step < 3 * rows))
+    def _():
+        r = step - 2 * rows
+
+        def between(k):
+            if k == kv_heads // 2 - 1:
+                chain.turn(rows + 2 * r, rows, False)
+
+        local_kernel(
+            kv_heads, group, row(qkv, r), row(tails, r), row(phik, r), frame_row(seg, r, span), qmap,
+            row(phiq, r), row(numer, r), row(den_local, r), lin_bias, win_bias, between,
+        )
+        phiq_out[...] = phiq[pl.ds(r, 1)]
+        chain.turn(rows + 2 * r + 1, rows, False)
+
+    @pl.when(step >= 3 * rows)
+    def _():
+        r = step - 3 * rows
+        state_out[...] = chain.result[pl.ds(r, 1)]
+        join_kernel(
+            kv_heads, group, row(phiq, r), row(numer, r), row(den_local, r), row(chain.result, r),
+            frame_row(seg, r, span), tok_again, wo, od, columns.at[1],
+            mixed, den, middle, normed2, inner_o, ext,
+        )
+
+    @pl.when(step == 4 * rows - 1)
+    def _():
+        chain.close(rows)
+
+        @pl.when(place.inside(1))
+        def _():
+            for r in range(rows):
+                tail_copy(r).wait_send()
 
 
 def ff_kernel(
@@ -679,7 +853,7 @@
         mid = middle[0]
         scale = rms(mid)
         unit = mid * scale
-        grad_unit = back * gain[...]
+        grad_unit = back * gain[0]
         grad_mid[0] = cot[0:width, lane].astype(F32) + scale * (
             grad_unit - unit * jnp.mean(grad_unit * unit, axis=0, keepdims=True)
         )
@@ -698,7 +872,7 @@
 
 
 def pull_kernel(
-    kv_heads, group, grad_mid, mixed, den, phiq, segq, inner, wo, down,
+    kv_heads, group, grad_mid, mixed, den, phiq, frames, inner, wo, down,
     dnum, dden, dstate, gup, gdown,
 ):
     width = mixed.shape[1]
@@ -712,7 +886,7 @@
     grad = (wide[:width] + dot(down[...], grad_inner, TN)).astype(BF).astype(F32)
     gup[...] += 2.0 * dot(inner[0], branch, NT)
     gdown[...] += dot(grad_inner, mixed[0], NT)
-    shown = jnp.where(segq[0] == 0, 1.0, 0.0)
+    shown = jnp.where(frames[0] == 0, 1.0, 0.0)
     dden[0] = jnp.zeros_like(dden[0])
     pad = jnp.zeros((AUG - head - 1, span), F32)
     for k in range(kv_heads):
@@ -733,7 +907,7 @@
 
 
 def back_kernel(
-    kv_heads, group, qkv, tails, phik, phiq, state, dcon, dnum, dden, segq, segk, keep, qmap, kmap,
+    kv_heads, group, qkv, tails, phik, phiq, state, dcon, dnum, dden, frames, qmap, kmap,
     dq_out, dkv_out, dtails, gqmap, gkmap, lin_bias, win_bias, between,
 ):
     head = qmap.shape[1]
@@ -741,12 +915,12 @@
     span = dq_out.shape[2]
     scale = head**-0.5
 
-    far, near = masks(segq[0], segk[0], span)
+    far, near = masks(frames[0], frames[1], span)
     lin_bias[...] = jnp.where(far, 1.0, 0.0)
     win_bias[...] = jnp.where(near, 0.0, -1e30)
-    shown = jnp.where(segq[0] == 0, 1.0, 0.0)
+    shown = jnp.where(frames[0] == 0, 1.0, 0.0)
     shown3 = jnp.concatenate([shown] * group, axis=1)
-    keeping = keep[0]
+    keeping = frames[2]
     pad = jnp.zeros((AUG - head - 1, group * span), F32)
     for k in range(kv_heads):
         at = width + k * head
@@ -824,16 +998,16 @@
 
 def backward_kernel(
     rows, kv_heads, group, tiles, shard_rows, layout,
-    kept, grad_mid_p, mixed, den, phiq_p, segq_p, inner_o, wo, odown,
-    qkv, tails, phik, phiq, state, segq, segk, keep, qmap, kmap,
-    tok, grad_mid, gain, normed, inner, wq, wkv, down, gpost, shards,
+    doc, grad_mid_p, mixed, den, phiq_p, inner_o, wo, odown,
+    qkv, tails, phik, phiq, state, qmap, kmap,
+    tok, grad_mid, normed, inner, gain, wq, wkv, down, gpost, shards,
     grad_tok, whole, small_out,
     dnum, dden, dq, dkv, dtails, returned, gup_o, gdown_o, gqmap, gkmap, ggain, gdown, gup, lin_bias, win_bias,
-    tail_sem, small_shard, small, *refs,
+    seg, kept, tail_sem, small_shard, small, *refs,
 ):
     step = pl.program_id(0)
     place = Place()
-    chain = Chain(place, True, kept, *refs[:9])
+    chain = Chain(place, True, 1, kept, *refs[:9])
     refs = refs[9:]
     n_gather = len(gather_scratch(shard_rows, tiles))
     gather = Gather(place, shard_rows, shards, whole, refs[:n_gather])
@@ -851,6 +1025,7 @@
     @pl.when(step == 0)
     def _():
         place.greet()
+        frame(place, tok.shape[2], doc, seg, kept)
         for ref in (gup_o, gdown_o, gqmap, gkmap, ggain, gdown, gup):
             ref[...] = jnp.zeros_like(ref)
 
@@ -861,7 +1036,7 @@
     @pl.when(step < rows)
     def _():
         pull_kernel(
-            kv_heads, group, grad_mid_p, mixed, den, phiq_p, segq_p, inner_o, wo, odown,
+            kv_heads, group, grad_mid_p, mixed, den, phiq_p, frame_row(seg, step, tok.shape[2]), inner_o, wo, odown,
             row(dnum, step), row(dden, step), row(chain.own, step), gup_o, gdown_o,
         )
 
@@ -875,7 +1050,7 @@
 
         back_kernel(
             kv_heads, group, qkv, tails, phik, phiq, state, row(chain.result, r), row(dnum, r), row(dden, r),
-            segq, segk, keep, qmap, kmap,
+            frame_row(seg, r, tok.shape[2]), qmap, kmap,
             row(dq, r), row(dkv, r), row(dtails, r), gqmap, gkmap, lin_bias, win_bias, between,
         )
 
@@ -892,7 +1067,7 @@
             tail_copy(r).wait_recv()
 
         final_kernel(
-            tok, grad_mid, gain, row(dq, r), row(dkv, r), row(returned, r), normed, inner, wq, wkv, down,
+            tok, grad_mid, gain.at[0], row(dq, r), row(dkv, r), row(returned, r), normed, inner, wq, wkv, down,
             grad_tok, ggain, gdown, gup,
         )
 
@@ -953,81 +1128,6 @@
     return jax.ShapeDtypeStruct(shape, kind)
 
 
-def row_call(kernel, rows, args, outs, scratch=()):
-    in_specs = [row_spec(*a.shape[1:]) if by_row else whole_spec(*a.shape) for a, by_row in args]
-    out_specs = tuple(row_spec(*s[1:]) if by_row else pl.BlockSpec(s, functools.partial(lambda n, r: (0,) * n, len(s))) for s, _, by_row in outs)
-    return pl.pallas_call(
-        kernel,
-        grid=(rows,),
-        in_specs=in_specs,
-        out_specs=out_specs,
-        out_shape=tuple(shape_of(s, kind) for s, kind, _ in outs),
-        scratch_shapes=list(scratch),
-        compiler_params=pltpu.CompilerParams(vmem_limit_bytes=VMEM),
-    )(*[a for a, _ in args])
-
-
-def shifted(array, route):
-    return lax.ppermute(array, "seq", route)
-
-
-def fold(parts, keeps):
-    total = None
-    for part, keep in zip(parts, keeps):
-        total = part if total is None else part + keep[:, None, None] * total
-    return total
-
-
-def carried_states(own, kept, index, count, reverse):
-    hi, lo, n_hi, n_lo = split_seq(index, count)
-    step = -1 if reverse else 1
-    ranks = range(count)
-
-    def keep_of(at):
-        return lax.dynamic_slice_in_dim(kept, at, 1, 1)[:, 0]
-
-    around = [own]
-    for d in range(1, n_lo):
-        route = [(i, i // n_lo * n_lo + (i % n_lo + d) % n_lo) for i in ranks]
-        around.append(shifted(own, route))
-    around = jnp.stack(around).astype(F32)
-    order = list(range(n_lo))[::step]
-    total = jnp.zeros_like(around[0])
-    before = jnp.zeros_like(around[0])
-    keep_all = jnp.ones_like(kept[:, 0])
-    keep_before = keep_all
-    for pos in order:
-        here = lo == pos
-        before = jnp.where(here, total, before)
-        keep_before = jnp.where(here, keep_all, keep_before)
-        part = lax.dynamic_index_in_dim(around, (lo - pos) % n_lo, 0, False)
-        keep = keep_of(hi * n_lo + pos)
-        total = part + keep[:, None, None] * total
-        keep_all = keep * keep_all
-    entering = jnp.zeros_like(total)
-    for hop in range(n_hi - 1):
-        leaving = (total + keep_all[:, None, None] * entering).astype(BF)
-        route = [(i, i + step * n_lo) for i in ranks if 0 <= i + step * n_lo < count]
-        got = shifted(leaving, route).astype(F32)
-        at = n_hi - 2 - hop if reverse else hop + 1
-        entering = jnp.where(hi == at, got, entering)
-    return (before + keep_before[:, None, None] * entering).astype(BF)
-
-
-def frames(doc_starts, index, count, span):
-    rows = doc_starts.shape[0]
-    padded = jnp.concatenate([jnp.zeros((rows, WINDOW), jnp.int32), doc_starts], axis=1)
-    kept = jnp.sum(padded[:, : count * span].reshape(rows, count, span), axis=2) == 0
-    marks = lax.dynamic_slice_in_dim(padded, index * span, span + WINDOW, 1)
-    segment = jnp.cumsum(marks, axis=1)
-    own, tail = segment[:, WINDOW:], segment[:, :WINDOW]
-    last = own[:, span - WINDOW - 1 : span - WINDOW]
-    keys = jnp.concatenate([own, tail], axis=1)
-    valid = jnp.concatenate([jnp.arange(span) < span - WINDOW, jnp.full((WINDOW,), True)])
-    keep = ((keys == last) & valid[None]).astype(F32)
-    return kept.astype(F32), own[:, None, :], keys[:, :, None], keep[:, None, :]
-
-
 def body(
     tokens, doc_starts, pregain, query_base, key_base, value_base, output_base, query_down, query_up,
     key_down, key_up, value_down, value_up, out_down, out_up, query_map, key_map, postgain, gate_proj,
@@ -1045,65 +1145,72 @@
     high = -(-width // 256) * 256
     feats = 2 * head
     slots = -(-heads // 8) * 8
-    count = lax.axis_size("seq")
-    index = lax.axis_index("seq")
 
     tok = jnp.swapaxes(tokens, 1, 2)
     cot = jnp.swapaxes(cotangent, 1, 2)
-    gain_one = pregain.astype(F32)[:, None]
-    gain_two = postgain.astype(F32)[:, None]
-    kept, segq, segk, keep = frames(doc_starts, index, count, span)
-
-    zeros = functools.partial(jnp.zeros, dtype=BF)
-    wq = jnp.concatenate([query_base, 2 * query_up, zeros((high - width - rank, width))], axis=0)
-    kup = jnp.concatenate([zeros((kv_width, rank)), 2 * key_up.T, zeros((kv_width, high - width - 2 * rank))], axis=1)
-    vup = jnp.concatenate([zeros((kv_width, 2 * rank)), 2 * value_up.T, zeros((kv_width, high - width - 3 * rank))], axis=1)
-    wkv = jnp.concatenate(
-        [jnp.concatenate([key_base.T, value_base.T], axis=0), jnp.concatenate([kup, vup], axis=0)], axis=1
-    )
-    wo = jnp.concatenate([output_base, 2 * out_up, zeros((high - width - rank, width))], axis=0)
-    down = jnp.concatenate([query_down.T, key_down.T, value_down.T], axis=0)
+    gains = jnp.stack([pregain, postgain]).astype(F32)
     odown = out_down.T
 
-    ext = pltpu.VMEM((high, span), BF)
+    def phase_spec(shape, phase):
+        tail = (0,) * (len(shape) - 1)
+        return pl.BlockSpec((1,) + tuple(shape[1:]), lambda s: (jnp.clip(s - phase * rows, 0, rows - 1),) + tail)
+
+    args = [
+        (tok, 0), (tok, 3), (doc_starts, None), (gains, None), (query_base, None), (key_base.T, None),
+        (value_base.T, None), (output_base, None), (query_up, None), (key_up, None), (value_up, None),
+        (out_up, None), (query_down.T, None), (key_down.T, None), (value_down.T, None), (odown, None),
+        (query_map, None), (key_map, None),
+    ]
+    made = [
+        ((rows, width + 2 * kv_width, span), BF, 0),
+        ((rows, width, span), BF, 0),
+        ((rows, 3 * rank, span), BF, 0),
+        ((rows, kv_width, 2 * WINDOW), BF, 1),
+        ((rows, kv_heads, feats, extent), BF, 1),
+        ((rows, heads, feats, span), BF, 2),
+        ((rows, kv_heads * AUG, feats), BF, 3),
+        ((rows, width, span), BF, 3),
+        ((rows, slots, span), F32, 3),
+        ((rows, width, span), F32, 3),
+        ((rows, width, span), BF, 3),
+        ((rows, rank, span), BF, 3),
+        ((high, width), BF, None),
+        ((2 * kv_width, high), BF, None),
+        ((high, width), BF, None),
+        ((3 * rank, width), BF, None),
+        ((2, width, 1), F32, None),
+    ]
     biases = [pltpu.VMEM((extent, span), F32)] * 2
-    qkv, normed, inner, tails = row_call(
-        qkv_kernel,
-        rows,
-        [(tok, 1), (gain_one, 0), (wq, 0), (wkv, 0), (down, 0)],
-        [
-            ((rows, width + 2 * kv_width, span), BF, 1),
-            ((rows, width, span), BF, 1),
-            ((rows, 3 * rank, span), BF, 1),
-            ((rows, kv_width, 2 * WINDOW), BF, 1),
-        ],
-        [ext],
-    )
-    tails = shifted(tails, [(i, i + 1) for i in range(count - 1)])
-    phik, con = row_call(
-        functools.partial(key_kernel, kv_heads),
-        rows,
-        [(qkv, 1), (tails, 1), (key_map, 0), (keep, 1)],
-        [((rows, kv_heads, feats, extent), BF, 1), ((rows, kv_heads * AUG, feats), BF, 1)],
-    )
-    state = carried_states(con, kept, index, count, False)
-    mixed, den, phiq, middle, normed2, inner_o = row_call(
-        functools.partial(attend_kernel, kv_heads, group),
-        rows,
-        [
-            (qkv, 1), (tails, 1), (phik, 1), (state, 1), (segq, 1), (segk, 1), (query_map, 0), (tok, 1),
-            (wo, 0), (odown, 0), (gain_two, 0),
-        ],
-        [
-            ((rows, width, span), BF, 1),
-            ((rows, slots, span), F32, 1),
-            ((rows, heads, feats, span), BF, 1),
-            ((rows, width, span), F32, 1),
-            ((rows, width, span), BF, 1),
-            ((rows, rank, span), BF, 1),
-        ],
-        [ext] + biases,
-    )
+    frame_scratch = [pltpu.VMEM((8, extent), F32), pltpu.VMEM((8, 128), F32)]
+    (
+        qkv, normed, inner, tails, phik, phiq, state, mixed, den, middle, normed2, inner_o, wq, wkv, wo, down, columns,
+    ) = pl.pallas_call(
+        functools.partial(forward_kernel, rows, kv_heads, group),
+        grid=(4 * rows,),
+        in_specs=[whole_spec(*a.shape) if phase is None else phase_spec(a.shape, phase) for a, phase in args],
+        out_specs=tuple(
+            pl.BlockSpec(shape, functools.partial(lambda n, s: (0,) * n, len(shape)))
+            if phase is None
+            else phase_spec(shape, phase)
+            for shape, _, phase in made
+        ),
+        out_shape=tuple(shape_of(shape, kind) for shape, kind, _ in made),
+        scratch_shapes=frame_scratch
+        + [
+            pltpu.VMEM((high, span), BF),
+            pltpu.VMEM((rows, width + 2 * kv_width, span), BF),
+            pltpu.VMEM((rows, kv_width, 2 * WINDOW), BF),
+            pltpu.VMEM((rows, kv_width, 2 * WINDOW), BF),
+            pltpu.VMEM((rows, kv_heads, feats, extent), BF),
+            pltpu.VMEM((rows, heads, feats, span), BF),
+            pltpu.VMEM((rows, width, span), F32),
+            pltpu.VMEM((rows, slots, span), F32),
+        ]
+        + biases
+        + [pltpu.SemaphoreType.DMA((2, rows))]
+        + chain_scratch(rows, kv_heads * AUG, feats),
+        compiler_params=pltpu.CompilerParams(vmem_limit_bytes=VMEM, collective_id=2, has_side_effects=True),
+    )(*[a for a, _ in args])
 
     last = lambda s: (jnp.maximum(s - tiles, 0), 0, 0)
     fixed = lambda s: (0, 0)
@@ -1113,7 +1220,7 @@
     layer_out, grad_mid, gpost, shards = pl.pallas_call(
         functools.partial(ff_kernel, width),
         grid=(tiles + rows,),
-        in_specs=[anywhere, anywhere, pl.BlockSpec((1, width, span), last), pl.BlockSpec((width, 1), fixed)]
+        in_specs=[anywhere, anywhere, pl.BlockSpec((1, width, span), last), pl.BlockSpec((1, width, 1), lambda s: (1, 0, 0))]
         + [anywhere] * 3,
         out_specs=(
             pl.BlockSpec((1, width, span), last),
@@ -1133,32 +1240,15 @@
         + [pltpu.SemaphoreType.DMA((tiles, 3)), pltpu.SemaphoreType.DMA((rows, 2))]
         + scatter_scratch(3 * high, BF),
         compiler_params=pltpu.CompilerParams(vmem_limit_bytes=VMEM, collective_id=0, has_side_effects=True),
-    )(normed2, cot, middle, gain_two, gate_proj, up_proj, down_proj.T)
+    )(normed2, cot, middle, columns, gate_proj, up_proj, down_proj.T)
 
     layout = Small(rank, width, kv_width, heads, kv_heads, head)
-    args, specs = [kept], [pl.BlockSpec(memory_space=pltpu.SMEM)]
-    for phase, arrays in enumerate(
-        (
-            (grad_mid, mixed, den, phiq, segq, inner_o),
-            (qkv, tails, phik, phiq, state, segq, segk, keep),
-            (tok, grad_mid, normed, inner),
-        )
-    ):
-        def at(s, *, phase=phase, n=0):
-            return (jnp.clip(s - phase * rows, 0, rows - 1),) + (0,) * n
-
-        for array in arrays:
-            args.append(array)
-            specs.append(
-                pl.BlockSpec((1,) + array.shape[1:], functools.partial(at, n=array.ndim - 1))
-            )
-        fixed_args = ((wo, odown), (query_map, key_map), (wq, wkv, down, gpost))[phase]
-        if phase == 2:
-            args.insert(len(args) - 2, gain_one)
-            specs.insert(len(specs) - 2, whole_spec(*gain_one.shape))
-        for array in fixed_args:
-            args.append(array)
-            specs.append(whole_spec(*array.shape))
+    args = [(doc_starts, None)]
+    args += [(a, 0) for a in (grad_mid, mixed, den, phiq, inner_o)] + [(wo, None), (odown, None)]
+    args += [(a, 1) for a in (qkv, tails, phik, phiq, state)] + [(query_map, None), (key_map, None)]
+    args += [(a, 2) for a in (tok, grad_mid, normed, inner)] + [(a, None) for a in (columns, wq, wkv, down, gpost)]
+    specs = [whole_spec(*a.shape) if phase is None else phase_spec(a.shape, phase) for a, phase in args]
+    args = [a for a, _ in args]
     args.append(shards)
     specs.append(anywhere)
     last = lambda s: (jnp.maximum(s - 2 * rows, 0), 0, 0)
@@ -1193,6 +1283,7 @@
             pltpu.VMEM((3 * rank, width + 2 * kv_width), F32),
         ]
         + biases
+        + frame_scratch
         + [
             pltpu.SemaphoreType.DMA((2, rows)),
             pltpu.VMEM((1, len(small_streams), small_streams[0][2][-1][1], 128), BF),
@@ -1205,21 +1296,32 @@
         compiler_params=pltpu.CompilerParams(vmem_limit_bytes=VMEM, collective_id=1, has_side_effects=True),
     )(*args)
 
-    column = pl.BlockSpec((width, 128), lambda j: (0, j))
+    column = pl.BlockSpec((width, TILE), lambda j: (0, j))
     flat = [(1, width)] * 2 + [(rank, width)] * 4 + [(rank, kv_width)] * 2 + [(rank, width)] * 2
     flat += [query_map.shape, key_map.shape]
+    pieces = next(n for n in range(tiles // rows, 0, -1) if width % (16 * n) == 0 and tiles >= n * rows)
+    part = pl.BlockSpec(
+        (1, width // pieces, span),
+        lambda j: (jnp.minimum(j // pieces, rows - 1), jnp.where(j < rows * pieces, j % pieces, pieces - 1), 0),
+    )
     outs = pl.pallas_call(
         functools.partial(widen_kernel, width, high, rank, layout),
-        grid=(2 * tiles,),
+        grid=(tiles,),
         in_specs=[
-            pl.BlockSpec((1, 1, 3 * high, 128), lambda j: (j // 2, j % 2, 0, 0)),
+            pl.BlockSpec((1, 2, 3 * high, 128), lambda j: (j, 0, 0, 0)),
             pl.BlockSpec((1, 2, layout.rows, 128), lambda j: (0, 0, 0, 0)),
+            part,
+            part,
         ],
-        out_specs=(column,) * 3 + tuple(pl.BlockSpec(f, functools.partial(lambda n, j: (0,) * n, len(f))) for f in flat),
-        out_shape=(shape_of((width, hidden), F32),) * 3 + tuple(shape_of(f, F32) for f in flat),
+        out_specs=(part, part)
+        + (column,) * 3
+        + tuple(pl.BlockSpec(f, functools.partial(lambda n, j: (0,) * n, len(f))) for f in flat),
+        out_shape=(shape_of(layer_out.shape, BF), shape_of(grad_tok.shape, F32))
+        + (shape_of((width, hidden), F32),) * 3
+        + tuple(shape_of(f, F32) for f in flat),
         compiler_params=pltpu.CompilerParams(vmem_limit_bytes=VMEM),
-    )(whole, small)
-    gate, up, down_t, pre, post, qd, kd, vd, qu, ku, vu, od, ou, gq, gk = outs
+    )(whole, small, layer_out, grad_tok)
+    layer_out, grad_tok, gate, up, down_t, pre, post, qd, kd, vd, qu, ku, vu, od, ou, gq, gk = outs
     return (
         jnp.swapaxes(layer_out, 1, 2),
         jnp.swapaxes(grad_tok, 1, 2),

time: 413 us -> 335 us (0.81)
  waiting for transfers between devices: 38 us -> 0 us
  starting transfers between devices: 22.3 us -> 0 us
  other arithmetic: 21.7 us -> 0.61 us
  Pallas kernels: 314 us -> 332 us
  local copies, waits for them, and re-layouts: 13.9 us -> 1.37 us
    ppermute x5 -> x0, waiting for transfers between devices: 38 us -> none  [shifted(): return lax.ppermute(array, 'seq', route)]
    ppermute x5 -> x0, starting transfers between devices: 22.3 us -> none  [shifted(): return lax.ppermute(array, 'seq', route)]
    pallas_call x3 -> x1, Pallas kernels: 44.6 us -> 61.5 us  [body(): pl.pallas_call(functools.partial(forward_kernel, rows, kv_heads, group),...]
    unnamed x17 -> x0, local copies, waits for them, and re-layouts: 9.25 us -> none
    convert_element_type x7 -> x1, other arithmetic: 9.54 us -> 0.61 us  [body(): gains = jnp.stack([pregain, postgain]).astype(F32)]
    concatenate x3 -> x0, other arithmetic: 7.52 us -> none  [the longest x1 4.82 us: body(): jnp.concatenate([output_base, 2 * out_up, zeros((high - width - rank, wid...]
  transfers between devices with their start and end apart: 5 -> 0, of which waited for: 5 -> 0; matrix products, arithmetic and copies ran while one was open for 1% -> 0% of each run, Pallas kernels for 0% -> 0%
where the time goes in v3:
time: 335 us
  Pallas kernels  332 us (99%)
    pallas_call x1, Pallas kernels, body(): pl.pallas_call(functools.partial(backward_kernel, rows, kv_heads, group,...  142 us
    pallas_call x1, Pallas kernels, body(): pl.pallas_call(functools.partial(ff_kernel, width), grid=(tiles + rows,),...  106 us
    pallas_call x1, Pallas kernels, body(): pl.pallas_call(functools.partial(forward_kernel, rows, kv_heads, group),...  61.5 us
    pallas_call x1, Pallas kernels, body(): pl.pallas_call(functools.partial(widen_kernel, width, high, rank, layout)...  21.8 us

profile of v3, /device:TPU:0, one launch (start us, length us, event | category | flops | bytes accessed | tf_op | source)
XLA Modules:
  0.0 334.9 jit_solution(6891106483590480120)
XLA Ops:
  0.7 0.7 stack.9
  1.3 0.7 stack.10
  2.0 0.6 maximum_convert_fusion.gains
  2.6 61.5 %shard_map.341 = (bf16[5,1600,256]{2,1,0:T(8,128)(2,1)}, bf16[5,960,256]{2,1,0:T(8,128)(2,1)}, bf16[5,24,256]{2,1,0:T(8,128)(2,1)}, bf16[5,320,128]{2,1,0:T(8,12...) custom-call(bf16[5,960,256]{2,1,0:T(8,128)(2,1)} %bitcast.18, ...), custom_call_target="tpu_custom_call" | custom-call | tf_op jit(solution)/shard_map/pallas_call | solution.py:1187
  64.2 106.4 %shard_map.342 = (bf16[5,960,256]{2,1,0:T(8,128)(2,1)}, f32[5,960,256]{2,1,0:T(8,128)}, f32[8,960]{1,0:T(8,128)}, bf16[10,2,96,128]{3,2,1,0:T(8,128)(2,1)}) custom-call(bf16[5,960,256]{2,1,0:T(8,128)(2,1)} %get-tuple-element.58.normed_h, bf16[5,960,256]{2,1,0:T(8,128)(2,1)} %bitcast.22, f32[5,960,256]{2,1,0:T(8,128)} %get-tuple-element.59.middle, ...), custom_call_target="tpu_custom_call" | custom-call | tf_op jit(solution)/shard_map/pallas_call | solution.py:1220
  170.6 142.3 %shard_map.343 = (f32[5,960,256]{2,1,0:T(8,128)}, bf16[10,2,3072,128]{3,2,1,0:T(8,128)(2,1)}, bf16[1,2,768,128]{3,2,1,0:T(8,128)(2,1)}) custom-call(s32[5,2048]{1,0:T(8,128)} %doc.3, f32[5,960,256]{2,1,0:T(8,128)} %get-tuple-element.61.grad_mid_p.grad_mid, bf16[5,960,256]{2,1,0:T(8,128)(2,1)} %get-tuple-element.62.mixed, ...), custom_call_target="tpu_custom_call" | custom-call | tf_op jit(solution)/shard_map/pallas_call | solution.py:1256
  312.9 21.8 %shard_map.344 = (bf16[5,960,256]{2,1,0:T(8,128)(2,1)}, f32[5,960,256]{2,1,0:T(8,128)}, f32[960,2560]{1,0:T(8,128)}, f32[960,2560]{1,0:T(8,128)}, f32[960,2560]{...) custom-call(bf16[10,2,3072,128]{3,2,1,0:T(8,128)(2,1)} %get-tuple-el, ...), custom_call_target="tpu_custom_call" | custom-call | tf_op jit(solution)/shard_map/pallas_call | solution.py:1307

commit v4 on v3

--- a/solution.py
+++ b/solution.py
@@ -50,7 +50,22 @@
     def inside(self, distance):
         return (self.seq + distance >= 0) & (self.seq + distance < self.size["hi"] * self.size["lo"])
 
-    def greet(self):
+    def others(self):
+        size = self.size
+        return [
+            (a, b, c)
+            for a in range(size["lo"])
+            for b in range(size["y"])
+            for c in range(size["hi"])
+            if a or b or c
+        ]
+
+    def other(self, offset):
+        at = [(self.at[n] + d) % self.size[n] for n, d in zip(("lo", "y", "hi"), offset)]
+        number = (at[0] * self.size["y"] + at[1]) * self.size["hi"] + at[2]
+        return (at[1] * 2 + self.at["core"], at[2] * self.size["lo"] + at[0]), number
+
+    def greet(self, everyone=False):
         barrier = pltpu.get_barrier_semaphore()
         total = 0
         for d in (-1, 1):
@@ -60,10 +75,14 @@
                 pl.semaphore_signal(barrier, inc=1, device_id=self.along(d), device_id_type=MESH)
 
             total = total + jnp.where(self.inside(d), 1, 0)
-        for axis, size in self.size.items():
-            for d in range(1, size):
-                pl.semaphore_signal(barrier, inc=1, device_id=self.peer(axis, d), device_id_type=MESH)
-                total = total + 1
+        peers = [self.peer("core", 1)]
+        if everyone:
+            peers += [self.other(offset)[0] for offset in self.others()]
+        else:
+            peers += [self.peer(axis, d) for axis in ("lo", "y", "hi") for d in range(1, self.size[axis])]
+        for peer in peers:
+            pl.semaphore_signal(barrier, inc=1, device_id=peer, device_id_type=MESH)
+            total = total + 1
         pl.semaphore_wait(barrier, total)
 
 
@@ -74,19 +93,24 @@
 
 def stream_plan(rows):
     size = axis_sizes()
-    orders = [("lo", "y", "hi"), ("y", "lo", "hi")]
-    devices = size["lo"] * size["y"] * size["hi"]
-    if rows // (2 * devices) % 16:
-        orders = orders[:1]
-    part = rows // len(orders)
+    grain = 16 * size["lo"] * size["y"] * size["hi"]
+    part = rows // (2 * grain) * grain
     plan = []
-    for i, order in enumerate(orders):
+    for i, order in enumerate((("lo", "y", "hi"), ("y", "lo", "hi"))):
         left, stages = part, []
         for axis in order:
             left = left // size[axis]
-            stages.append((axis, left))
+            stages.append((axis, left, True))
         plan.append((i * part, part, stages))
+    rest = rows - 2 * part
+    if rest:
+        left = rest // size["hi"]
+        plan.append((2 * part, rest, [("hi", left, True), ("lo", left, False), ("y", left, False)]))
     return plan
+
+
+def shard_rows(rows):
+    return max(stages[-1][1] for _, _, stages in stream_plan(rows))
 
 
 def remote(src, dst, send, recv, peer):
@@ -111,7 +135,7 @@
         pltpu.SemaphoreType.DMA((2, slots)),
     ]
     for _, _, stages in stream_plan(rows):
-        for k, (axis, left) in enumerate(stages, 1):
+        for k, (axis, left, _) in enumerate(stages, 1):
             peers = max(size[axis] - 1, 1)
             made.append(pltpu.VMEM((stage_slots(k, slots), peers, left, 128), kind))
             made.append(pltpu.VMEM((slots, left, 128), kind))
@@ -127,8 +151,8 @@
         at = 4
         for first, part, stages in stream_plan(rows):
             made = []
-            for axis, left in stages:
-                made.append((axis, left) + tuple(refs[at : at + 3]))
+            for axis, left, divides in stages:
+                made.append((axis, left) + tuple(refs[at : at + 3]) + (divides,))
                 at += 3
             self.streams.append((first, part, made))
 
@@ -144,10 +168,10 @@
         slot = t % stage_slots(k, self.slots)
         made = []
         for first, part, stages in self.streams:
-            axis, left, got, _, sem = stages[k - 1]
+            axis, left, got, _, sem, divides = stages[k - 1]
             size = self.place.size[axis]
             for d in range(1, size):
-                to = (self.place.at[axis] + d) % size
+                to = (self.place.at[axis] + d) % size if divides else 0
                 if k == 1:
                     src = self.base.at[slot, pl.ds(pl.multiple_of(first + to * left, 16), left)]
                 else:
@@ -170,31 +194,33 @@
         if k == 0:
             self.core_copy(t).wait()
             core = self.place.at["core"]
-            self.base[t % stage_slots(1, self.slots)] = (self.mine[slot, core].astype(F32) + self.other[slot].astype(F32)).astype(self.base.dtype)
+            total = self.mine[slot, core].astype(F32) + self.other[slot].astype(F32)
+            self.base[t % stage_slots(1, self.slots)] = total.astype(self.base.dtype)
             return
         for copy in self.copies(k, t):
             copy.wait()
         for i, (first, part, stages) in enumerate(self.streams):
-            axis, left, got, out, _ = stages[k - 1]
-            at = self.place.at[axis] * left
+            axis, left, got, out, _, divides = stages[k - 1]
+            size = self.place.size[axis]
+            at = self.place.at[axis] * left if divides else 0
             if k == 1:
                 own = self.base[ahead, pl.ds(pl.multiple_of(first + at, 16), left)]
             else:
                 own = stages[k - 2][3][slot, pl.ds(pl.multiple_of(at, 16), left)]
-            total = own.astype(F32)
-            for d in range(1, self.place.size[axis]):
-                total = total + got[ahead, d - 1].astype(F32)
+            if divides or size == 2:
+                total = own.astype(F32)
+                for d in range(1, size):
+                    total = total + got[ahead, d - 1].astype(F32)
+            else:
+                total = jnp.zeros(own.shape, F32)
+                for p in range(size):
+                    d = (self.place.at[axis] - p) % size
+                    part = jnp.where(d == 0, own, got[ahead, jnp.maximum(d - 1, 0)])
+                    total = total + part.astype(F32)
             if k == 3:
                 into(i, total)
             else:
                 out[slot] = total.astype(out.dtype)
-
-    def run(self, into):
-        self.start(0, 0)
-        for k in range(4):
-            self.finish(k, 0, into)
-            if k < 3:
-                self.start(k + 1, 0)
 
     def turn(self, step, tiles, into):
         for k in (3, 2, 1, 0):
@@ -218,7 +244,7 @@
     size = axis_sizes()
     made = [pltpu.SemaphoreType.DMA((2, tiles)), pltpu.SemaphoreType.DMA((tiles, len(stream_plan(rows))))]
     for _, _, stages in stream_plan(rows):
-        for axis, left in stages:
+        for axis, left, _ in stages:
             made.append(pltpu.SemaphoreType.DMA((2, tiles, max(size[axis] - 1, 1))))
     return made
 
@@ -236,13 +262,16 @@
     def region(self, t, stream, k):
         first, _, stages = self.streams[stream]
         at = first
-        for axis, left, _ in stages[:k]:
-            at = at + self.place.at[axis] * left
+        for axis, left, divides, _ in stages[:k]:
+            at = at + (self.place.at[axis] * left if divides else 0)
         return self.whole.at[t, self.place.at["core"], pl.ds(pl.multiple_of(at, 16), stages[k - 1][1])]
+
+    def shard(self, t, stream):
+        return self.shards.at[t, stream, 0 : self.streams[stream][2][-1][1]]
 
     def own_copies(self, t):
         return [
-            pltpu.make_async_copy(self.shards.at[t, i], self.region(t, i, 3), self.own_sem.at[t, i])
+            pltpu.make_async_copy(self.shard(t, i), self.region(t, i, 3), self.own_sem.at[t, i])
             for i in range(len(self.streams))
         ]
 
@@ -252,22 +281,14 @@
             return [remote(half, half, self.core_sem.at[0, t], self.core_sem.at[1, t], self.place.peer("core", 1))]
         made = []
         for i, (_, _, stages) in enumerate(self.streams):
-            axis, left, sem = stages[k - 1]
+            axis, left, divides, sem = stages[k - 1]
+            if not divides:
+                continue
             dst = self.region(t, i, k)
-            src = self.shards.at[t, i] if k == 3 else dst
+            src = self.shard(t, i) if k == 3 else dst
             for d in range(1, self.place.size[axis]):
                 made.append(remote(src, dst, sem.at[0, t, d - 1], sem.at[1, t, d - 1], self.place.peer(axis, d)))
         return made
-
-    def run(self):
-        for copy in self.own_copies(0) + self.copies(3, 0):
-            copy.start()
-        for k in (3, 2, 1, 0):
-            for copy in self.copies(k, 0) + (self.own_copies(0) if k == 3 else []):
-                copy.wait()
-            if k > 0:
-                for copy in self.copies(k - 1, 0):
-                    copy.start()
 
     def turn(self, step, tiles):
         for k in (0, 1, 2, 3):
@@ -405,6 +426,73 @@
         pltpu.VMEM(shape, BF),
         pltpu.SemaphoreType.DMA((2, rows, peers)),
         pltpu.SemaphoreType.DMA((2, rows)),
+    ]
+
+
+class Direct:
+    def __init__(self, place, whole, mine, other, base, got, core_sem, out_sem, back_sem):
+        self.place, self.whole = place, whole
+        self.mine, self.other, self.base, self.got = mine, other, base, got
+        self.core_sem, self.out_sem, self.back_sem = core_sem, out_sem, back_sem
+        self.offsets = place.others()
+        self.rows = base.shape[0] // (len(self.offsets) + 1)
+        self.own = self.region(place.other((0, 0, 0))[1])
+
+    def region(self, number):
+        return pl.ds(pl.multiple_of(number * self.rows, 16), self.rows)
+
+    def copies(self, k):
+        core = self.place.at["core"]
+        made = []
+        if k == 0:
+            partner = self.place.peer("core", 1)
+            made.append(
+                remote(self.mine.at[0, 1 - core], self.other, self.core_sem.at[0, 0], self.core_sem.at[1, 0], partner)
+            )
+        elif k == 3:
+            half = self.whole.at[0, core]
+            made.append(
+                remote(half, half, self.core_sem.at[0, 1], self.core_sem.at[1, 1], self.place.peer("core", 1))
+            )
+        else:
+            for i, offset in enumerate(self.offsets):
+                peer, number = self.place.other(offset)
+                if k == 1:
+                    src, dst, sem = self.base.at[self.region(number)], self.got.at[i], self.out_sem
+                else:
+                    src = dst = self.whole.at[0, core, self.own]
+                    sem = self.back_sem
+                made.append(remote(src, dst, sem.at[0, i], sem.at[1, i], peer))
+        return made
+
+    def start(self, k):
+        for copy in self.copies(k):
+            copy.start()
+
+    def finish(self, k):
+        for copy in self.copies(k):
+            copy.wait()
+        core = self.place.at["core"]
+        if k == 0:
+            self.base[...] = self.mine[0, core] + self.other[...]
+        elif k == 1:
+            total = self.base[self.own].astype(F32)
+            for i in range(len(self.offsets)):
+                total = total + self.got[i].astype(F32)
+            self.whole[0, core, self.own] = total.astype(BF)
+
+
+def direct_scratch(rows):
+    size = axis_sizes()
+    peers = size["lo"] * size["y"] * size["hi"] - 1
+    return [
+        pltpu.VMEM((1, 2, rows, 128), BF),
+        pltpu.VMEM((rows, 128), BF),
+        pltpu.VMEM((rows, 128), BF),
+        pltpu.VMEM((peers, rows // (peers + 1), 128), BF),
+        pltpu.SemaphoreType.DMA((2, 2)),
+        pltpu.SemaphoreType.DMA((2, peers)),
+        pltpu.SemaphoreType.DMA((2, peers)),
     ]
 
 
@@ -458,7 +546,7 @@
     tok_out[...] = tok_in[...]
     for i, out in enumerate((gate, up, down)):
         for half in range(2):
-            out[:, half * 128 : (half + 1) * 128] = whole[0, half, i * high : i * high + width].astype(F32)
+            out[:, half * 128 : (half + 1) * 128] = whole[0, half, i * width : (i + 1) * width].astype(F32)
 
     @pl.when(pl.program_id(0) == 0)
     def _():
@@ -779,8 +867,8 @@
 
 def ff_kernel(
     width, normed_h, cot_h, middle, gain, gate_h, up_h, down_h,
-    out, grad_mid, grad_gain, shards,
-    normed, cot, gate_v, up_v, down_v, hid, dgate, dup, sem, act_sem, *refs,
+    hid_out, grad_mid, grad_gain, shards,
+    normed, cot, gate_v, up_v, down_v, hid, dgate, dup, sem, act_sem, hid_sem, *refs,
 ):
     step = pl.program_id(0)
     rows = normed_h.shape[0]
@@ -789,7 +877,7 @@
     hidden = gate_h.shape[1]
     tiles = hidden // TILE
     place = Place()
-    scatter = Scatter(place, 3 * high, refs)
+    scatter = Scatter(place, 3 * width, refs)
 
     def act_copies():
         made = []
@@ -841,9 +929,9 @@
             dgate[at, lane] = (dh * u * (sig + act * (1.0 - sig))).astype(BF)
         slot = step % 2
         for i, (left, right) in enumerate(((normed, dgate), (normed, dup), (cot, hid))):
-            grad = dot(left[...], right[at, :], NT).astype(BF)
+            grad = dot(left[...], right[at, :], NT)[:width].astype(BF)
             for half in range(2):
-                scatter.mine[slot, half, i * high : (i + 1) * high] = grad[:, half * 128 : (half + 1) * 128]
+                scatter.mine[slot, half, i * width : (i + 1) * width] = grad[:, half * 128 : (half + 1) * 128]
 
     @pl.when(step >= tiles)
     def _():
@@ -852,21 +940,27 @@
         back = dot(gate_v[0:width], dgate[:, lane]) + dot(up_v[0:width], dup[:, lane])
         mid = middle[0]
         scale = rms(mid)
-        unit = mid * scale
-        grad_unit = back * gain[0]
-        grad_mid[0] = cot[0:width, lane].astype(F32) + scale * (
-            grad_unit - unit * jnp.mean(grad_unit * unit, axis=0, keepdims=True)
-        )
+        unit = back * mid
+        column = gain[0]
+        pull = jnp.mean(unit * column, axis=0, keepdims=True) * (scale * scale * scale)
+        grad_mid[0] = cot[0:width, lane].astype(F32) + (back * column) * scale - mid * pull
 
         @pl.when(r == 0)
         def _():
             grad_gain[...] = jnp.zeros_like(grad_gain)
 
-        grad_gain[...] += row_sum(back * unit)
-        out[0] = (mid + dot(down_v[0:width], hid[:, lane])).astype(BF)
+        grad_gain[...] += row_sum(unit * scale)
+
+        @pl.when(r == 0)
+        def _():
+            pltpu.make_async_copy(hid, hid_out, hid_sem).start()
+
+        @pl.when(r == rows - 1)
+        def _():
+            pltpu.make_async_copy(hid, hid_out, hid_sem).wait()
 
     def into(tile, stream, total):
-        shards[tile, stream] = total.astype(BF)
+        shards[tile, stream, 0 : total.shape[0]] = total.astype(BF)
 
     scatter.turn(step, tiles, into)
 
@@ -1000,21 +1094,19 @@
     rows, kv_heads, group, tiles, shard_rows, layout,
     doc, grad_mid_p, mixed, den, phiq_p, inner_o, wo, odown,
     qkv, tails, phik, phiq, state, qmap, kmap,
-    tok, grad_mid, normed, inner, gain, wq, wkv, down, gpost, shards,
-    grad_tok, whole, small_out,
+    tok, grad_mid, normed, inner, gain, wq, wkv, down, gpost, shards, hid_h, down_h, middle_h,
+    grad_tok, whole, small_out, layer_out,
     dnum, dden, dq, dkv, dtails, returned, gup_o, gdown_o, gqmap, gkmap, ggain, gdown, gup, lin_bias, win_bias,
-    seg, kept, tail_sem, small_shard, small, *refs,
+    seg, kept, tail_sem, small, hid, down_v, middle, out, in_sem, out_sem, *refs,
 ):
     step = pl.program_id(0)
+    early = 3
     place = Place()
     chain = Chain(place, True, 1, kept, *refs[:9])
     refs = refs[9:]
     n_gather = len(gather_scratch(shard_rows, tiles))
     gather = Gather(place, shard_rows, shards, whole, refs[:n_gather])
-    refs = refs[n_gather:]
-    n_small = len(gather_scratch(layout.rows, 1))
-    small_gather = Gather(place, layout.rows, small_shard, small, refs[:n_small])
-    small_scatter = Scatter(place, layout.rows, refs[n_small:], 1)
+    direct = Direct(place, small, *refs[n_gather:])
 
     def row(ref, r):
         return ref.at[pl.ds(r, 1)]
@@ -1022,9 +1114,23 @@
     def tail_copy(r):
         return remote(dtails.at[r], returned.at[r], tail_sem.at[0, r], tail_sem.at[1, r], place.along(-1))
 
+    def fetches():
+        pairs = ((hid_h, hid), (down_h, down_v), (middle_h, middle))
+        return [pltpu.make_async_copy(src, dst, in_sem.at[i]) for i, (src, dst) in enumerate(pairs)]
+
+    def out_copy(r):
+        return pltpu.make_async_copy(out.at[r], layer_out.at[r], out_sem.at[r])
+
+    def make_out(r):
+        lane = slice(r * tok.shape[2], (r + 1) * tok.shape[2])
+        out[r] = (middle[r] + dot(down_v[...], hid[:, lane])).astype(BF)
+        out_copy(r).start()
+
     @pl.when(step == 0)
     def _():
-        place.greet()
+        for copy in fetches():
+            copy.start()
+        place.greet(True)
         frame(place, tok.shape[2], doc, seg, kept)
         for ref in (gup_o, gdown_o, gqmap, gkmap, ggain, gdown, gup):
             ref[...] = jnp.zeros_like(ref)
@@ -1046,7 +1152,10 @@
 
         def between(k):
             if k == kv_heads // 2:
-                gather.turn(2 * r, tiles)
+
+                @pl.when(r % 2 == 1)
+                def _():
+                    gather.turn(early + r + r // 2, tiles)
 
         back_kernel(
             kv_heads, group, qkv, tails, phik, phiq, state, row(chain.result, r), row(dnum, r), row(dden, r),
@@ -1073,9 +1182,13 @@
 
     chain.turn(step, rows)
 
-    @pl.when(step >= rows)
-    def _():
-        gather.turn(jnp.where(step < 2 * rows, 2 * (step - rows) + 1, step), tiles)
+    r = step - rows
+    late = early + rows + rows // 2
+    turn = jnp.where(step < rows, step - (rows - early), jnp.where(r < rows, early + r + (r + 1) // 2, late + (r - rows) // 2))
+
+    @pl.when((step >= rows - early) & ((r < rows) | ((r - rows) % 2 == 0)))
+    def _():
+        gather.turn(turn, tiles)
 
     @pl.when(step == 3 * rows - 1)
     def _():
@@ -1089,7 +1202,7 @@
         rank = gdown_o.shape[0]
         width = gdown_o.shape[1]
         kv_width = kv_heads * qmap.shape[1]
-        mine = small_scatter.mine
+        mine = direct.mine
         mine[...] = jnp.zeros_like(mine)
         pad = [jnp.zeros((6, width), F32)]
         layout.put(mine, "down", jnp.concatenate([gdown[...], ggain[0:1], gpost[0:1]] + pad, axis=0))
@@ -1104,14 +1217,20 @@
         layout.put_heads(mine, "qmap", gqmap)
         layout.put_heads(mine, "kmap", gkmap)
 
-        def into(stream, total):
-            small_shard[0, stream] = total.astype(BF)
-
-        small_scatter.run(into)
-        small_gather.run()
+        turns = list(range(late + rows // 2 + 1, tiles + WAYS[0]))
+        for copy in fetches():
+            copy.wait()
+        shares = [list(range(rows))[n::4] for n in range(4)]
+        for k in range(4):
+            direct.start(k)
+            for r in shares[k]:
+                make_out(r)
+            for turn in turns[k : k + 1] if k < 3 else turns[3:]:
+                gather.turn(jnp.int32(turn), tiles)
+            direct.finish(k)
         small_out[...] = small[...]
-        for turn in range(3 * rows, tiles + WAYS[0]):
-            gather.turn(jnp.int32(turn), tiles)
+        for r in range(rows):
+            out_copy(r).wait()
 
 
 def row_spec(*shape):
@@ -1215,21 +1334,20 @@
     last = lambda s: (jnp.maximum(s - tiles, 0), 0, 0)
     fixed = lambda s: (0, 0)
     anywhere = pl.BlockSpec(memory_space=pl.ANY)
-    streams = stream_plan(3 * high)
-    shard_shape = (tiles, len(streams), streams[0][2][-1][1], 128)
-    layer_out, grad_mid, gpost, shards = pl.pallas_call(
+    shard_shape = (tiles, len(stream_plan(3 * width)), shard_rows(3 * width), 128)
+    hid, grad_mid, gpost, shards = pl.pallas_call(
         functools.partial(ff_kernel, width),
         grid=(tiles + rows,),
         in_specs=[anywhere, anywhere, pl.BlockSpec((1, width, span), last), pl.BlockSpec((1, width, 1), lambda s: (1, 0, 0))]
         + [anywhere] * 3,
         out_specs=(
-            pl.BlockSpec((1, width, span), last),
+            anywhere,
             pl.BlockSpec((1, width, span), last),
             pl.BlockSpec((8, width), fixed),
             pl.BlockSpec(shard_shape, lambda s: (0, 0, 0, 0)),
         ),
         out_shape=(
-            shape_of((rows, width, span), BF),
+            shape_of((hidden, rows * span), BF),
             shape_of((rows, width, span), F32),
             shape_of((8, width), F32),
             shape_of(shard_shape, BF),
@@ -1237,8 +1355,8 @@
         scratch_shapes=[pltpu.VMEM((high, rows * span), BF)] * 2
         + [pltpu.VMEM((high, hidden), BF)] * 3
         + [pltpu.VMEM((hidden, rows * span), BF)] * 3
-        + [pltpu.SemaphoreType.DMA((tiles, 3)), pltpu.SemaphoreType.DMA((rows, 2))]
-        + scatter_scratch(3 * high, BF),
+        + [pltpu.SemaphoreType.DMA((tiles, 3)), pltpu.SemaphoreType.DMA((rows, 2)), pltpu.SemaphoreType.DMA(())]
+        + scatter_scratch(3 * width, BF),
         compiler_params=pltpu.CompilerParams(vmem_limit_bytes=VMEM, collective_id=0, has_side_effects=True),
     )(normed2, cot, middle, columns, gate_proj, up_proj, down_proj.T)
 
@@ -1249,23 +1367,24 @@
     args += [(a, 2) for a in (tok, grad_mid, normed, inner)] + [(a, None) for a in (columns, wq, wkv, down, gpost)]
     specs = [whole_spec(*a.shape) if phase is None else phase_spec(a.shape, phase) for a, phase in args]
     args = [a for a, _ in args]
-    args.append(shards)
-    specs.append(anywhere)
+    args += [shards, hid, down_proj.T, middle]
+    specs += [anywhere] * 4
     last = lambda s: (jnp.maximum(s - 2 * rows, 0), 0, 0)
-    small_streams = stream_plan(layout.rows)
-    grad_tok, whole, small = pl.pallas_call(
-        functools.partial(backward_kernel, rows, kv_heads, group, tiles, 3 * high, layout),
+    grad_tok, whole, small, layer_out = pl.pallas_call(
+        functools.partial(backward_kernel, rows, kv_heads, group, tiles, 3 * width, layout),
         grid=(3 * rows,),
         in_specs=specs,
         out_specs=(
             pl.BlockSpec((1, width, span), last),
             anywhere,
             pl.BlockSpec((1, 2, layout.rows, 128), lambda s: (0, 0, 0, 0)),
+            anywhere,
         ),
         out_shape=(
             shape_of((rows, width, span), F32),
-            shape_of((tiles, 2, 3 * high, 128), BF),
+            shape_of((tiles, 2, 3 * width, 128), BF),
             shape_of((1, 2, layout.rows, 128), BF),
+            shape_of((rows, width, span), BF),
         ),
         scratch_shapes=[
             pltpu.VMEM((rows, width, span), BF),
@@ -1286,13 +1405,17 @@
         + frame_scratch
         + [
             pltpu.SemaphoreType.DMA((2, rows)),
-            pltpu.VMEM((1, len(small_streams), small_streams[0][2][-1][1], 128), BF),
             pltpu.VMEM((1, 2, layout.rows, 128), BF),
+            pltpu.VMEM((hidden, rows * span), BF),
+            pltpu.VMEM((width, hidden), BF),
+            pltpu.VMEM((rows, width, span), F32),
+            pltpu.VMEM((rows, width, span), BF),
+            pltpu.SemaphoreType.DMA((3,)),
+            pltpu.SemaphoreType.DMA((rows,)),
         ]
         + chain_scratch(rows, kv_heads * AUG, feats)
-        + gather_scratch(3 * high, tiles)
-        + gather_scratch(layout.rows, 1)
-        + scatter_scratch(layout.rows, BF, 1),
+        + gather_scratch(3 * width, tiles)
+        + direct_scratch(layout.rows),
         compiler_params=pltpu.CompilerParams(vmem_limit_bytes=VMEM, collective_id=1, has_side_effects=True),
     )(*args)
 
@@ -1308,7 +1431,7 @@
         functools.partial(widen_kernel, width, high, rank, layout),
         grid=(tiles,),
         in_specs=[
-            pl.BlockSpec((1, 2, 3 * high, 128), lambda j: (j, 0, 0, 0)),
+            pl.BlockSpec((1, 2, 3 * width, 128), lambda j: (j, 0, 0, 0)),
             pl.BlockSpec((1, 2, layout.rows, 128), lambda j: (0, 0, 0, 0)),
             part,
             part,

time: 335 us -> 307 us (0.916)
  Pallas kernels: 332 us -> 303 us
    pallas_call x1, Pallas kernels: 106 us -> 89.4 us  [body(): pl.pallas_call(functools.partial(ff_kernel, width), grid=(tiles + rows,),...]
    pallas_call x1, Pallas kernels: 142 us -> 130 us  [body(): pl.pallas_call(functools.partial(backward_kernel, rows, kv_heads, group,...]
where the time goes in v4:
time: 307 us; the launch traced here: 306 us
  Pallas kernels  303 us (99%)
    pallas_call x1, Pallas kernels, body(): pl.pallas_call(functools.partial(backward_kernel, rows, kv_heads, group,...  130 us
    pallas_call x1, Pallas kernels, body(): pl.pallas_call(functools.partial(ff_kernel, width), grid=(tiles + rows,),...  89.4 us
    pallas_call x1, Pallas kernels, body(): pl.pallas_call(functools.partial(forward_kernel, rows, kv_heads, group),...  61.6 us
    pallas_call x1, Pallas kernels, body(): pl.pallas_call(functools.partial(widen_kernel, width, high, rank, layout)...  22.1 us

profile of v4, /device:TPU:0, one launch (start us, length us, event | category | flops | bytes accessed | tf_op | source)
XLA Modules:
  0.0 306.3 jit_solution(3714787812909842016)
XLA Ops:
  0.7 0.7 stack.9
  1.3 0.7 stack.10
  2.0 0.6 maximum_convert_fusion.gains
  2.6 61.6 %shard_map.341 = (bf16[5,1600,256]{2,1,0:T(8,128)(2,1)}, bf16[5,960,256]{2,1,0:T(8,128)(2,1)}, bf16[5,24,256]{2,1,0:T(8,128)(2,1)}, bf16[5,320,128]{2,1,0:T(8,12...) custom-call(bf16[5,960,256]{2,1,0:T(8,128)(2,1)} %bitcast.18, ...), custom_call_target="tpu_custom_call" | custom-call | tf_op jit(solution)/shard_map/pallas_call | solution.py:1306
  64.2 89.4 %shard_map.342 = (bf16[2560,1280]{1,0:T(8,128)(2,1)}, f32[5,960,256]{2,1,0:T(8,128)}, f32[8,960]{1,0:T(8,128)}, bf16[10,3,80,128]{3,2,1,0:T(8,128)(2,1)}) custom-call(bf16[5,960,256]{2,1,0:T(8,128)(2,1)} %get-tuple-element.59.normed_h, bf16[5,960,256]{2,1,0:T(8,128)(2,1)} %bitcast.23, f32[5,960,256]{2,1,0:T(8,128)} %get-tuple-element.60.middle.middle_h, ...), custom_call_target="tpu_custom_call" | custom-call | tf_op jit(solution)/shard_map/pallas_call | solution.py:1338
  153.6 130.4 %shard_map.343 = (f32[5,960,256]{2,1,0:T(8,128)}, bf16[10,2,2880,128]{3,2,1,0:T(8,128)(2,1)}, bf16[1,2,768,128]{3,2,1,0:T(8,128)(2,1)}, bf16[5,960,256]{2,1,0:T(8,128)(2,1)}) custom-call(s32[5,2048]{1,0:T(8,128)} %doc.3, f32[5,960,256]{2,1,0:T(8,128)} %get-tuple-element.62.grad_mid_p.grad_mid, bf16[5,960,256]{2,1,0:T(8,128)(2,1)} %get-tuple-element.63.mixed, ...), custom_call_target="tpu_custom_call" | custom-call | tf_op jit(solution)/shard_map/pallas_call | solution.py:1373
  284.0 22.1 %shard_map.344 = (bf16[5,960,256]{2,1,0:T(8,128)(2,1)}, f32[5,960,256]{2,1,0:T(8,128)}, f32[960,2560]{1,0:T(8,128)}, f32[960,2560]{1,0:T(8,128)}, f32[960,2560]{...) custom-call(bf16[10,2,2880,128]{3,2,1,0:T(8,128)(2,1)} %get-tuple-el, ...), custom_call_target="tpu_custom_call" | custom-call | tf_op jit(solution)/shard_map/pallas_call | solution.py:1430

commit v5 on v4

--- a/solution.py
+++ b/solution.py
@@ -1100,7 +1100,7 @@
     seg, kept, tail_sem, small, hid, down_v, middle, out, in_sem, out_sem, *refs,
 ):
     step = pl.program_id(0)
-    early = 3
+    early = rows
     place = Place()
     chain = Chain(place, True, 1, kept, *refs[:9])
     refs = refs[9:]

time: 307 us -> 306 us (level)
  no operation moved by 1% of the time
where the time goes in v5:
time: 306 us
  Pallas kernels  303 us (99%)
    pallas_call x1, Pallas kernels, body(): pl.pallas_call(functools.partial(backward_kernel, rows, kv_heads, group,...  130 us
    pallas_call x1, Pallas kernels, body(): pl.pallas_call(functools.partial(ff_kernel, width), grid=(tiles + rows,),...  89.4 us
    pallas_call x1, Pallas kernels, body(): pl.pallas_call(functools.partial(forward_kernel, rows, kv_heads, group),...  61.6 us
    pallas_call x1, Pallas kernels, body(): pl.pallas_call(functools.partial(widen_kernel, width, high, rank, layout)...  22.1 us

profile of v5, /device:TPU:0, one launch (start us, length us, event | category | flops | bytes accessed | tf_op | source)
XLA Modules:
  0.0 305.6 jit_solution(12097301075571887477)
XLA Ops:
  0.7 0.7 stack.9
  1.3 0.7 stack.10
  2.0 0.6 maximum_convert_fusion.gains
  2.6 61.6 %shard_map.341 = (bf16[5,1600,256]{2,1,0:T(8,128)(2,1)}, bf16[5,960,256]{2,1,0:T(8,128)(2,1)}, bf16[5,24,256]{2,1,0:T(8,128)(2,1)}, bf16[5,320,128]{2,1,0:T(8,12...) custom-call(bf16[5,960,256]{2,1,0:T(8,128)(2,1)} %bitcast.18, ...), custom_call_target="tpu_custom_call" | custom-call | tf_op jit(solution)/shard_map/pallas_call | solution.py:1306
  64.2 89.4 %shard_map.342 = (bf16[2560,1280]{1,0:T(8,128)(2,1)}, f32[5,960,256]{2,1,0:T(8,128)}, f32[8,960]{1,0:T(8,128)}, bf16[10,3,80,128]{3,2,1,0:T(8,128)(2,1)}) custom-call(bf16[5,960,256]{2,1,0:T(8,128)(2,1)} %get-tuple-element.59.normed_h, bf16[5,960,256]{2,1,0:T(8,128)(2,1)} %bitcast.23, f32[5,960,256]{2,1,0:T(8,128)} %get-tuple-element.60.middle.middle_h, ...), custom_call_target="tpu_custom_call" | custom-call | tf_op jit(solution)/shard_map/pallas_call | solution.py:1338
  153.6 129.7 %shard_map.343 = (f32[5,960,256]{2,1,0:T(8,128)}, bf16[10,2,2880,128]{3,2,1,0:T(8,128)(2,1)}, bf16[1,2,768,128]{3,2,1,0:T(8,128)(2,1)}, bf16[5,960,256]{2,1,0:T(8,128)(2,1)}) custom-call(s32[5,2048]{1,0:T(8,128)} %doc.3, f32[5,960,256]{2,1,0:T(8,128)} %get-tuple-element.62.grad_mid_p.grad_mid, bf16[5,960,256]{2,1,0:T(8,128)(2,1)} %get-tuple-element.63.mixed, ...), custom_call_target="tpu_custom_call" | custom-call | tf_op jit(solution)/shard_map/pallas_call | solution.py:1373
  283.3 22.1 %shard_map.344 = (bf16[5,960,256]{2,1,0:T(8,128)(2,1)}, f32[5,960,256]{2,1,0:T(8,128)}, f32[960,2560]{1,0:T(8,128)}, f32[960,2560]{1,0:T(8,128)}, f32[960,2560]{...) custom-call(bf16[10,2,2880,128]{3,2,1,0:T(8,128)(2,1)} %get-tuple-el, ...), custom_call_target="tpu_custom_call" | custom-call | tf_op jit(solution)/shard_map/pallas_call | solution.py:1430
